TPU v7x, 32 devices: a whole 2x2x4 slice. The times are simulated.
32 devices in a mesh: dp: 8 (over y, x, core), seq: 4 (over z).
Axes of the slice: x: 2, y: 2, z: 4, core: 2. Of those that a mesh axis runs over, the one named last changes fastest.
Arguments:
- tokens: bfloat16 [32, 1024, 768], P('dp', 'seq'), may hold values from -8 to 8
- doc_lengths: int32 [32, 4], P('dp'), may hold values from 1 to 768, 1024 in all within a row
- query_weight: bfloat16 [768, 768], P(('dp', 'seq')), may hold values from -0.21875 to 0.21875
- key_weight: bfloat16 [768, 768], P(('dp', 'seq')), may hold values from -0.21875 to 0.21875
- value_weight: bfloat16 [768, 768], P(('dp', 'seq')), may hold values from -0.21875 to 0.21875
- out_weight: bfloat16 [768, 768], P(('dp', 'seq')), may hold values from -1.75 to 1.75
- pool_weight: bfloat16 [10, 768], P(None, ('dp', 'seq')), may hold values from -2.5 to 2.5
- first_gain: bfloat16 [768], P(('dp', 'seq')), may hold values from 0.5 to 1.5
- first_shift: bfloat16 [768], P(('dp', 'seq')), may hold values from -1.25 to 1.25
- inner_weight: bfloat16 [768, 3072], P(('dp', 'seq')), may hold values from -0.21875 to 0.21875
- inner_bias: bfloat16 [3072], P(('dp', 'seq')), may hold values from -1.75 to 1.75
- outer_weight: bfloat16 [3072, 768], P(('dp', 'seq')), may hold values from -0.21875 to 0.21875
- outer_bias: bfloat16 [768], P(('dp', 'seq')), may hold values from -1.25 to 1.25
- second_gain: bfloat16 [768], P(('dp', 'seq')), may hold values from 0.5 to 1.5
- second_shift: bfloat16 [768], P(('dp', 'seq')), may hold values from -1.25 to 1.25
- cotangent: bfloat16 [32, 1024, 768], P('dp', 'seq'), may hold values from -6 to 6
Outputs:
- block_output: bfloat16 [32, 1024, 768], P('dp', 'seq')
- input_grad: bfloat16 [32, 1024, 768], P('dp', 'seq')
- query_grad: float32 [768, 768], P(('dp', 'seq'))
- key_grad: float32 [768, 768], P(('dp', 'seq'))
- value_grad: float32 [768, 768], P(('dp', 'seq'))
- out_grad: float32 [768, 768], P(('dp', 'seq'))
- pool_grad: float32 [10, 768], P(None, ('dp', 'seq'))
- first_gain_grad: float32 [768], P(('dp', 'seq'))
- first_shift_grad: float32 [768], P(('dp', 'seq'))
- inner_grad: float32 [768, 3072], P(('dp', 'seq'))
- inner_bias_grad: float32 [3072], P(('dp', 'seq'))
- outer_grad: float32 [3072, 768], P(('dp', 'seq'))
- outer_bias_grad: float32 [768], P(('dp', 'seq'))
- second_gain_grad: float32 [768], P(('dp', 'seq'))
- second_shift_grad: float32 [768], P(('dp', 'seq'))
Inputs may be any that keep to these rules, and one draw needn't show every extreme that they name: `doc_lengths`: each row's 4 lengths sum to 1024; the largest of each row is exactly 768.
All inputs are finite; a program needn't handle non-finite values.
Results may differ from a plain program's by a relative error of at most 0.015.
The roundings to bfloat16 on the way count: a program that leaves them out, or rounds other values in their place, can miss the bound.
Values may be sent and summed in bfloat16 or wider, within the bound.
No kernel may reach another device: no remote copies, remote signals or barrier semaphores. Data moves between devices by JAX's collectives and lax.ppermute only.
A program may use at most 256 MiB of HBM per device.

v0:
```python
import functools

import jax
import jax.numpy as jnp
from jax import lax
from jax.experimental import pallas as pl
from jax.experimental.pallas import tpu as pltpu
from jax.sharding import Mesh
from jax.sharding import PartitionSpec as P

HEADS = 12
HEAD_DIM = 64
WIN = 128
PWIN = 512
EPS = 1e-05

LANES = 128
QB = 128
GROUP = 6
GROUP_BACK = 2
HALO = PWIN // 2
PAD = 16
NEAR = QB + WIN
FAR = (QB + PWIN) // 4
KEYS = NEAR + FAR
MASKED = -1e30
QUICK = pl.CostEstimate(flops=1 << 20, bytes_accessed=1 << 20, transcendentals=0)

F32 = jnp.float32
BF16 = jnp.bfloat16


def nt(left, right):
    return lax.dot_general(left, right, (((1,), (1,)), ((), ())), preferred_element_type=F32)


def tn(left, right):
    return lax.dot_general(left, right, (((0,), (0,)), ((), ())), preferred_element_type=F32)


def nn(left, right):
    return lax.dot_general(left, right, (((1,), (0,)), ((), ())), preferred_element_type=F32)


def slot_taps(wide, slots):
    return [wide[pl.ds(tap, slots, stride=4), :] for tap in range(5)]


def pool(taps, same_ref, w_ref, first, lanes):
    total = None
    for tap in range(5):
        term = taps[tap] * same_ref[0, tap] * w_ref[first + tap : first + tap + 1, lanes]
        total = term if total is None else total + term
    return total.astype(BF16)


def pair_stack(rows):
    lane = lax.broadcasted_iota(jnp.int32, rows.shape, 1)
    zero = jnp.zeros_like(rows)
    return jnp.concatenate(
        (jnp.where(lane < HEAD_DIM, rows, zero), jnp.where(lane < HEAD_DIM, zero, rows)), axis=0
    )


def pair_join(both):
    joined = jnp.concatenate((both[:HEAD_DIM, :QB], both[HEAD_DIM:, QB:]), axis=0)
    return joined.T


def rows_of(block):
    return slice(block * QB, (block + 1) * QB)


def keys_of(ref, pooled, block, lanes):
    near = HALO - WIN // 2 + block * QB
    far = block * QB // 4
    return jnp.concatenate((ref[0, near : near + NEAR, lanes], pooled[far : far + FAR, :]), axis=0)


def scores_of(keys, stacked, bias):
    return nt(keys, stacked) + jnp.concatenate((bias, bias), axis=1)


def attn_fwd_kernel(
    q_ref, k_ref, v_ref, w_ref, same_ref, bias_ref, out_ref, lse_ref, k_wide, v_wide, pk_ref, pv_ref
):
    slots = pk_ref.shape[1]
    scale = jnp.asarray(HEAD_DIM**-0.5, BF16)

    blocks = q_ref.shape[1] // QB

    def body(step, carry):
        jobs = []
        for lane in range(GROUP):
            pair = step * GROUP + lane
            lanes = pl.ds(pl.multiple_of(pair * LANES, LANES), LANES)
            k_wide[lane] = k_ref[0, :, lanes].astype(F32)
            v_wide[lane] = v_ref[0, :, lanes].astype(F32)
            pk_ref[lane] = pool(slot_taps(k_wide.at[lane], slots), same_ref, w_ref, 0, lanes)
            pv_ref[lane] = pool(slot_taps(v_wide.at[lane], slots), same_ref, w_ref, 5, lanes)
            jobs += [(lane, pair, lanes, block) for block in range(blocks)]
        scores = []
        for lane, pair, lanes, block in jobs:
            stacked = pair_stack(q_ref[0, rows_of(block), lanes] * scale)
            keys = keys_of(k_ref, pk_ref.at[lane], block, lanes)
            scores.append(scores_of(keys, stacked, bias_ref[0, block]))
        probs = []
        for (lane, pair, lanes, block), score in zip(jobs, scores):
            top = jnp.max(score, axis=0, keepdims=True)
            weights = jnp.exp(score - top)
            denom = jnp.sum(weights, axis=0, keepdims=True)
            probs.append((weights * (1.0 / denom)).astype(BF16))
            lse_ref[0, pair, block : block + 1, :] = top + jnp.log(denom)
        mixed = []
        for (lane, pair, lanes, block), prob in zip(jobs, probs):
            mixed.append(tn(keys_of(v_ref, pv_ref.at[lane], block, lanes), prob))
        for (lane, pair, lanes, block), value in zip(jobs, mixed):
            out_ref[0, rows_of(block), lanes] = pair_join(value).astype(BF16)
        return carry

    lax.fori_loop(0, q_ref.shape[2] // (LANES * GROUP), body, 0)


def attn_bwd_kernel(
    q_ref,
    k_ref,
    v_ref,
    w_ref,
    same_ref,
    bias_ref,
    lse_ref,
    do_ref,
    dq_ref,
    dk_ref,
    dv_ref,
    dw_ref,
    k_wide,
    v_wide,
    pk_ref,
    pv_ref,
    dpk_ref,
    dpv_ref,
):
    slots = pk_ref.shape[1]
    scale = jnp.asarray(HEAD_DIM**-0.5, BF16)
    blocks = q_ref.shape[1] // QB

    def body(step, carry):
        jobs = []
        for lane in range(GROUP_BACK):
            pair = step * GROUP_BACK + lane
            lanes = pl.ds(pl.multiple_of(pair * LANES, LANES), LANES)
            k_wide[lane] = k_ref[0, :, lanes].astype(F32)
            v_wide[lane] = v_ref[0, :, lanes].astype(F32)
            pk_ref[lane] = pool(slot_taps(k_wide.at[lane], slots), same_ref, w_ref, 0, lanes)
            pv_ref[lane] = pool(slot_taps(v_wide.at[lane], slots), same_ref, w_ref, 5, lanes)
            jobs += [(lane, pair, lanes, block) for block in range(blocks)]
        dpk_ref[...] = jnp.zeros_like(dpk_ref)
        dpv_ref[...] = jnp.zeros_like(dpv_ref)
        scores, d_probs = [], []
        for lane, pair, lanes, block in jobs:
            keys = keys_of(k_ref, pk_ref.at[lane], block, lanes)
            stacked = pair_stack(q_ref[0, rows_of(block), lanes] * scale)
            scores.append(scores_of(keys, stacked, bias_ref[0, block]))
            values = keys_of(v_ref, pv_ref.at[lane], block, lanes)
            d_probs.append(nt(values, pair_stack(do_ref[0, rows_of(block), lanes])))
        probs, d_scores = [], []
        for (lane, pair, lanes, block), score, d_prob in zip(jobs, scores, d_probs):
            prob = jnp.exp(score - lse_ref[0, pair, block : block + 1, :])
            row_dot = jnp.sum(prob * d_prob, axis=0, keepdims=True)
            d_scores.append((prob * (d_prob - row_dot)).astype(BF16))
            probs.append(prob.astype(BF16))
        parts = []
        for (lane, pair, lanes, block), prob, d_score in zip(jobs, probs, d_scores):
            d_values = nn(prob, pair_stack(do_ref[0, rows_of(block), lanes]))
            d_keys = nn(d_score, pair_stack(q_ref[0, rows_of(block), lanes] * scale))
            far = slice(block * QB // 4, block * QB // 4 + FAR)
            dpk_ref[lane, far, :] += d_keys[NEAR:]
            dpv_ref[lane, far, :] += d_values[NEAR:]
            parts.append((d_keys[:NEAR], d_values[:NEAR]))
        d_queries = []
        for (lane, pair, lanes, block), d_score in zip(jobs, d_scores):
            d_queries.append(tn(keys_of(k_ref, pk_ref.at[lane], block, lanes), d_score))
        for (lane, pair, lanes, block), value in zip(jobs, d_queries):
            dq_ref[0, rows_of(block), lanes] = (pair_join(value) * HEAD_DIM**-0.5).astype(BF16)
        for lane in range(GROUP_BACK):
            lanes = jobs[lane * blocks][2]
            for side, (wide_ref, d_pool_ref, out_ref) in enumerate(
                ((k_wide, dpk_ref, dk_ref), (v_wide, dpv_ref, dv_ref))
            ):
                wide = wide_ref.at[lane]
                d_pool = d_pool_ref[lane]
                taps = slot_taps(wide, slots)
                masked = [d_pool * same_ref[0, tap] for tap in range(5)]
                places = [5 * side + tap for tap in range(5)]
                for tap, row in enumerate(places):
                    dw_ref[0, row : row + 1, lanes] = jnp.sum(
                        masked[tap] * taps[tap], axis=0, keepdims=True
                    )
                spread = [
                    masked[tap] * w_ref[row : row + 1, lanes] for tap, row in enumerate(places)
                ]
                wide[4 * slots :, :] = jnp.zeros((wide.shape[0] - 4 * slots, LANES), F32)
                for tap in range(4):
                    wide[pl.ds(tap, slots, stride=4), :] = spread[tap]
                wide[pl.ds(4, slots, stride=4), :] += spread[4]
                for block in range(blocks):
                    near = HALO - WIN // 2 + block * QB
                    wide[near : near + NEAR, :] += parts[lane * blocks + block][side]
                out_ref[0, :, lanes] = wide[...].astype(BF16)
        return carry

    lax.fori_loop(0, q_ref.shape[2] // (LANES * GROUP_BACK), body, 0)
    dw_ref[0, 10:, :] = jnp.zeros((dw_ref.shape[1] - 10, dw_ref.shape[2]), F32)


def by_seq(*shape, first=0):
    return pl.BlockSpec((1,) + shape, lambda s: (s + first,) + (0,) * len(shape))


def attention_specs(ext, group, slots, width, first=0):
    return [
        by_seq(group, width, first=first),
        by_seq(ext, width, first=first),
        by_seq(ext, width, first=first),
        pl.BlockSpec((16, width), lambda s: (0, 0)),
        by_seq(5, slots, LANES, first=first),
        by_seq(group // QB, KEYS, LANES, first=first),
    ]


def attention_forward(queries, keys, values, taps, same, bias):
    seqs, group, width = queries.shape
    ext = keys.shape[1]
    slots = same.shape[2]
    pairs = width // LANES
    blocks = group // QB
    wide = pltpu.VMEM((GROUP, ext, LANES), F32)
    pooled = pltpu.VMEM((GROUP, slots, LANES), BF16)
    return pl.pallas_call(
        attn_fwd_kernel,
        grid=(seqs,),
        in_specs=attention_specs(ext, group, slots, width),
        out_specs=[by_seq(group, width), by_seq(pairs, blocks, 2 * QB)],
        out_shape=[
            jax.ShapeDtypeStruct((seqs, group, width), BF16),
            jax.ShapeDtypeStruct((seqs, pairs, blocks, 2 * QB), F32),
        ],
        scratch_shapes=[wide, wide, pooled, pooled],
        compiler_params=pltpu.CompilerParams(vmem_limit_bytes=60 << 20),
        cost_estimate=QUICK,
        name="attn_fwd",
    )(queries, keys, values, taps, same, bias)


def attention_backward(queries, keys, values, taps, same, bias, lse, d_mixed, first, count, earlier):
    seqs, group, width = queries.shape
    ext = keys.shape[1]
    slots = same.shape[2]
    pairs = width // LANES
    blocks = group // QB
    wide = pltpu.VMEM((GROUP_BACK, ext, LANES), F32)
    pooled = pltpu.VMEM((GROUP_BACK, slots, LANES), BF16)
    d_pooled = pltpu.VMEM((GROUP_BACK, slots, LANES), F32)
    args = (queries, keys, values, taps, same, bias, lse, d_mixed)

    def kernel(*refs):
        attn_bwd_kernel(*refs[: len(args)], *refs[len(args) + len(earlier) :])

    return pl.pallas_call(
        kernel,
        grid=(count,),
        in_specs=attention_specs(ext, group, slots, width, first)
        + [by_seq(pairs, blocks, 2 * QB, first=first), by_seq(group, width, first=first)]
        + [pl.BlockSpec(memory_space=pl.ANY)] * len(earlier),
        out_specs=[
            by_seq(*shape, first=first)
            for shape in ((group, width), (ext, width), (ext, width), (16, width))
        ],
        out_shape=[
            jax.ShapeDtypeStruct((seqs, group, width), BF16),
            jax.ShapeDtypeStruct((seqs, ext, width), BF16),
            jax.ShapeDtypeStruct((seqs, ext, width), BF16),
            jax.ShapeDtypeStruct((seqs, 16, width), F32),
        ],
        input_output_aliases={len(args) + i: i for i in range(len(earlier))},
        scratch_shapes=[wide, wide, pooled, pooled, d_pooled, d_pooled],
        compiler_params=pltpu.CompilerParams(vmem_limit_bytes=60 << 20),
        cost_estimate=QUICK,
        name="attn_bwd",
    )(*args, *earlier)


ROWS = 512
HALF_PI = 0.3989422804014327


def row_sum(value):
    return jnp.sum(value, axis=0, keepdims=True)


def row_mean(value):
    return jnp.mean(value, axis=1, keepdims=True)


def normalize(value):
    centered = value - row_mean(value)
    inv = lax.rsqrt(row_mean(centered * centered) + EPS)
    return centered * inv, inv


def normalize_back(grad, normed, inv):
    return inv * (grad - row_mean(grad) - normed * row_mean(grad * normed))


def ffn_kernel(
    panels,
    x_ref,
    mixed_ref,
    cot_ref,
    wo_ref,
    small_ref,
    bias_ref,
    w_in_ref,
    w_out_ref,
    y_ref,
    d_first_ref,
    d_mixed_ref,
    d_small_ref,
    d_bias_ref,
    d_weights_ref,
    n_one,
    inv_one,
    low,
    hidden,
    slope,
    d_inner,
    d_in_stage,
    d_out_stage,
    in_sems,
    out_sems,
):
    step = pl.program_id(0)
    tokens, width = x_ref.shape
    chunks = tokens // ROWS
    acc, d_outer = d_first_ref, d_mixed_ref
    units = d_weights_ref.shape[0]
    some = units // panels

    def in_copy(panel, slot):
        return pltpu.make_async_copy(
            d_in_stage.at[slot], d_weights_ref.at[:, panels + panel], in_sems.at[slot]
        )

    def out_copy(panel, slot):
        return pltpu.make_async_copy(
            d_out_stage.at[slot],
            d_weights_ref.at[pl.ds(panel * some, some), pl.ds(0, panels)],
            out_sems.at[slot],
        )

    def square(ref):
        return ref[...].reshape(width, width)

    gain_one, shift_one, outer_bias, gain_two, shift_two = (
        small_ref[i : i + 1, :] for i in range(5)
    )

    @pl.when(step == 0)
    def _():
        def body(i, carry):
            rows = pl.ds(pl.multiple_of(i * ROWS, ROWS), ROWS)
            first = x_ref[rows, :].astype(F32) + nn(mixed_ref[rows, :], square(wo_ref))
            normed, inv = normalize(first)
            n_one[rows, :] = normed
            inv_one[rows, :] = jnp.broadcast_to(inv, (ROWS, LANES))
            out = normed * gain_one + shift_one
            low[rows, :] = out.astype(BF16)
            acc[rows, :] = out + outer_bias
            return carry

        lax.fori_loop(0, chunks, body, 0)

    @pl.when(step < panels)
    def _():
        def body(i, carry):
            rows = pl.ds(pl.multiple_of(i * ROWS, ROWS), ROWS)
            inner = nn(low[rows, :], square(w_in_ref)) + bias_ref[0]
            cdf = 0.5 * (1.0 + lax.erf(inner * 0.7071067811865476))
            pdf = HALF_PI * jnp.exp(-0.5 * inner * inner)
            out = (inner * cdf).astype(BF16)
            hidden[step, rows, :] = out
            slope[step, rows, :] = cdf + inner * pdf
            acc[rows, :] += nn(out, square(w_out_ref))
            return carry

        lax.fori_loop(0, chunks, body, 0)

    @pl.when(step == panels)
    def _():
        def body(i, carry):
            d_gain, d_shift, d_bias = carry
            rows = pl.ds(pl.multiple_of(i * ROWS, ROWS), ROWS)
            normed, inv = normalize(acc[rows, :])
            y_ref[rows, :] = (normed * gain_two + shift_two).astype(BF16)
            grad = cot_ref[rows, :].astype(F32)
            d_second = normalize_back(grad * gain_two, normed, inv)
            low_grad = d_second.astype(BF16)
            acc[rows, :] = d_second
            d_outer[rows, :] = low_grad
            return (
                d_gain + row_sum(grad * normed),
                d_shift + row_sum(grad),
                d_bias + row_sum(low_grad.astype(F32)),
            )

        zero = jnp.zeros((1, width), F32)
        d_gain, d_shift, d_bias = lax.fori_loop(0, chunks, body, (zero, zero, zero))
        d_small_ref[2:3, :] = d_bias
        d_small_ref[3:4, :] = d_gain
        d_small_ref[4:5, :] = d_shift
        d_small_ref[5:, :] = jnp.zeros((3, width), F32)

    @pl.when(step >= panels)
    def _():
        panel = step - panels

        def body(i, d_bias):
            rows = pl.ds(pl.multiple_of(i * ROWS, ROWS), ROWS)
            d_hidden = nt(d_outer[rows, :], square(w_out_ref))
            grad = (d_hidden * slope[panel, rows, :]).astype(BF16)
            d_inner[rows, :] = grad
            acc[rows, :] += nt(grad, square(w_in_ref))
            return d_bias + row_sum(grad.astype(F32))

        d_bias_ref[0] = lax.fori_loop(0, chunks, body, jnp.zeros(d_bias_ref.shape[1:], F32))
        slot = lax.rem(panel, 2)

        @pl.when(panel >= 2)
        def _():
            in_copy(panel - 2, slot).wait()
            out_copy(panel - 2, slot).wait()

        d_out_stage[slot] = tn(hidden[panel], d_outer[...]).astype(BF16).reshape(d_out_stage.shape[1:])
        out_copy(panel, slot).start()
        d_in_stage[slot] = tn(low[...], d_inner[...]).astype(BF16).reshape(d_in_stage.shape[1:])
        in_copy(panel, slot).start()

    @pl.when(step == 2 * panels - 1)
    def _():
        def body(i, carry):
            d_gain, d_shift = carry
            rows = pl.ds(pl.multiple_of(i * ROWS, ROWS), ROWS)
            grad = acc[rows, :]
            normed = n_one[rows, :]
            d_first = normalize_back(grad * gain_one, normed, inv_one[rows, 0:1])
            d_first_ref[rows, :] = d_first
            low_grad = d_first.astype(BF16)
            d_inner[rows, :] = low_grad
            d_mixed_ref[rows, :] = nt(low_grad, square(wo_ref)).astype(BF16)
            return d_gain + row_sum(grad * normed), d_shift + row_sum(grad)

        zero = jnp.zeros((1, width), F32)
        d_gain, d_shift = lax.fori_loop(0, chunks, body, (zero, zero))
        d_small_ref[0:1, :] = d_gain
        d_small_ref[1:2, :] = d_shift
        slot = panels % 2
        in_copy(panels - 2, slot).wait()
        d_wo = tn(mixed_ref[...], d_inner[...])
        d_in_stage[slot] = d_wo.astype(BF16).reshape(d_in_stage.shape[1:])
        in_copy(panels, slot).start()
        out_copy(panels - 2, slot).wait()
        in_copy(panels - 1, 1 - slot).wait()
        out_copy(panels - 1, 1 - slot).wait()
        in_copy(panels, slot).wait()


def feed_forward(x, mixed, cot, small, bias, weights):
    tokens, width = x.shape
    units, groups, rows_in, _ = weights.shape
    panels = groups // 2
    panel = width

    def whole(*shape):
        return pl.BlockSpec(
            shape, lambda j: (0,) * len(shape), pipeline_mode=pl.Buffered(buffer_count=1)
        )

    def later(j):
        return jnp.maximum(j - panels, 0)

    return pl.pallas_call(
        functools.partial(ffn_kernel, panels),
        grid=(2 * panels,),
        in_specs=[
            whole(tokens, width),
            whole(tokens, width),
            whole(tokens, width),
            pl.BlockSpec(
                (units, 1, rows_in, width),
                lambda j: (0, 2 * panels, 0, 0),
                pipeline_mode=pl.Buffered(buffer_count=1),
            ),
            whole(8, width),
            pl.BlockSpec((1, 1, panel), lambda j: (lax.rem(j, panels), 0, 0)),
            pl.BlockSpec((units, 1, rows_in, width), lambda j: (0, panels + lax.rem(j, panels), 0, 0)),
            pl.BlockSpec(
                (units // panels, panels, rows_in, width), lambda j: (lax.rem(j, panels), 0, 0, 0)
            ),
        ],
        out_specs=[
            whole(tokens, width),
            whole(tokens, width),
            whole(tokens, width),
            whole(8, width),
            pl.BlockSpec((1, 1, panel), lambda j: (later(j), 0, 0)),
            pl.BlockSpec(memory_space=pl.ANY),
        ],
        out_shape=[
            jax.ShapeDtypeStruct((tokens, width), BF16),
            jax.ShapeDtypeStruct((tokens, width), F32),
            jax.ShapeDtypeStruct((tokens, width), BF16),
            jax.ShapeDtypeStruct((8, width), F32),
            jax.ShapeDtypeStruct((panels, 1, panel), F32),
            jax.ShapeDtypeStruct(weights.shape, BF16),
        ],
        scratch_shapes=[
            pltpu.VMEM((tokens, width), F32),
            pltpu.VMEM((tokens, LANES), F32),
            pltpu.VMEM((tokens, width), BF16),
            pltpu.VMEM((panels, tokens, panel), BF16),
            pltpu.VMEM((panels, tokens, panel), F32),
            pltpu.VMEM((tokens, panel), BF16),
            pltpu.VMEM((2, units, rows_in, width), BF16),
            pltpu.VMEM((2, units // panels, panels, rows_in, width), BF16),
            pltpu.SemaphoreType.DMA((2,)),
            pltpu.SemaphoreType.DMA((2,)),
        ],
        compiler_params=pltpu.CompilerParams(vmem_limit_bytes=60 << 20),
        cost_estimate=QUICK,
        name="ffn",
    )(x, mixed, cot, weights, small, bias, weights, weights)


def pack_kernel(outer_ref, inner_ref, out_ref, packed_ref):
    rows, width = outer_ref.shape
    share = out_ref.shape[0]
    packed_ref[:rows, :] = outer_ref[...]
    for panel in range(inner_ref.shape[1] // width):
        at = rows + panel * share
        packed_ref[at : at + share, :] = inner_ref[:, panel * width : (panel + 1) * width]
    packed_ref[packed_ref.shape[0] - share :, :] = out_ref[...]


def pack(outer, inner, out):
    share, width = out.shape
    panels = inner.shape[1] // width
    if share % 8:
        inner = inner.reshape(share, panels, width).swapaxes(0, 1).reshape(-1, width)
        return jnp.concatenate((outer, inner, out), axis=0)
    rows = outer.shape[0] + (panels + 1) * share
    return pl.pallas_call(
        pack_kernel,
        out_shape=jax.ShapeDtypeStruct((rows, width), BF16),
        cost_estimate=QUICK,
        name="pack",
    )(outer, inner, out)


SOON = 160
SMALL = 16


def small_block(taps, vectors, bias, width):
    share = taps.shape[1]
    rows = jnp.concatenate([taps.astype(F32)] + [v.astype(F32) for v in vectors], axis=0)
    rows = jnp.concatenate((rows, jnp.zeros((rows.shape[0], width - share), F32)), axis=1)
    bias = bias.astype(F32)
    last = jnp.concatenate((bias, jnp.zeros((1, width - bias.shape[1]), F32)), axis=1)
    return jnp.concatenate((rows, last), axis=0).astype(BF16)


def stack_kernel(q_ref, k_ref, v_ref, taps_ref, a_ref, b_ref, c_ref, d_ref, e_ref, bias_ref, out_ref):
    share, width = q_ref.shape
    for place, ref in enumerate((q_ref, k_ref, v_ref)):
        out_ref[place * share : (place + 1) * share, :] = ref[...]
    vectors = [ref[...] for ref in (a_ref, b_ref, c_ref, d_ref, e_ref)]
    out_ref[3 * share :, :] = small_block(taps_ref[...], vectors, bias_ref[...], width)


def stack(query, key, value, taps, vectors, bias):
    share, width = query.shape
    vectors = [v.reshape(1, -1) for v in vectors]
    bias = bias.reshape(1, -1)
    if share % 8:
        return jnp.concatenate((query, key, value, small_block(taps, vectors, bias, width)), axis=0)
    return pl.pallas_call(
        stack_kernel,
        out_shape=jax.ShapeDtypeStruct((3 * share + SMALL, width), BF16),
        cost_estimate=QUICK,
        name="stack",
    )(query, key, value, taps, *vectors, bias)


def square_of(w_ref, place):
    units, _, width = w_ref.shape
    part = width // units
    return w_ref[:, place * part : (place + 1) * part, :].reshape(width, width)


def project_own_kernel(x_ref, w_ref, q_ref, k_ref, v_ref):
    for place, ref in enumerate((q_ref, k_ref, v_ref)):
        ref[0] = nn(x_ref[0], square_of(w_ref, place)).astype(BF16)


def project_halos_kernel(
    x_ref, own_k_ref, own_v_ref, left_ref, right_ref, far_ref, w_ref, k_ref, v_ref, ext_ref
):
    group, width = x_ref.shape[1:]
    right = HALO + group
    ext_ref[0, :HALO, :] = left_ref[0]
    ext_ref[0, HALO:right, :] = x_ref[0]
    ext_ref[0, right : right + HALO, :] = right_ref[0]
    row = lax.broadcasted_iota(jnp.int32, (PAD, width), 0)
    far = jnp.where(row == 0, jnp.broadcast_to(far_ref[0].astype(F32), (PAD, width)), 0.0)
    ext_ref[0, right + HALO :, :] = far.astype(BF16)
    halos = jnp.concatenate((ext_ref[0, :HALO, :], ext_ref[0, right:, :]), axis=0)
    for place, own_ref, ref in ((1, own_k_ref, k_ref), (2, own_v_ref, v_ref)):
        rows = nn(halos, square_of(w_ref, place)).astype(BF16)
        ref[0, :HALO, :] = rows[:HALO]
        ref[0, HALO:right, :] = own_ref[0]
        ref[0, right:, :] = rows[HALO:]


def resident(*shape):
    return pl.BlockSpec(
        shape, lambda s: (0,) * len(shape), pipeline_mode=pl.Buffered(buffer_count=1)
    )


def project_own(x, weights):
    seqs, group, width = x.shape
    return pl.pallas_call(
        project_own_kernel,
        grid=(seqs,),
        in_specs=[by_seq(group, width), resident(*weights.shape)],
        out_specs=[by_seq(group, width)] * 3,
        out_shape=[jax.ShapeDtypeStruct(x.shape, BF16)] * 3,
        compiler_params=pltpu.CompilerParams(vmem_limit_bytes=60 << 20),
        cost_estimate=QUICK,
        name="project_own",
    )(x, weights)


def project_halos(x, own_keys, own_values, left, right, far, weights):
    seqs, group, width = x.shape
    ext = group + 2 * HALO + PAD
    return pl.pallas_call(
        project_halos_kernel,
        grid=(seqs,),
        in_specs=[by_seq(group, width)] * 3
        + [by_seq(HALO, width), by_seq(HALO, width), by_seq(1, width), resident(*weights.shape)],
        out_specs=[by_seq(ext, width)] * 3,
        out_shape=[jax.ShapeDtypeStruct((seqs, ext, width), BF16)] * 3,
        compiler_params=pltpu.CompilerParams(vmem_limit_bytes=60 << 20),
        cost_estimate=QUICK,
        name="project_halos",
    )(x, own_keys, own_values, left, right, far, weights)


def input_grad_kernel(
    dq_ref, dk_ref, dv_ref, first_ref, w_ref, a_ref, b_ref, c_ref, d_ref, far_ref, own_ref
):
    right = HALO + dq_ref.shape[1]
    grad = nt(dk_ref[0], square_of(w_ref, 1)) + nt(dv_ref[0], square_of(w_ref, 2))
    for ref, at in ((a_ref, 0), (b_ref, right), (c_ref, SOON), (d_ref, right + SOON)):
        ref[0] = grad[at : at + ref.shape[1]].astype(BF16)
    far_ref[0] = grad[right + HALO : right + HALO + 1].astype(BF16)
    own_ref[0] = grad[HALO:right] + nt(dq_ref[0], square_of(w_ref, 0)) + first_ref[0]


def input_grads(d_queries, d_keys, d_values, d_first, weights):
    seqs, group, width = d_queries.shape
    ext = d_keys.shape[1]
    rows = (SOON, SOON, HALO - SOON, HALO - SOON)
    return pl.pallas_call(
        input_grad_kernel,
        grid=(seqs,),
        in_specs=[
            by_seq(group, width),
            by_seq(ext, width),
            by_seq(ext, width),
            by_seq(group, width),
            resident(*weights.shape),
        ],
        out_specs=[by_seq(n, width) for n in rows + (1, group)],
        out_shape=[jax.ShapeDtypeStruct((seqs, n, width), BF16) for n in rows + (1,)]
        + [jax.ShapeDtypeStruct((seqs, group, width), F32)],
        compiler_params=pltpu.CompilerParams(vmem_limit_bytes=60 << 20),
        cost_estimate=QUICK,
        name="input_grads",
    )(d_queries, d_keys, d_values, d_first, weights)


def weight_grad_kernel(
    x_ref, dq_ref, dk_ref, dv_ref, small_ref, out_ref, acc, x_tail, dk_tail, dv_tail
):
    seq = pl.program_id(0)
    group, width = dq_ref.shape[1:]
    units = out_ref.shape[0]
    part = width // units
    main = 2 * HALO + group

    @pl.when(seq == 0)
    def _():
        acc[...] = jnp.zeros_like(acc)

    rows = pl.ds(pl.multiple_of(seq * PAD, PAD), PAD)
    for tail, ref in ((x_tail, x_ref), (dk_tail, dk_ref), (dv_tail, dv_ref)):
        tail[rows, :] = ref[0, main:, :]
    acc[0] += tn(x_ref[0, HALO : HALO + group, :], dq_ref[0])
    acc[1] += tn(x_ref[0, :main, :], dk_ref[0, :main, :])
    acc[2] += tn(x_ref[0, :main, :], dv_ref[0, :main, :])

    @pl.when(seq == pl.num_programs(0) - 1)
    def _():
        ends = (None, tn(x_tail[...], dk_tail[...]), tn(x_tail[...], dv_tail[...]))
        for place, end in enumerate(ends):
            total = acc[place] if end is None else acc[place] + end
            out_ref[:, place * part : (place + 1) * part, :] = total.astype(BF16).reshape(
                units, part, width
            )
        out_ref[:, 3 * part :, :] = small_ref[...]


def weight_grads(x_ext, d_queries, d_keys, d_values, small):
    seqs, group, width = d_queries.shape
    ext = x_ext.shape[1]
    units, small_rows, _ = small.shape
    shape = (units, 3 * (width // units) + small_rows, width)
    tail = pltpu.VMEM((seqs * PAD, width), BF16)
    return pl.pallas_call(
        weight_grad_kernel,
        grid=(seqs,),
        in_specs=[
            by_seq(ext, width),
            by_seq(group, width),
            by_seq(ext, width),
            by_seq(ext, width),
            resident(*small.shape),
        ],
        out_specs=resident(*shape),
        out_shape=jax.ShapeDtypeStruct(shape, BF16),
        scratch_shapes=[pltpu.VMEM((3, width, width), F32), tail, tail, tail],
        compiler_params=pltpu.CompilerParams(vmem_limit_bytes=60 << 20),
        cost_estimate=QUICK,
        name="weight_grads",
    )(x_ext, d_queries, d_keys, d_values, small)


def document_of(positions, lengths, seq_len):
    count = lengths.shape[1]
    order = jnp.arange(count)
    ends = jnp.sum(jnp.where(order[None, :] <= order[:, None], lengths[:, None, :], 0), axis=2)
    counted = jnp.sum((positions[None, :, None] >= ends[:, None, :]).astype(jnp.int32), axis=2)
    inside = (positions >= 0) & (positions < seq_len)
    return jnp.where(inside[None, :], counted, -1)


def masks(lengths, offset, group, seq_len):
    ext = group + 2 * HALO
    slots = ext // 4
    positions = offset - HALO + jnp.arange(ext + PAD, dtype=jnp.int32)
    doc = document_of(positions, lengths, seq_len)
    slot_doc = doc[:, 2:ext:4]
    biases = []
    for block in range(group // QB):
        near = HALO - WIN // 2 + block * QB
        far = block * QB // 4
        key_place = jnp.concatenate((jnp.arange(near, near + NEAR), 4 * jnp.arange(far, far + FAR) + 2))
        reach = jnp.concatenate((jnp.full((NEAR,), WIN // 2), jnp.full((FAR,), PWIN // 2)))
        key_doc = jnp.concatenate((doc[:, near : near + NEAR], slot_doc[:, far : far + FAR]), axis=1)
        query_place = HALO + block * QB + jnp.arange(QB)
        query_doc = doc[:, HALO + block * QB : HALO + (block + 1) * QB]
        allowed = (jnp.abs(key_place[:, None] - query_place[None, :]) <= reach[:, None])[None] & (
            key_doc[:, :, None] == query_doc[:, None, :]
        )
        biases.append(jnp.where(allowed, 0.0, MASKED).astype(F32))
    same = jnp.stack(
        [(doc[:, tap : tap + ext : 4] == slot_doc).astype(F32) for tap in range(5)], axis=1
    )
    same = jnp.broadcast_to(same[..., None], same.shape + (LANES,))
    return jnp.stack(biases, axis=1), same, slots


def steps(count):
    for k in range(1, count):
        if count & (count - 1) == 0:
            yield [(i, i ^ k) for i in range(count)], lambda me, k=k: (me ^ k, me ^ k)
        else:
            yield (
                [(i, (i + k) % count) for i in range(count)],
                lambda me, k=k: (lax.rem(me + k, count), lax.rem(me - k + count, count)),
            )


def pick(value, index, dim=0):
    return lax.dynamic_index_in_dim(value, index, dim, keepdims=False)


def gather_seq(block, *earlier):
    count, me = lax.axis_size("seq"), lax.axis_index("seq")
    zeros = (0,) * block.ndim
    came_all = after(tuple(lax.ppermute(block, "seq", pairs) for pairs, _ in steps(count)), *earlier)
    column = jnp.zeros((count,) + block.shape, block.dtype)
    column = lax.dynamic_update_slice(column, block[None], (me,) + zeros)
    for came, (_, met) in zip(came_all, steps(count)):
        column = lax.dynamic_update_slice(column, came[None], (met(me)[1],) + zeros)
    return column


def gather_yx(column):
    me = lax.axis_index("yx")
    pieces = [(column, me)]
    for pairs, met in steps(lax.axis_size("yx")):
        pieces.append((lax.ppermute(column, "yx", pairs), met(me)[1]))
    return pieces


def assemble_kernel(count, *refs):
    places, parts, whole, sems = refs[0], refs[1 : 1 + count], refs[-2], refs[-1]
    copies = [
        pltpu.make_async_copy(part, whole.at[places[i]], sems.at[i]) for i, part in enumerate(parts)
    ]
    for copy in copies:
        copy.start()
    for copy in copies:
        copy.wait()


def gather_core(pieces):
    count, me = lax.axis_size("core"), lax.axis_index("core")
    parts, places = [], []
    for piece, place in pieces:
        parts.append(piece)
        places.append(place * count + me)
        for pairs, met in steps(count):
            parts.append(lax.ppermute(piece, "core", pairs))
            places.append(place * count + met(me)[1])
    return pl.pallas_call(
        functools.partial(assemble_kernel, len(parts)),
        in_specs=[pl.BlockSpec(memory_space=pltpu.SMEM)]
        + [pl.BlockSpec(memory_space=pltpu.VMEM)] * len(parts),
        out_specs=pl.BlockSpec(memory_space=pl.ANY),
        out_shape=jax.ShapeDtypeStruct((len(parts),) + parts[0].shape, BF16),
        compiler_params=pltpu.CompilerParams(vmem_limit_bytes=60 << 20),
        scratch_shapes=[pltpu.SemaphoreType.DMA((len(parts),))],
        cost_estimate=QUICK,
        name="assemble",
    )(jnp.stack(places).astype(jnp.int32), *parts)


def after(value, *earlier):
    return lax.optimization_barrier((value, earlier))[0] if earlier else lax.optimization_barrier(value)


def exchange_sum(pieces, axis, *earlier):
    me = lax.axis_index(axis)
    came = [
        lax.ppermute(pick(pieces, met(me)[0]), axis, pairs)
        for pairs, met in steps(lax.axis_size(axis))
    ]
    total = pick(pieces, me).astype(F32)
    for part in after(came, *earlier):
        total = total + part.astype(F32)
    return total


def local(
    tokens,
    doc_lengths,
    query_weight,
    key_weight,
    value_weight,
    out_weight,
    pool_weight,
    first_gain,
    first_shift,
    inner_weight,
    inner_bias,
    outer_weight,
    outer_bias,
    second_gain,
    second_shift,
    cotangent,
):
    seq_count = lax.axis_size("seq")
    yx_count = lax.axis_size("yx")
    core_count = lax.axis_size("core")
    units = yx_count * core_count
    parts = units * seq_count
    seq_place = lax.axis_index("seq")
    seqs, group, width = tokens.shape
    ff = inner_weight.shape[1]
    panels = ff // width
    share = query_weight.shape[0]
    count = seqs * group

    def shift(value, by):
        pairs = [(i, i + by) for i in range(seq_count) if 0 <= i + by < seq_count]
        return lax.ppermute(value, "seq", pairs)

    early = stack(
        query_weight,
        key_weight,
        value_weight,
        pool_weight,
        (first_gain, first_shift, outer_bias, second_gain, second_shift),
        inner_bias,
    )
    late = pack(outer_weight, inner_weight, out_weight)
    bias, same, _ = masks(doc_lengths, seq_place * group, group, group * seq_count)
    early_column, bias, same = after((gather_seq(early), bias, same))
    sent = after(tokens, early_column)
    came = (
        shift(sent[:, group - HALO :], 1),
        shift(sent[:, :HALO], -1),
        shift(sent[:, :1], -2),
    )
    early_column = jnp.concatenate(
        [early_column[:, i * share : (i + 1) * share].reshape(-1, width) for i in range(3)]
        + [early_column[:, 3 * share :].reshape(-1, width)],
        axis=0,
    )
    early_pieces = gather_yx(early_column)
    early = gather_core(early_pieces)
    late_column = lax.all_gather(late, "seq", axis=0)
    late_column = after(late_column, [piece for piece, _ in early_pieces[1:]])
    outer_rows = panels * share
    late_column = jnp.concatenate(
        (
            late_column[:, :outer_rows].reshape(-1, width),
            late_column[:, outer_rows:]
            .reshape(seq_count, panels + 1, share, width)
            .swapaxes(0, 1)
            .reshape(-1, width),
        ),
        axis=0,
    )
    late = lax.all_gather(late_column, ("yx", "core"), axis=0)
    late = late.reshape(units, 2 * panels + 1, seq_count * share, width)
    small = early[:, 3 * seq_count * share :].reshape(parts, SMALL, width)
    vectors = small[:, : SMALL - 1, :share].transpose(1, 0, 2).reshape(SMALL - 1, width).astype(F32)
    taps = jnp.pad(vectors[:10], ((0, 6), (0, 0)))
    small_rows_f32 = jnp.pad(vectors[10:], ((0, 3), (0, 0)))
    bias_inner = small[:, SMALL - 1, : ff // parts].reshape(panels, 1, width).astype(F32)

    flat = tokens.reshape(count, width)

    queries, own_keys, own_values = project_own(tokens, early)
    keys, values, x_ext = project_halos(tokens, own_keys, own_values, *came, early)
    mixed, lse = attention_forward(queries, keys, values, taps, same, bias)
    y, d_first, d_mixed, d_small, d_bias, d_late = feed_forward(
        flat,
        mixed.reshape(count, width),
        cotangent.reshape(count, width),
        small_rows_f32,
        bias_inner,
        late,
    )
    late_sum = lax.psum_scatter(
        d_late.reshape(-1, width), ("yx", "core"), scatter_dimension=0, tiled=True
    )
    d_queries, d_keys, d_values, d_taps = attention_backward(
        queries,
        keys,
        values,
        taps,
        same,
        bias,
        lse,
        d_mixed.reshape(seqs, group, width),
        0,
        seqs,
        (),
    )
    left_a, right_a, left_b, right_b, far, own = input_grads(
        d_queries, d_keys, d_values, d_first.reshape(seqs, group, width), early
    )
    came = (shift(left_a, -1), shift(right_a, 1))
    later_came = (shift(left_b, -1), shift(right_b, 1), shift(far, 2))

    d_taps = jnp.sum(d_taps, axis=0)[:10]
    d_vectors = jnp.concatenate((d_taps, d_small[:5]), axis=0)
    d_vectors = d_vectors.reshape(SMALL - 1, parts, share).transpose(1, 0, 2)
    d_vectors = jnp.pad(d_vectors, ((0, 0), (0, 0), (0, width - share)))
    d_bias = jnp.pad(d_bias.reshape(parts, 1, -1), ((0, 0), (0, 0), (0, width - ff // parts)))
    d_vectors = jnp.concatenate((d_vectors, d_bias), axis=1).astype(BF16)
    d_vectors = d_vectors.reshape(units, seq_count * SMALL, width)
    early_sum = weight_grads(after(x_ext, own), d_queries, d_keys, d_values, d_vectors)
    early_sum = early_sum.reshape(yx_count, core_count, -1, width)
    early_sum, came = after((early_sum, came))
    early_sum = exchange_sum(early_sum.swapaxes(0, 1), "core").astype(BF16)
    outer_all = seq_count * outer_rows
    late_sum = jnp.concatenate(
        (
            late_sum[:outer_all].reshape(seq_count, outer_rows, width),
            late_sum[outer_all:]
            .reshape(panels + 1, seq_count, share, width)
            .swapaxes(0, 1)
            .reshape(seq_count, (panels + 1) * share, width),
        ),
        axis=1,
    )
    late_sum = exchange_sum(late_sum, "seq")
    early_sum = exchange_sum(early_sum, "yx", late_sum, later_came).astype(BF16)
    whole = 3 * seq_count * share
    early_sum = jnp.concatenate(
        [
            early_sum[:whole]
            .reshape(3, seq_count, share, width)
            .swapaxes(0, 1)
            .reshape(seq_count, 3 * share, width),
            early_sum[whole:].reshape(seq_count, SMALL, width),
        ],
        axis=1,
    )
    early_sum = exchange_sum(early_sum, "seq")

    edge = group - HALO
    from_right, from_left = (
        jnp.concatenate(parts, axis=1).astype(F32) for parts in zip(came, later_came)
    )
    from_far = later_came[2].astype(F32)
    d_input = own + jnp.pad(from_right, ((0, 0), (edge, 0), (0, 0)))
    d_input = d_input + jnp.pad(from_left, ((0, 0), (0, edge), (0, 0)))
    d_input = d_input + jnp.pad(from_far, ((0, 0), (0, group - 1), (0, 0)))

    vector_sum = early_sum[3 * share :]
    pieces = [vector_sum[10 + i, :share] for i in range(5)]
    return (
        y.reshape(seqs, group, width),
        d_input.astype(BF16),
        early_sum[:share],
        early_sum[share : 2 * share],
        early_sum[2 * share : 3 * share],
        late_sum[2 * outer_rows :],
        vector_sum[:10, :share],
        pieces[0],
        pieces[1],
        late_sum[outer_rows : 2 * outer_rows]
        .reshape(panels, share, width)
        .transpose(1, 0, 2)
        .reshape(share, ff),
        vector_sum[SMALL - 1, : ff // parts],
        late_sum[:outer_rows],
        pieces[2],
        pieces[3],
        pieces[4],
    )


def solution(mesh):
    dp, seq = mesh.devices.shape
    cores = 2 if dp % 2 == 0 else 1
    mesh = Mesh(mesh.devices.reshape(dp // cores, cores, seq), ("yx", "core", "seq"))
    every = ("yx", "core", "seq")
    rows = P(every, None)
    vector = P(every)
    whole = P(("yx", "core"), "seq", None)
    taps = P(None, every)
    weights = (rows, rows, rows, rows, taps, vector, vector, rows, vector, rows, vector, vector, vector)
    return jax.shard_map(
        local,
        mesh=mesh,
        in_specs=(whole, P(("yx", "core"), None)) + weights + (whole,),
        out_specs=(whole, whole) + weights,
        check_vma=False,
    )
```

profile of v0, /device:TPU:16, one launch (start us, length us, event | category | flops | bytes accessed | tf_op | source)
XLA Modules:
  0.0 329.8 jit_solution(7047691928635604176)
XLA Ops:
  7.2 1.5 stack.76
  9.2 3.5 %collective-permute-start.1 = (bf16[88,768]{1,0:T(8,128)(2,1)}, bf16[88,768]{1,0:T(8,128)(2,1)S(1)}, u32[]{:S(2)}, u32[]{:S(2)}) collective-permute-start(bf16[88,768]{1,0:T(8,128)(2,1)} %stack.76), channel_id=1, source_target_pairs={{0,2},{1,3},{2,0},{3,1},{4,6},{5,7},{6,4},{7,5},{8,10},{9,11},{10,... | collective-permute-start | bytes 405512 | tf_op jit(solution)/shard_map/ppermute | solution.py:814
  12.7 1.7 pack.1
  14.6 0.8 select_reduce_fusion
  17.2 0.9 abs_compare_fusion.1
  18.8 1.3 pad_maximum_fusion.bias_ref.refs_5_
  20.2 1.1 collective-permute-done.2
  21.3 1.8 broadcast_in_dim.87.same_ref.refs_4_
  23.2 2.5 collective-permute-start.8
  26.8 12.7 %collective-permute-done.8.refs_7_ = bf16[352,768]{1,0:T(8,128)(2,1)S(1)} collective-permute-done((bf16[352,768]{1,0:T(8,128)(2,1)S(1)}, bf16[352,768]{1,0:T(8,128)(2,1)S(1)}, u32[]{:S(2)}, u32[]{:S(2)}) %collective-permute-start.8) | collective-permute-done | bytes 540704 | tf_op jit(solution)/shard_map/ppermute | solution.py:826
  39.5 9.5 %collective-permute-done.6.refs_5_ = bf16[352,768]{1,0:T(8,128)(2,1)S(1)} collective-permute-done((bf16[352,768]{1,0:T(8,128)(2,1)S(1)}, bf16[352,768]{1,0:T(8,128)(2,1)S(1)}, u32[]{:S(2)}, u32[]{:S(2)}) %collective-permute-start.6) | collective-permute-done | bytes 540704 | tf_op jit(solution)/shard_map/ppermute | solution.py:826
  49.1 1.1 slice.166
  50.3 1.2 slice.167
  51.5 1.2 pad_maximum_fusion.1
  52.8 0.6 copy-done.1
  53.4 3.3 %collective-permute-start.11 = (bf16[4,256,768]{2,1,0:T(8,128)(2,1)S(1)}, bf16[4,256,768]{2,1,0:T(8,128)(2,1)}, u32[]{:S(2)}, u32[]{:S(2)}) collective-permute-start(bf16[4,256,768]{2,1,0:T(8,128)(2,1)S(1)} %copy-done.1), channel_id=1, source_target_pairs={{1,0},{2,1},{3,2},{5,4},{6,5},{7,6},{9,8},{10,9},{11,10},{13,12},{... | collective-permute-start | bytes 4718600 | tf_op jit(solution)/shard_map/ppermute | solution.py:911
  56.7 4.3 %collective-permute-start.10 = (bf16[4,256,768]{2,1,0:T(8,128)(2,1)S(1)}, bf16[4,256,768]{2,1,0:T(8,128)(2,1)}, u32[]{:S(2)}, u32[]{:S(2)}) collective-permute-start(bf16[4,256,768]{2,1,0:T(8,128)(2,1)S(1)} %copy-done.1), channel_id=1, source_target_pairs={{0,1},{1,2},{2,3},{4,5},{5,6},{6,7},{8,9},{9,10},{10,11},{12,13},{... | collective-permute-start | bytes 4718600 | tf_op jit(solution)/shard_map/ppermute | solution.py:911
  61.6 1.3 collective-permute-done.3.refs_2_
  63.0 0.8 copy-done.9
  63.9 0.6 stack.67.refs_0_
  64.5 4.7 %collective-permute-start.12 = (bf16[4,1,768]{2,1,0:T(2,128)(2,1)S(1)}, bf16[4,1,768]{2,1,0:T(2,128)(2,1)S(1)}, u32[]{:S(2)}, u32[]{:S(2)}) collective-permute-start(bf16[4,1,768]{2,1,0:T(2,128)(2,1)S(1)} %slice.161), channel_id=1, source_target_pairs={{2,0},{3,1},{6,4},{7,5},{10,8},{11,9},{14,12},{15,13},{18,16},{19,... | collective-permute-start | bytes 18440 | tf_op jit(solution)/shard_map/ppermute | solution.py:911
  69.3 0.8 copy-done.10
  70.1 4.3 %assemble.1.w_ref = bf16[8,352,768]{2,1,0:T(8,128)(2,1)} custom-call(s32[8]{0:T(128)} %stack.67.refs_0_, bf16[352,768]{1,0:T(8,128)(2,1)} %copy-done.4, bf16[352,768]{1,0:T(8,128)(2,1)} %copy-done.9, bf16[352,768]{1,0:T(8,128)(2,1)} %collective-permute-done.4.refs_3_, bf16[352,768]{1,0:T(8,128)(2,1)} %copy-done.10, bf16[352,768]{1,0:T(8,128)(2,1)} %copy-done.8, ...), custom_call_target="tpu_custom_call" | custom-call | flops 1048576 | bytes 1048576 | tf_op jit(solution)/shard_map/assemble/pallas_call | solution.py:850
  74.4 1.2 slice.196
  75.7 0.7 reshape.321.bias_ref
  76.6 0.6 pad.25.w_ref.refs_3_
  77.3 0.6 pad.26.small_ref
  77.9 7.5 %project_own.1 = (bf16[4,256,768]{2,1,0:T(8,128)(2,1)}, bf16[4,256,768]{2,1,0:T(8,128)(2,1)}, bf16[4,256,768]{2,1,0:T(8,128)(2,1)}) custom-call(bf16[4,256,768]{2,1,0:T(8,128)(2,1)} %x_ref.3, bf16[8,352,768]{2,1,0:T(8,128)(2,1)} %assemble.1.w_ref), custom_call_target="tpu_custom_call" | custom-call | flops 1048576 | bytes 1048576 | tf_op jit(solution)/shard_map/project_own/pallas_call | solution.py:643
  85.4 5.4 %collective-permute-done.12.far_ref = bf16[4,1,768]{2,1,0:T(2,128)(2,1)S(1)} collective-permute-done((bf16[4,1,768]{2,1,0:T(2,128)(2,1)S(1)}, bf16[4,1,768]{2,1,0:T(2,128)(2,1)S(1)}, u32[]{:S(2)}, u32[]{:S(2)}) %collective-permute-start.12) | collective-permute-done | bytes 6176 | tf_op jit(solution)/shard_map/ppermute | solution.py:911
  90.9 1.9 collective-permute-done.11.right_ref
  92.8 2.8 collective-permute-done.10.left_ref
  95.5 12.7 %project_halos.1 = (bf16[4,784,768]{2,1,0:T(8,128)(2,1)}, bf16[4,784,768]{2,1,0:T(8,128)(2,1)}, bf16[4,784,768]{2,1,0:T(8,128)(2,1)}) custom-call(bf16[4,256,768]{2,1,0:T(8,128)(2,1)} %x_ref.3, bf16[4,256,768]{2,1,0:T(8,128)(2,1)} %get-tuple-element.65.own_k_ref, bf16[4,256,768]{2,1,0:T(8,128)(2,1)} %get-tuple-element.66.own_v_ref, ...), custom_call_target="tpu_custom_call" | custom-call | flops 1048576 | bytes 1048576 | tf_op jit(solution)/shard_map/project_halos/pallas_call | solution.py:658
  108.3 16.5 %attn_fwd.1 = (bf16[4,256,768]{2,1,0:T(8,128)(2,1)}, f32[4,6,2,256]{3,2,1,0:T(2,128)}) custom-call(bf16[4,256,768]{2,1,0:T(8,128)(2,1)} %get-tuple-element.64.q_ref.refs_0_, bf16[4,784,768]{2,1,0:T(8,128)(2,1)} %get-tuple-element.68.k_ref.refs_1_, bf16[4,784,768]{2,1,0:T(8,128)(2,1)} %get-tuple-element.69.v_ref.refs_2_, f32[16,768]{1,0:T(8,128)} %pad.25.w_ref.refs_3_, ...), custom_call_target="tpu_custom_call" | custom-call | flops 1048576 | bytes 1048576 | tf_op jit(solution)/shard_map/attn_fwd/pallas_call | solution.py:240
  124.8 55.2 %ffn.1 = (bf16[1024,768]{1,0:T(8,128)(2,1)}, f32[1024,768]{1,0:T(8,128)}, bf16[1024,768]{1,0:T(8,128)(2,1)}, f32[8,768]{1,0:T(8,128)}, f32[4,1,768]{2,1,0:T(1,128)}, /*index=5*/bf16[8,9,96,768]{3,2,1,0:T(8,128)(2,1)}) custom-call(bf16[1024,768]{1,0:T(8,128)(2,1)} %bitcast.127, bf16[1024,768]{1,0:T(8,128)(2,1)} %bitcast.143, bf16[1024,768]{1,0:T(8,128)(2,1)} %bitcast.142, ...), custom_call_target="tpu_custom_call" | custom-call | flops 1048576 | bytes 1048576 | tf_op jit(solution)/shard_map/ffn/pallas_call | solution.py:492
  180.1 28.8 %attn_bwd.1 = (bf16[4,256,768]{2,1,0:T(8,128)(2,1)}, bf16[4,784,768]{2,1,0:T(8,128)(2,1)}, bf16[4,784,768]{2,1,0:T(8,128)(2,1)}, f32[4,16,768]{2,1,0:T(8,128)}) custom-call(bf16[4,256,768]{2,1,0:T(8,128)(2,1)} %get-tuple-element.64.q_ref.refs_0_, bf16[4,784,768]{2,1,0:T(8,128)(2,1)} %get-tuple-element.68.k_ref.refs_1_, ...), custom_call_target="tpu_custom_call" | custom-call | flops 1048576 | bytes 1048576 | tf_op jit(solution)/shard_map/attn_bwd/pallas_call | solution.py:270
  208.9 14.6 %input_grads.1 = (bf16[4,160,768]{2,1,0:T(8,128)(2,1)}, bf16[4,160,768]{2,1,0:T(8,128)(2,1)}, bf16[4,96,768]{2,1,0:T(8,128)(2,1)}, bf16[4,96,768]{2,1,0:T(8,128)...) custom-call(bf16[4,256,768]{2,1,0:T(8,128)(2,1)} %get-tuple-element.77.dq_ref, ...), custom_call_target="tpu_custom_call" | custom-call | flops 1048576 | bytes 1048576 | tf_op jit(solution)/shard_map/input_grads/pallas_call | solution.py:686
  223.5 3.6 %collective-permute-start.13 = (bf16[4,160,768]{2,1,0:T(8,128)(2,1)}, bf16[4,160,768]{2,1,0:T(8,128)(2,1)S(1)}, u32[]{:S(2)}, u32[]{:S(2)}) collective-permute-start(bf16[4,160,768]{2,1,0:T(8,128)(2,1)} %get-tuple-element.87), channel_id=1, source_target_pairs={{1,0},{2,1},{3,2},{5,4},{6,5},{7,6},{9,8},{10,9},{11,10},{13,12},{... | collective-permute-start | bytes 2949128 | tf_op jit(solution)/shard_map/ppermute | solution.py:911
  227.1 2.3 collective-permute-start.14
  229.9 1.4 copy.51
  231.3 15.5 %weight_grads.1 = bf16[8,352,768]{2,1,0:T(8,128)(2,1)} custom-call(bf16[4,784,768]{2,1,0:T(8,128)(2,1)} %get-tuple-element.83.x_ref, bf16[4,256,768]{2,1,0:T(8,128)(2,1)} %get-tuple-element.77.dq_ref, bf16[4,784,768]{2,1,0:T(8,128)(2,1)} %get-tuple-element.78.dk_ref, bf16[4,784,768]{2,1,0:T(8,128)(2,1)} %get-tuple-element.79.dv_ref, ...), custom_call_target="tpu_custom_call" | custom-call | flops 1048576 | bytes 1048576 | tf_op jit(solution)/shard_map/weight_grads/pallas_call | solution.py:742
  246.8 1.9 collective-permute-done.13
  248.7 2.8 collective-permute-done.14
  251.5 0.9 copy-done.5
  252.5 3.2 dynamic-slice_bitcast_fusion
  255.7 1.3 collective-permute-start.17
  257.0 4.9 %collective-permute-start.15 = (bf16[4,96,768]{2,1,0:T(8,128)(2,1)}, bf16[4,96,768]{2,1,0:T(8,128)(2,1)}, u32[]{:S(2)}, u32[]{:S(2)}) collective-permute-start(bf16[4,96,768]{2,1,0:T(8,128)(2,1)} %get-tuple-element.90), channel_id=1, source_target_pairs={{1,0},{2,1},{3,2},{5,4},{6,5},{7,6},{9,8},{10,9},{11,10},{13,12},{... | collective-permute-start | bytes 1769480 | tf_op jit(solution)/shard_map/ppermute | solution.py:911
  261.9 1.9 collective-permute-start.16
  263.9 1.1 slice-done
  265.6 2.1 collective-permute-start.24
  268.3 1.1 collective-permute-start.21
  269.4 1.8 collective-permute-start.20
  271.3 11.7 %collective-permute-done.15 = bf16[4,96,768]{2,1,0:T(8,128)(2,1)} collective-permute-done((bf16[4,96,768]{2,1,0:T(8,128)(2,1)}, bf16[4,96,768]{2,1,0:T(8,128)(2,1)}, u32[]{:S(2)}, u32[]{:S(2)}) %collective-permute-start.15) | collective-permute-done | bytes 589856 | tf_op jit(solution)/shard_map/ppermute | solution.py:911
  283.0 1.4 collective-permute-start.19
  284.4 3.0 collective-permute-done.16
  287.4 6.4 %collective-permute-done.24 = bf16[216,768]{1,0:T(8,128)(2,1)S(1)} collective-permute-done((bf16[216,768]{1,0:T(8,128)(2,1)S(1)}, bf16[216,768]{1,0:T(8,128)(2,1)S(1)}, u32[]{:S(2)}, u32[]{:S(2)}) %collective-permute-start.24) | collective-permute-done | bytes 331808 | tf_op jit(solution)/shard_map/ppermute | solution.py:870
  293.9 3.1 add_convert_fusion
  297.0 10.2 %collective-permute-done.23 = bf16[216,768]{1,0:T(8,128)(2,1)S(1)} collective-permute-done((bf16[216,768]{1,0:T(8,128)(2,1)S(1)}, bf16[216,768]{1,0:T(8,128)(2,1)S(1)}, u32[]{:S(2)}, u32[]{:S(2)}) %collective-permute-start.23) | collective-permute-done | bytes 331808 | tf_op jit(solution)/shard_map/ppermute | solution.py:870
  307.3 0.6 slice.210
  308.5 4.7 %collective-permute-start.25 = (bf16[88,768]{1,0:T(8,128)(2,1)S(1)}, bf16[88,768]{1,0:T(8,128)(2,1)S(1)}, u32[]{:S(2)}, u32[]{:S(2)}) collective-permute-start(bf16[88,768]{1,0:T(8,128)(2,1)S(1)} %get-tuple-element.114), channel_id=1, source_target_pairs={{0,1},{1,0},{2,3},{3,2},{4,5},{5,4},{6,7},{7,6},{8,9},{9,8},{10,11... | collective-permute-start | bytes 405512 | tf_op jit(solution)/shard_map/ppermute | solution.py:870
  313.3 0.8 fusion.27
  314.0 0.7 copy.57
  314.8 3.2 collective-permute-done.27
  318.0 2.4 collective-permute-done.25
  322.5 0.7 fusion.29
  (136 shorter events, 10.2 us)
Async XLA Ops:
  7.2 42.0 %all-gather.5.cloned.1.call-start = ((), (), s32[]{:S(2)}) async-start(), calls=%async_computation.2 | async-start | bytes 1658880 | tf_op jit(solution)/shard_map/all_gather | solution.py:937
  8.8 12.5 %collective-permute-start.2 = (bf16[88,768]{1,0:T(8,128)(2,1)}, bf16[88,768]{1,0:T(8,128)(2,1)S(1)}, u32[]{:S(2)}, u32[]{:S(2)}) collective-permute-start(bf16[88,768]{1,0:T(8,128)(2,1)} %stack.76), channel_id=1, source_target_pairs={{0,3},{1,2},{2,1},{3,0},{4,7},{5,6},{6,5},{7,4},{8,11},{9,10},{10,... | collective-permute-start | bytes 405512 | tf_op jit(solution)/shard_map/ppermute | solution.py:814
  9.2 12.0 %collective-permute-start.1 = (bf16[88,768]{1,0:T(8,128)(2,1)}, bf16[88,768]{1,0:T(8,128)(2,1)S(1)}, u32[]{:S(2)}, u32[]{:S(2)}) collective-permute-start(bf16[88,768]{1,0:T(8,128)(2,1)} %stack.76), channel_id=1, source_target_pairs={{0,2},{1,3},{2,0},{3,1},{4,6},{5,7},{6,4},{7,5},{8,10},{9,11},{10,... | collective-permute-start | bytes 405512 | tf_op jit(solution)/shard_map/ppermute | solution.py:814
  12.7 8.6 %collective-permute-start = (bf16[88,768]{1,0:T(8,128)(2,1)}, bf16[88,768]{1,0:T(8,128)(2,1)S(1)}, u32[]{:S(2)}, u32[]{:S(2)}) collective-permute-start(bf16[88,768]{1,0:T(8,128)(2,1)} %stack.76), channel_id=1, source_target_pairs={{0,1},{1,0},{2,3},{3,2},{4,5},{5,4},{6,7},{7,6},{8,9},{9,8},{10,11... | collective-permute-start | bytes 405512 | tf_op jit(solution)/shard_map/ppermute | solution.py:814
  14.4 4.4 %copy-start.11 = (bf16[88,768]{1,0:T(8,128)(2,1)S(1)}, bf16[88,768]{1,0:T(8,128)(2,1)}, u32[]{:S(2)}) copy-start(bf16[88,768]{1,0:T(8,128)(2,1)} %stack.76) | copy-start | bytes 405508
  14.5 110.4 %all-gather.7.cloned.1.call-start = ((), (), s32[]{:S(2)}) async-start(), calls=%async_computation.3 | async-start | bytes 11943936 | tf_op jit(solution)/shard_map/all_gather | solution.py:950
  23.2 37.7 %copy-start.4 = (bf16[352,768]{1,0:T(8,128)(2,1)}, bf16[352,768]{1,0:T(8,128)(2,1)S(1)}, u32[]{:S(2)}) copy-start(bf16[352,768]{1,0:T(8,128)(2,1)S(1)} %pad_maximum_fusion.2.refs_1_) | copy-start | bytes 1622020
  23.2 16.2 %collective-permute-start.8 = (bf16[352,768]{1,0:T(8,128)(2,1)S(1)}, bf16[352,768]{1,0:T(8,128)(2,1)S(1)}, u32[]{:S(2)}, u32[]{:S(2)}) collective-permute-start(bf16[352,768]{1,0:T(8,128)(2,1)S(1)} %pad_maximum_fusion.2.refs_1_), channel_id=1, source_target_pairs={{0,24},{8,16},{16,8},{24,0},{1,25},{9,17},{17,9},{25,1},{2,26},{10... | collective-permute-start | bytes 1622024 | tf_op jit(solution)/shard_map/ppermute | solution.py:826
  25.8 23.2 %collective-permute-start.6 = (bf16[352,768]{1,0:T(8,128)(2,1)S(1)}, bf16[352,768]{1,0:T(8,128)(2,1)S(1)}, u32[]{:S(2)}, u32[]{:S(2)}) collective-permute-start(bf16[352,768]{1,0:T(8,128)(2,1)S(1)} %pad_maximum_fusion.2.refs_1_), channel_id=1, source_target_pairs={{0,16},{8,24},{16,0},{24,8},{1,17},{9,25},{17,1},{25,9},{2,18},{10... | collective-permute-start | bytes 1622024 | tf_op jit(solution)/shard_map/ppermute | solution.py:826
  26.3 22.9 %collective-permute-start.4 = (bf16[352,768]{1,0:T(8,128)(2,1)S(1)}, bf16[352,768]{1,0:T(8,128)(2,1)}, u32[]{:S(2)}, u32[]{:S(2)}) collective-permute-start(bf16[352,768]{1,0:T(8,128)(2,1)S(1)} %pad_maximum_fusion.2.refs_1_), channel_id=1, source_target_pairs={{0,8},{8,0},{16,24},{24,16},{1,9},{9,1},{17,25},{25,17},{2,10},{10... | collective-permute-start | bytes 1622024 | tf_op jit(solution)/shard_map/ppermute | solution.py:826
  39.5 21.6 %copy-start.7 = (bf16[352,768]{1,0:T(8,128)(2,1)}, bf16[352,768]{1,0:T(8,128)(2,1)S(1)}, u32[]{:S(2)}) copy-start(bf16[352,768]{1,0:T(8,128)(2,1)S(1)} %collective-permute-done.8.refs_7_) | copy-start | bytes 1622020
  48.9 12.6 %copy-start.8 = (bf16[352,768]{1,0:T(8,128)(2,1)}, bf16[352,768]{1,0:T(8,128)(2,1)S(1)}, u32[]{:S(2)}) copy-start(bf16[352,768]{1,0:T(8,128)(2,1)S(1)} %collective-permute-done.6.refs_5_) | copy-start | bytes 1622020
  51.5 1.9 copy-start.1
  52.7 211.2 %reduce-scatter.2.cloned.1.call-start = ((), (), s32[]{:S(2)}) async-start(), calls=%async_computation.1 | async-start | bytes 11943936 | tf_op jit(solution)/shard_map/reduce_scatter | solution.py:971
  53.4 39.4 %collective-permute-start.11 = (bf16[4,256,768]{2,1,0:T(8,128)(2,1)S(1)}, bf16[4,256,768]{2,1,0:T(8,128)(2,1)}, u32[]{:S(2)}, u32[]{:S(2)}) collective-permute-start(bf16[4,256,768]{2,1,0:T(8,128)(2,1)S(1)} %copy-done.1), channel_id=1, source_target_pairs={{1,0},{2,1},{3,2},{5,4},{6,5},{7,6},{9,8},{10,9},{11,10},{13,12},{... | collective-permute-start | bytes 4718600 | tf_op jit(solution)/shard_map/ppermute | solution.py:911
  56.7 38.8 %collective-permute-start.10 = (bf16[4,256,768]{2,1,0:T(8,128)(2,1)S(1)}, bf16[4,256,768]{2,1,0:T(8,128)(2,1)}, u32[]{:S(2)}, u32[]{:S(2)}) collective-permute-start(bf16[4,256,768]{2,1,0:T(8,128)(2,1)S(1)} %copy-done.1), channel_id=1, source_target_pairs={{0,1},{1,2},{2,3},{4,5},{5,6},{6,7},{8,9},{9,10},{10,11},{12,13},{... | collective-permute-start | bytes 4718600 | tf_op jit(solution)/shard_map/ppermute | solution.py:911
  61.0 2.0 collective-permute-start.3
  61.1 3.5 %collective-permute-start.9 = (bf16[352,768]{1,0:T(8,128)(2,1)S(1)}, bf16[352,768]{1,0:T(8,128)(2,1)}, u32[]{:S(2)}, u32[]{:S(2)}) collective-permute-start(bf16[352,768]{1,0:T(8,128)(2,1)S(1)} %collective-permute-done.8.refs_7_), channel_id=1, source_target_pairs={{0,4},{4,0},{1,5},{5,1},{2,6},{6,2},{3,7},{7,3},{8,12},{12,8},{9,1... | collective-permute-start | bytes 1622024 | tf_op jit(solution)/shard_map/ppermute | solution.py:848
  61.6 7.7 %collective-permute-start.7 = (bf16[352,768]{1,0:T(8,128)(2,1)S(1)}, bf16[352,768]{1,0:T(8,128)(2,1)}, u32[]{:S(2)}, u32[]{:S(2)}) collective-permute-start(bf16[352,768]{1,0:T(8,128)(2,1)S(1)} %collective-permute-done.6.refs_5_), channel_id=1, source_target_pairs={{0,4},{4,0},{1,5},{5,1},{2,6},{6,2},{3,7},{7,3},{8,12},{12,8},{9,1... | collective-permute-start | bytes 1622024 | tf_op jit(solution)/shard_map/ppermute | solution.py:848
  63.0 0.8 copy-start.9
  63.8 5.5 %collective-permute-start.5 = (bf16[352,768]{1,0:T(8,128)(2,1)}, bf16[352,768]{1,0:T(8,128)(2,1)S(1)}, u32[]{:S(2)}, u32[]{:S(2)}) collective-permute-start(bf16[352,768]{1,0:T(8,128)(2,1)} %collective-permute-done.4.refs_3_), channel_id=1, source_target_pairs={{0,4},{4,0},{1,5},{5,1},{2,6},{6,2},{3,7},{7,3},{8,12},{12,8},{9,1... | collective-permute-start | bytes 1622024 | tf_op jit(solution)/shard_map/ppermute | solution.py:848
  64.5 26.3 %collective-permute-start.12 = (bf16[4,1,768]{2,1,0:T(2,128)(2,1)S(1)}, bf16[4,1,768]{2,1,0:T(2,128)(2,1)S(1)}, u32[]{:S(2)}, u32[]{:S(2)}) collective-permute-start(bf16[4,1,768]{2,1,0:T(2,128)(2,1)S(1)} %slice.161), channel_id=1, source_target_pairs={{2,0},{3,1},{6,4},{7,5},{10,8},{11,9},{14,12},{15,13},{18,16},{19,... | collective-permute-start | bytes 18440 | tf_op jit(solution)/shard_map/ppermute | solution.py:911
  69.3 0.8 copy-start.10
  90.9 4.7 %copy-start.13 = (bf16[4,1,768]{2,1,0:T(2,128)(2,1)}, bf16[4,1,768]{2,1,0:T(2,128)(2,1)S(1)}, u32[]{:S(2)}) copy-start(bf16[4,1,768]{2,1,0:T(2,128)(2,1)S(1)} %collective-permute-done.12.far_ref) | copy-start | bytes 18436
  208.9 20.6 %copy-start.12 = (f32[4,16,768]{2,1,0:T(8,128)S(1)}, f32[4,16,768]{2,1,0:T(8,128)}, u32[]{:S(2)}) copy-start(f32[4,16,768]{2,1,0:T(8,128)} %get-tuple-element.84) | copy-start | bytes 589828
  208.9 20.6 %copy-start.14 = (f32[4,1,768]{2,1,0:T(1,128)S(1)}, f32[4,1,768]{2,1,0:T(1,128)}, u32[]{:S(2)}) copy-start(f32[4,1,768]{2,1,0:T(1,128)} %get-tuple-element.86) | copy-start | bytes 36868
  208.9 20.7 %copy-start.15 = (f32[8,768]{1,0:T(8,128)S(1)}, f32[8,768]{1,0:T(8,128)}, u32[]{:S(2)}) copy-start(f32[8,768]{1,0:T(8,128)} %get-tuple-element.85) | copy-start | bytes 73732
  223.5 25.2 %collective-permute-start.13 = (bf16[4,160,768]{2,1,0:T(8,128)(2,1)}, bf16[4,160,768]{2,1,0:T(8,128)(2,1)S(1)}, u32[]{:S(2)}, u32[]{:S(2)}) collective-permute-start(bf16[4,160,768]{2,1,0:T(8,128)(2,1)} %get-tuple-element.87), channel_id=1, source_target_pairs={{1,0},{2,1},{3,2},{5,4},{6,5},{7,6},{9,8},{10,9},{11,10},{13,12},{... | collective-permute-start | bytes 2949128 | tf_op jit(solution)/shard_map/ppermute | solution.py:911
  227.1 24.4 %collective-permute-start.14 = (bf16[4,160,768]{2,1,0:T(8,128)(2,1)}, bf16[4,160,768]{2,1,0:T(8,128)(2,1)S(1)}, u32[]{:S(2)}, u32[]{:S(2)}) collective-permute-start(bf16[4,160,768]{2,1,0:T(8,128)(2,1)} %get-tuple-element.88), channel_id=1, source_target_pairs={{0,1},{1,2},{2,3},{4,5},{5,6},{6,7},{8,9},{9,10},{10,11},{12,13},{... | collective-permute-start | bytes 2949128 | tf_op jit(solution)/shard_map/ppermute | solution.py:911
  251.5 0.9 copy-start.5
  252.5 3.2 copy-start.16
  255.7 8.1 %collective-permute-start.18 = (bf16[4,352,768]{2,1,0:T(8,128)(2,1)}, bf16[4,352,768]{2,1,0:T(8,128)(2,1)S(1)}, u32[]{:S(2)}, u32[]{:S(2)}) collective-permute-start(bf16[4,352,768]{2,1,0:T(8,128)(2,1)} %dynamic-slice_bitcast_fusion), channel_id=1, source_target_pairs={{0,4},{4,0},{1,5},{5,1},{2,6},{6,2},{3,7},{7,3},{8,12},{12,8},{9,1... | collective-permute-start | bytes 6488072 | tf_op jit(solution)/shard_map/ppermute | solution.py:870
  255.7 13.7 %collective-permute-start.17 = (bf16[4,1,768]{2,1,0:T(2,128)(2,1)S(1)}, bf16[4,1,768]{2,1,0:T(2,128)(2,1)S(1)}, u32[]{:S(2)}, u32[]{:S(2)}) collective-permute-start(bf16[4,1,768]{2,1,0:T(2,128)(2,1)S(1)} %copy-done.16), channel_id=1, source_target_pairs={{0,2},{1,3},{4,6},{5,7},{8,10},{9,11},{12,14},{13,15},{16,18},{17,... | collective-permute-start | bytes 18440 | tf_op jit(solution)/shard_map/ppermute | solution.py:911
  257.0 26.0 %collective-permute-start.15 = (bf16[4,96,768]{2,1,0:T(8,128)(2,1)}, bf16[4,96,768]{2,1,0:T(8,128)(2,1)}, u32[]{:S(2)}, u32[]{:S(2)}) collective-permute-start(bf16[4,96,768]{2,1,0:T(8,128)(2,1)} %get-tuple-element.90), channel_id=1, source_target_pairs={{1,0},{2,1},{3,2},{5,4},{6,5},{7,6},{9,8},{10,9},{11,10},{13,12},{... | collective-permute-start | bytes 1769480 | tf_op jit(solution)/shard_map/ppermute | solution.py:911
  261.9 25.5 %collective-permute-start.16 = (bf16[4,96,768]{2,1,0:T(8,128)(2,1)}, bf16[4,96,768]{2,1,0:T(8,128)(2,1)}, u32[]{:S(2)}, u32[]{:S(2)}) collective-permute-start(bf16[4,96,768]{2,1,0:T(8,128)(2,1)} %get-tuple-element.92), channel_id=1, source_target_pairs={{0,1},{1,2},{2,3},{4,5},{5,6},{6,7},{8,9},{9,10},{10,11},{12,13},{... | collective-permute-start | bytes 1769480 | tf_op jit(solution)/shard_map/ppermute | solution.py:911
  263.9 1.1 slice-start
  263.9 1.5 copy-start.3
  265.0 2.6 copy-start
  265.6 28.3 %collective-permute-start.24 = (bf16[216,768]{1,0:T(8,128)(2,1)S(1)}, bf16[216,768]{1,0:T(8,128)(2,1)S(1)}, u32[]{:S(2)}, u32[]{:S(2)}) collective-permute-start(bf16[216,768]{1,0:T(8,128)(2,1)S(1)} %get-tuple-element.108), channel_id=1, source_target_pairs={{0,3},{1,2},{2,1},{3,0},{4,7},{5,6},{6,5},{7,4},{8,11},{9,10},{10,... | collective-permute-start | bytes 995336 | tf_op jit(solution)/shard_map/ppermute | solution.py:870
  267.6 26.2 %copy-start.6 = (bf16[4,160,768]{2,1,0:T(8,128)(2,1)S(1)}, bf16[4,160,768]{2,1,0:T(8,128)(2,1)}, u32[]{:S(2)}) copy-start(bf16[4,160,768]{2,1,0:T(8,128)(2,1)} %copy-done.5) | copy-start | bytes 2949124
  268.2 25.7 %copy-start.2 = (f32[4,256,768]{2,1,0:T(8,128)S(1)}, f32[4,256,768]{2,1,0:T(8,128)}, u32[]{:S(2)}) copy-start(f32[4,256,768]{2,1,0:T(8,128)} %get-tuple-element.81) | copy-start | bytes 9437188
  268.3 39.7 %collective-permute-start.21 = (bf16[352,768]{1,0:T(8,128)(2,1)S(1)}, bf16[352,768]{1,0:T(8,128)(2,1)S(1)}, u32[]{:S(2)}, u32[]{:S(2)}) collective-permute-start(bf16[352,768]{1,0:T(8,128)(2,1)S(1)} %get-tuple-element.105), channel_id=1, source_target_pairs={{0,24},{8,16},{16,8},{24,0},{1,25},{9,17},{17,9},{25,1},{2,26},{10... | collective-permute-start | bytes 1622024 | tf_op jit(solution)/shard_map/ppermute | solution.py:870
  269.4 38.5 %collective-permute-start.20 = (bf16[352,768]{1,0:T(8,128)(2,1)S(1)}, bf16[352,768]{1,0:T(8,128)(2,1)S(1)}, u32[]{:S(2)}, u32[]{:S(2)}) collective-permute-start(bf16[352,768]{1,0:T(8,128)(2,1)S(1)} %get-tuple-element.106), channel_id=1, source_target_pairs={{0,16},{8,24},{16,0},{24,8},{1,17},{9,25},{17,1},{25,9},{2,18},{10... | collective-permute-start | bytes 1622024 | tf_op jit(solution)/shard_map/ppermute | solution.py:870
  283.0 25.0 %collective-permute-start.19 = (bf16[352,768]{1,0:T(8,128)(2,1)S(1)}, bf16[352,768]{1,0:T(8,128)(2,1)S(1)}, u32[]{:S(2)}, u32[]{:S(2)}) collective-permute-start(bf16[352,768]{1,0:T(8,128)(2,1)S(1)} %get-tuple-element.107), channel_id=1, source_target_pairs={{0,8},{8,0},{16,24},{24,16},{1,9},{9,1},{17,25},{25,17},{2,10},{10... | collective-permute-start | bytes 1622024 | tf_op jit(solution)/shard_map/ppermute | solution.py:870
  287.4 9.5 %collective-permute-start.22 = (bf16[216,768]{1,0:T(8,128)(2,1)S(1)}, bf16[216,768]{1,0:T(8,128)(2,1)S(1)}, u32[]{:S(2)}, u32[]{:S(2)}) collective-permute-start(bf16[216,768]{1,0:T(8,128)(2,1)S(1)} %get-tuple-element.109), channel_id=1, source_target_pairs={{0,1},{1,0},{2,3},{3,2},{4,5},{5,4},{6,7},{7,6},{8,9},{9,8},{10,11... | collective-permute-start | bytes 995336 | tf_op jit(solution)/shard_map/ppermute | solution.py:870
  293.9 13.3 %collective-permute-start.23 = (bf16[216,768]{1,0:T(8,128)(2,1)S(1)}, bf16[216,768]{1,0:T(8,128)(2,1)S(1)}, u32[]{:S(2)}, u32[]{:S(2)}) collective-permute-start(bf16[216,768]{1,0:T(8,128)(2,1)S(1)} %get-tuple-element.110), channel_id=1, source_target_pairs={{0,2},{1,3},{2,0},{3,1},{4,6},{5,7},{6,4},{7,5},{8,10},{9,11},{10,... | collective-permute-start | bytes 995336 | tf_op jit(solution)/shard_map/ppermute | solution.py:870
  308.4 9.6 %collective-permute-start.27 = (bf16[88,768]{1,0:T(8,128)(2,1)S(1)}, bf16[88,768]{1,0:T(8,128)(2,1)S(1)}, u32[]{:S(2)}, u32[]{:S(2)}) collective-permute-start(bf16[88,768]{1,0:T(8,128)(2,1)S(1)} %get-tuple-element.113), channel_id=1, source_target_pairs={{0,3},{1,2},{2,1},{3,0},{4,7},{5,6},{6,5},{7,4},{8,11},{9,10},{10,... | collective-permute-start | bytes 405512 | tf_op jit(solution)/shard_map/ppermute | solution.py:870
  308.5 11.9 %collective-permute-start.25 = (bf16[88,768]{1,0:T(8,128)(2,1)S(1)}, bf16[88,768]{1,0:T(8,128)(2,1)S(1)}, u32[]{:S(2)}, u32[]{:S(2)}) collective-permute-start(bf16[88,768]{1,0:T(8,128)(2,1)S(1)} %get-tuple-element.114), channel_id=1, source_target_pairs={{0,1},{1,0},{2,3},{3,2},{4,5},{5,4},{6,7},{7,6},{8,9},{9,8},{10,11... | collective-permute-start | bytes 405512 | tf_op jit(solution)/shard_map/ppermute | solution.py:870
  313.3 7.5 %collective-permute-start.26 = (bf16[88,768]{1,0:T(8,128)(2,1)S(1)}, bf16[88,768]{1,0:T(8,128)(2,1)S(1)}, u32[]{:S(2)}, u32[]{:S(2)}) collective-permute-start(bf16[88,768]{1,0:T(8,128)(2,1)S(1)} %get-tuple-element.115), channel_id=1, source_target_pairs={{0,2},{1,3},{2,0},{3,1},{4,6},{5,7},{6,4},{7,5},{8,10},{9,11},{10,... | collective-permute-start | bytes 405512 | tf_op jit(solution)/shard_map/ppermute | solution.py:870
Sparse Core Ops, SparseCore 0:
  14.6 33.5 all-gather.4
  52.8 65.8 all-gather.6
  180.2 82.7 reduce-scatter.1
where the time goes:
time: 335 us; the launch traced here: 330 us
  Pallas kernels  159 us (47%)
  waiting for transfers between devices  77 us (23%)
  starting transfers between devices  46.1 us (14%)
  local copies, waits for them, and re-layouts  24.1 us (7%)
  between operations  14.5 us (4%)
  other arithmetic  9.55 us (3%)
    pallas_call x1, Pallas kernels, feed_forward(): pl.pallas_call(functools.partial(ffn_kernel, panels), grid=(2 * panels,),...  55.2 us
    ppermute x8, waiting for transfers between devices, shift(): return lax.ppermute(value, 'seq', pairs)  29.5 us
    pallas_call x1, Pallas kernels, attention_backward(): pl.pallas_call(kernel, grid=(count,), in_specs=attention_specs(ext, group...  28.8 us
    ppermute x8, starting transfers between devices, shift(): return lax.ppermute(value, 'seq', pairs)  26.3 us
    ppermute x10, waiting for transfers between devices, exchange_sum(): lax.ppermute(pick(pieces, met(me)[0]), axis, pairs)  22.6 us
    ppermute x3, waiting for transfers between devices, gather_yx(): pieces.append((lax.ppermute(column, 'yx', pairs), met(me)[1]))  22.3 us
    pallas_call x1, Pallas kernels, attention_forward(): pl.pallas_call(attn_fwd_kernel, grid=(seqs,), in_specs=attention_specs(ex...  16.5 us
    pallas_call x1, Pallas kernels, weight_grads(): pl.pallas_call(weight_grad_kernel, grid=(seqs,), in_specs=[by_seq(ext, wi...  15.5 us
  transfers between devices with their start and end apart: 31, of which 17 were waited for; matrix products, arithmetic and copies ran while one was open for 7% of the time, Pallas kernels for 31%

commit v1 on v0

--- a/solution.py
+++ b/solution.py
@@ -567,7 +567,6 @@
     )(outer, inner, out)
 
 
-SOON = 160
 SMALL = 16
 
 
@@ -614,22 +613,25 @@
 
 
 def project_halos_kernel(
-    x_ref, own_k_ref, own_v_ref, left_ref, right_ref, far_ref, w_ref, k_ref, v_ref, ext_ref
+    own_k_ref, own_v_ref, left_ref, right_ref, far_ref, w_ref, k_ref, v_ref, halos
 ):
-    group, width = x_ref.shape[1:]
+    group, width = own_k_ref.shape[1:]
     right = HALO + group
-    ext_ref[0, :HALO, :] = left_ref[0]
-    ext_ref[0, HALO:right, :] = x_ref[0]
-    ext_ref[0, right : right + HALO, :] = right_ref[0]
-    row = lax.broadcasted_iota(jnp.int32, (PAD, width), 0)
-    far = jnp.where(row == 0, jnp.broadcast_to(far_ref[0].astype(F32), (PAD, width)), 0.0)
-    ext_ref[0, right + HALO :, :] = far.astype(BF16)
-    halos = jnp.concatenate((ext_ref[0, :HALO, :], ext_ref[0, right:, :]), axis=0)
+    halos[:HALO, :] = left_ref[0]
+    halos[HALO : 2 * HALO, :] = right_ref[0]
+    halos[2 * HALO :, :] = padded(far_ref)
     for place, own_ref, ref in ((1, own_k_ref, k_ref), (2, own_v_ref, v_ref)):
-        rows = nn(halos, square_of(w_ref, place)).astype(BF16)
+        rows = nn(halos[...], square_of(w_ref, place)).astype(BF16)
         ref[0, :HALO, :] = rows[:HALO]
         ref[0, HALO:right, :] = own_ref[0]
         ref[0, right:, :] = rows[HALO:]
+
+
+def padded(far_ref):
+    width = far_ref.shape[2]
+    row = lax.broadcasted_iota(jnp.int32, (PAD, width), 0)
+    far = jnp.broadcast_to(far_ref[0].astype(F32), (PAD, width))
+    return jnp.where(row == 0, far, 0.0).astype(BF16)
 
 
 def resident(*shape):
@@ -652,29 +654,30 @@
     )(x, weights)
 
 
-def project_halos(x, own_keys, own_values, left, right, far, weights):
-    seqs, group, width = x.shape
+def project_halos(own_keys, own_values, left, right, far, weights):
+    seqs, group, width = own_keys.shape
     ext = group + 2 * HALO + PAD
     return pl.pallas_call(
         project_halos_kernel,
         grid=(seqs,),
-        in_specs=[by_seq(group, width)] * 3
+        in_specs=[by_seq(group, width)] * 2
         + [by_seq(HALO, width), by_seq(HALO, width), by_seq(1, width), resident(*weights.shape)],
-        out_specs=[by_seq(ext, width)] * 3,
-        out_shape=[jax.ShapeDtypeStruct((seqs, ext, width), BF16)] * 3,
+        out_specs=[by_seq(ext, width)] * 2,
+        out_shape=[jax.ShapeDtypeStruct((seqs, ext, width), BF16)] * 2,
+        scratch_shapes=[pltpu.VMEM((2 * HALO + PAD, width), BF16)],
         compiler_params=pltpu.CompilerParams(vmem_limit_bytes=60 << 20),
         cost_estimate=QUICK,
         name="project_halos",
-    )(x, own_keys, own_values, left, right, far, weights)
+    )(own_keys, own_values, left, right, far, weights)
 
 
 def input_grad_kernel(
-    dq_ref, dk_ref, dv_ref, first_ref, w_ref, a_ref, b_ref, c_ref, d_ref, far_ref, own_ref
+    dq_ref, dk_ref, dv_ref, first_ref, w_ref, left_ref, right_ref, far_ref, own_ref
 ):
     right = HALO + dq_ref.shape[1]
     grad = nt(dk_ref[0], square_of(w_ref, 1)) + nt(dv_ref[0], square_of(w_ref, 2))
-    for ref, at in ((a_ref, 0), (b_ref, right), (c_ref, SOON), (d_ref, right + SOON)):
-        ref[0] = grad[at : at + ref.shape[1]].astype(BF16)
+    left_ref[0] = grad[:HALO].astype(BF16)
+    right_ref[0] = grad[right : right + HALO].astype(BF16)
     far_ref[0] = grad[right + HALO : right + HALO + 1].astype(BF16)
     own_ref[0] = grad[HALO:right] + nt(dq_ref[0], square_of(w_ref, 0)) + first_ref[0]
 
@@ -682,7 +685,7 @@
 def input_grads(d_queries, d_keys, d_values, d_first, weights):
     seqs, group, width = d_queries.shape
     ext = d_keys.shape[1]
-    rows = (SOON, SOON, HALO - SOON, HALO - SOON)
+    rows = (HALO, HALO)
     return pl.pallas_call(
         input_grad_kernel,
         grid=(seqs,),
@@ -702,12 +705,34 @@
     )(d_queries, d_keys, d_values, d_first, weights)
 
 
+def split_cores(value, core):
+    both = value.reshape((-1, 2) + value.shape[1:])
+    mine, other = both[:, 0], both[:, 1]
+    return jnp.where(core == 0, mine, other), jnp.where(core == 0, other, mine)
+
+
 def weight_grad_kernel(
-    x_ref, dq_ref, dk_ref, dv_ref, small_ref, out_ref, acc, x_tail, dk_tail, dv_tail
+    core_ref,
+    x_ref,
+    left_ref,
+    right_ref,
+    far_ref,
+    dq_ref,
+    dk_ref,
+    dv_ref,
+    small_ref,
+    mine_ref,
+    other_ref,
+    acc,
+    rows,
+    x_tail,
+    dk_tail,
+    dv_tail,
 ):
     seq = pl.program_id(0)
+    core = core_ref[0]
     group, width = dq_ref.shape[1:]
-    units = out_ref.shape[0]
+    units = 2 * mine_ref.shape[0]
     part = width // units
     main = 2 * HALO + group
 
@@ -715,47 +740,64 @@
     def _():
         acc[...] = jnp.zeros_like(acc)
 
-    rows = pl.ds(pl.multiple_of(seq * PAD, PAD), PAD)
-    for tail, ref in ((x_tail, x_ref), (dk_tail, dk_ref), (dv_tail, dv_ref)):
-        tail[rows, :] = ref[0, main:, :]
-    acc[0] += tn(x_ref[0, HALO : HALO + group, :], dq_ref[0])
-    acc[1] += tn(x_ref[0, :main, :], dk_ref[0, :main, :])
-    acc[2] += tn(x_ref[0, :main, :], dv_ref[0, :main, :])
+    rows[:HALO, :] = left_ref[0]
+    rows[HALO : HALO + group, :] = x_ref[0]
+    rows[HALO + group :, :] = right_ref[0]
+    tail = pl.ds(pl.multiple_of(seq * PAD, PAD), PAD)
+    x_tail[tail, :] = padded(far_ref)
+    dk_tail[tail, :] = dk_ref[0, main:, :]
+    dv_tail[tail, :] = dv_ref[0, main:, :]
+    acc[0] += tn(x_ref[0], dq_ref[0])
+    acc[1] += tn(rows[...], dk_ref[0, :main, :])
+    acc[2] += tn(rows[...], dv_ref[0, :main, :])
 
     @pl.when(seq == pl.num_programs(0) - 1)
     def _():
         ends = (None, tn(x_tail[...], dk_tail[...]), tn(x_tail[...], dv_tail[...]))
         for place, end in enumerate(ends):
             total = acc[place] if end is None else acc[place] + end
-            out_ref[:, place * part : (place + 1) * part, :] = total.astype(BF16).reshape(
-                units, part, width
-            )
-        out_ref[:, 3 * part :, :] = small_ref[...]
-
-
-def weight_grads(x_ext, d_queries, d_keys, d_values, small):
+            mine, other = split_cores(total.reshape(units, part, width), core)
+            at = slice(place * part, (place + 1) * part)
+            mine_ref[:, at, :] = mine.astype(BF16)
+            other_ref[:, at, :] = other.astype(BF16)
+        mine, other = split_cores(small_ref[...], core)
+        mine_ref[:, 3 * part :, :] = mine.astype(BF16)
+        other_ref[:, 3 * part :, :] = other.astype(BF16)
+
+
+def weight_grads(core, x, left, right, far, d_queries, d_keys, d_values, small):
     seqs, group, width = d_queries.shape
-    ext = x_ext.shape[1]
+    ext = d_keys.shape[1]
     units, small_rows, _ = small.shape
-    shape = (units, 3 * (width // units) + small_rows, width)
+    shape = (units // 2, 3 * (width // units) + small_rows, width)
     tail = pltpu.VMEM((seqs * PAD, width), BF16)
     return pl.pallas_call(
         weight_grad_kernel,
         grid=(seqs,),
         in_specs=[
-            by_seq(ext, width),
+            pl.BlockSpec(memory_space=pltpu.SMEM),
+            by_seq(group, width),
+            by_seq(HALO, width),
+            by_seq(HALO, width),
+            by_seq(1, width),
             by_seq(group, width),
             by_seq(ext, width),
             by_seq(ext, width),
             resident(*small.shape),
         ],
-        out_specs=resident(*shape),
-        out_shape=jax.ShapeDtypeStruct(shape, BF16),
-        scratch_shapes=[pltpu.VMEM((3, width, width), F32), tail, tail, tail],
+        out_specs=[resident(*shape)] * 2,
+        out_shape=[jax.ShapeDtypeStruct(shape, BF16)] * 2,
+        scratch_shapes=[
+            pltpu.VMEM((3, width, width), F32),
+            pltpu.VMEM((2 * HALO + group, width), BF16),
+            tail,
+            tail,
+            tail,
+        ],
         compiler_params=pltpu.CompilerParams(vmem_limit_bytes=60 << 20),
         cost_estimate=QUICK,
         name="weight_grads",
-    )(x_ext, d_queries, d_keys, d_values, small)
+    )(core, x, left, right, far, d_queries, d_keys, d_values, small)
 
 
 def document_of(positions, lengths, seq_len):
@@ -899,6 +941,7 @@
     core_count = lax.axis_size("core")
     units = yx_count * core_count
     parts = units * seq_count
+    core = lax.axis_index("core")
     seq_place = lax.axis_index("seq")
     seqs, group, width = tokens.shape
     ff = inner_weight.shape[1]
@@ -958,7 +1001,7 @@
     flat = tokens.reshape(count, width)
 
     queries, own_keys, own_values = project_own(tokens, early)
-    keys, values, x_ext = project_halos(tokens, own_keys, own_values, *came, early)
+    keys, values = project_halos(own_keys, own_values, *came, early)
     mixed, lse = attention_forward(queries, keys, values, taps, same, bias)
     y, d_first, d_mixed, d_small, d_bias, d_late = feed_forward(
         flat,
@@ -984,11 +1027,10 @@
         seqs,
         (),
     )
-    left_a, right_a, left_b, right_b, far, own = input_grads(
+    left, right, far, own = input_grads(
         d_queries, d_keys, d_values, d_first.reshape(seqs, group, width), early
     )
-    came = (shift(left_a, -1), shift(right_a, 1))
-    later_came = (shift(left_b, -1), shift(right_b, 1), shift(far, 2))
+    back = (shift(left, -1), shift(right, 1), shift(far, 2))
 
     d_taps = jnp.sum(d_taps, axis=0)[:10]
     d_vectors = jnp.concatenate((d_taps, d_small[:5]), axis=0)
@@ -997,10 +1039,18 @@
     d_bias = jnp.pad(d_bias.reshape(parts, 1, -1), ((0, 0), (0, 0), (0, width - ff // parts)))
     d_vectors = jnp.concatenate((d_vectors, d_bias), axis=1).astype(BF16)
     d_vectors = d_vectors.reshape(units, seq_count * SMALL, width)
-    early_sum = weight_grads(after(x_ext, own), d_queries, d_keys, d_values, d_vectors)
-    early_sum = early_sum.reshape(yx_count, core_count, -1, width)
-    early_sum, came = after((early_sum, came))
-    early_sum = exchange_sum(early_sum.swapaxes(0, 1), "core").astype(BF16)
+    mine, other = weight_grads(
+        core.astype(jnp.int32).reshape(1),
+        after(tokens, own),
+        *came,
+        d_queries,
+        d_keys,
+        d_values,
+        d_vectors,
+    )
+    (mine, other), back = after(((mine, other), back))
+    swapped = lax.ppermute(other, "core", [(0, 1), (1, 0)])
+    early_sum = (mine.astype(F32) + swapped.astype(F32)).astype(BF16)
     outer_all = seq_count * outer_rows
     late_sum = jnp.concatenate(
         (
@@ -1013,7 +1063,7 @@
         axis=1,
     )
     late_sum = exchange_sum(late_sum, "seq")
-    early_sum = exchange_sum(early_sum, "yx", late_sum, later_came).astype(BF16)
+    early_sum = exchange_sum(early_sum, "yx", late_sum).astype(BF16)
     whole = 3 * seq_count * share
     early_sum = jnp.concatenate(
         [
@@ -1028,10 +1078,7 @@
     early_sum = exchange_sum(early_sum, "seq")
 
     edge = group - HALO
-    from_right, from_left = (
-        jnp.concatenate(parts, axis=1).astype(F32) for parts in zip(came, later_came)
-    )
-    from_far = later_came[2].astype(F32)
+    from_right, from_left, from_far = (part.astype(F32) for part in back)
     d_input = own + jnp.pad(from_right, ((0, 0), (edge, 0), (0, 0)))
     d_input = d_input + jnp.pad(from_left, ((0, 0), (0, edge), (0, 0)))
     d_input = d_input + jnp.pad(from_far, ((0, 0), (0, group - 1), (0, 0)))

time: 335 us -> 326 us (0.973)
  starting transfers between devices: 46.1 us -> 38.2 us
  waiting for transfers between devices: 77 us -> 83.5 us
  local copies, waits for them, and re-layouts: 24.1 us -> 20.5 us
    ppermute x8 -> x6, starting transfers between devices: 26.3 us -> 19.3 us  [shift(): return lax.ppermute(value, 'seq', pairs)]
    ppermute x10 -> x9, waiting for transfers between devices: 22.6 us -> 28.4 us  [exchange_sum(): lax.ppermute(pick(pieces, met(me)[0]), axis, pairs)]
    ppermute x8 -> x6, waiting for transfers between devices: 29.5 us -> 27.4 us  [shift(): return lax.ppermute(value, 'seq', pairs)]
    ppermute x10 -> x9, starting transfers between devices: 11.4 us -> 10.4 us  [exchange_sum(): lax.ppermute(pick(pieces, met(me)[0]), axis, pairs)]
  transfers between devices with their start and end apart: 31 -> 29, of which waited for: 17 -> 16; matrix products, arithmetic and copies ran while one was open for 7% -> 6% of each run, Pallas kernels for 31% -> 31%
where the time goes in v1:
time: 326 us; the launch traced here: 322 us
  Pallas kernels  158 us (48%)
  waiting for transfers between devices  83.5 us (26%)
  starting transfers between devices  38.2 us (12%)
  local copies, waits for them, and re-layouts  20.5 us (6%)
  between operations  14.4 us (4%)
  other arithmetic  8.15 us (2%)
    pallas_call x1, Pallas kernels, feed_forward(): pl.pallas_call(functools.partial(ffn_kernel, panels), grid=(2 * panels,),...  55.2 us
    pallas_call x1, Pallas kernels, attention_backward(): pl.pallas_call(kernel, grid=(count,), in_specs=attention_specs(ext, group...  28.8 us
    ppermute x9, waiting for transfers between devices, exchange_sum(): lax.ppermute(pick(pieces, met(me)[0]), axis, pairs)  28.4 us
    ppermute x6, waiting for transfers between devices, shift(): return lax.ppermute(value, 'seq', pairs)  27.4 us
    ppermute x3, waiting for transfers between devices, gather_yx(): pieces.append((lax.ppermute(column, 'yx', pairs), met(me)[1]))  22.1 us
    ppermute x6, starting transfers between devices, shift(): return lax.ppermute(value, 'seq', pairs)  19.3 us
    pallas_call x1, Pallas kernels, attention_forward(): pl.pallas_call(attn_fwd_kernel, grid=(seqs,), in_specs=attention_specs(ex...  16.5 us
    pallas_call x1, Pallas kernels, weight_grads(): pl.pallas_call(weight_grad_kernel, grid=(seqs,), in_specs=[pl.BlockSpec(m...  16.2 us
  transfers between devices with their start and end apart: 29, of which 16 were waited for; matrix products, arithmetic and copies ran while one was open for 6% of the time, Pallas kernels for 31%

profile of v1, /device:TPU:16, one launch (start us, length us, event | category | flops | bytes accessed | tf_op | source)
XLA Modules:
  0.0 322.4 jit_solution(14057468850343538984)
XLA Ops:
  7.2 1.5 stack.76
  9.2 3.5 %collective-permute-start.1 = (bf16[88,768]{1,0:T(8,128)(2,1)}, bf16[88,768]{1,0:T(8,128)(2,1)S(1)}, u32[]{:S(2)}, u32[]{:S(2)}) collective-permute-start(bf16[88,768]{1,0:T(8,128)(2,1)} %stack.76), channel_id=1, source_target_pairs={{0,2},{1,3},{2,0},{3,1},{4,6},{5,7},{6,4},{7,5},{8,10},{9,11},{10,... | collective-permute-start | bytes 405512 | tf_op jit(solution)/shard_map/ppermute | solution.py:856
  12.7 1.7 pack.1
  14.6 0.8 select_reduce_fusion
  17.2 0.9 abs_compare_fusion.1
  18.8 1.3 pad_maximum_fusion.bias_ref.refs_5_
  20.2 1.1 collective-permute-done.2
  21.3 1.8 broadcast_in_dim.87.same_ref.refs_4_
  23.3 2.5 collective-permute-start.8
  25.8 0.5 collective-permute-start.6
  26.3 0.5 collective-permute-start.4
  26.8 12.7 %collective-permute-done.8.refs_7_ = bf16[352,768]{1,0:T(8,128)(2,1)S(1)} collective-permute-done((bf16[352,768]{1,0:T(8,128)(2,1)S(1)}, bf16[352,768]{1,0:T(8,128)(2,1)S(1)}, u32[]{:S(2)}, u32[]{:S(2)}) %collective-permute-start.8) | collective-permute-done | bytes 540704 | tf_op jit(solution)/shard_map/ppermute | solution.py:868
  39.5 9.5 %collective-permute-done.6.refs_5_ = bf16[352,768]{1,0:T(8,128)(2,1)S(1)} collective-permute-done((bf16[352,768]{1,0:T(8,128)(2,1)S(1)}, bf16[352,768]{1,0:T(8,128)(2,1)S(1)}, u32[]{:S(2)}, u32[]{:S(2)}) %collective-permute-start.6) | collective-permute-done | bytes 540704 | tf_op jit(solution)/shard_map/ppermute | solution.py:868
  49.0 0.8 copy-done.11
  49.8 1.1 slice.166
  50.9 1.2 slice.167
  52.1 1.2 pad_maximum_fusion.1
  53.4 0.6 copy-done
  54.0 3.3 %collective-permute-start.11 = (bf16[4,256,768]{2,1,0:T(8,128)(2,1)S(1)}, bf16[4,256,768]{2,1,0:T(8,128)(2,1)S(1)}, u32[]{:S(2)}, u32[]{:S(2)}) collective-permute-start(bf16[4,256,768]{2,1,0:T(8,128)(2,1)S(1)} %copy-done), channel_id=1, source_target_pairs={{1,0},{2,1},{3,2},{5,4},{6,5},{7,6},{9,8},{10,9},{11,10},{13,12},{... | collective-permute-start | bytes 4718600 | tf_op jit(solution)/shard_map/ppermute | solution.py:954
  57.3 3.2 collective-permute-start.10
  61.2 1.7 collective-permute-done.3.refs_2_
  63.0 0.6 stack.67.refs_0_
  63.6 5.6 %collective-permute-start.12 = (bf16[4,1,768]{2,1,0:T(2,128)(2,1)S(1)}, bf16[4,1,768]{2,1,0:T(2,128)(2,1)S(1)}, u32[]{:S(2)}, u32[]{:S(2)}) collective-permute-start(bf16[4,1,768]{2,1,0:T(2,128)(2,1)S(1)} %slice.161), channel_id=1, source_target_pairs={{2,0},{3,1},{6,4},{7,5},{10,8},{11,9},{14,12},{15,13},{18,16},{19,... | collective-permute-start | bytes 18440 | tf_op jit(solution)/shard_map/ppermute | solution.py:954
  69.3 4.3 %assemble.1.w_ref = bf16[8,352,768]{2,1,0:T(8,128)(2,1)} custom-call(s32[8]{0:T(128)} %stack.67.refs_0_, bf16[352,768]{1,0:T(8,128)(2,1)} %copy-done.5, bf16[352,768]{1,0:T(8,128)(2,1)} %collective-permute-done.3.refs_2_, bf16[352,768]{1,0:T(8,128)(2,1)} %collective-permute-done.4.refs_3_, bf16[352,768]{1,0:T(8,128)(2,1)} %collective-permute-done.5.refs_4_, ...), custom_call_target="tpu_custom_call" | custom-call | flops 1048576 | bytes 1048576 | tf_op jit(solution)/shard_map/assemble/pallas_call | solution.py:892
  73.6 1.2 slice.196
  75.0 0.7 reshape.315.bias_ref
  75.9 0.6 pad.25.w_ref.refs_3_
  76.5 0.6 pad.26.small_ref
  77.1 7.6 %project_own.1 = (bf16[4,256,768]{2,1,0:T(8,128)(2,1)}, bf16[4,256,768]{2,1,0:T(8,128)(2,1)}, bf16[4,256,768]{2,1,0:T(8,128)(2,1)}) custom-call(bf16[4,256,768]{2,1,0:T(8,128)(2,1)} %x_ref.2, bf16[8,352,768]{2,1,0:T(8,128)(2,1)} %assemble.1.w_ref), custom_call_target="tpu_custom_call" | custom-call | flops 1048576 | bytes 1048576 | tf_op jit(solution)/shard_map/project_own/pallas_call | solution.py:645
  84.7 6.8 %collective-permute-done.12.far_ref = bf16[4,1,768]{2,1,0:T(2,128)(2,1)S(1)} collective-permute-done((bf16[4,1,768]{2,1,0:T(2,128)(2,1)S(1)}, bf16[4,1,768]{2,1,0:T(2,128)(2,1)S(1)}, u32[]{:S(2)}, u32[]{:S(2)}) %collective-permute-start.12) | collective-permute-done | bytes 6176 | tf_op jit(solution)/shard_map/ppermute | solution.py:954
  91.5 1.8 collective-permute-done.11.right_ref
  93.3 2.9 collective-permute-done.10.left_ref
  96.2 11.2 %project_halos.1 = (bf16[4,784,768]{2,1,0:T(8,128)(2,1)}, bf16[4,784,768]{2,1,0:T(8,128)(2,1)}) custom-call(bf16[4,256,768]{2,1,0:T(8,128)(2,1)} %get-tuple-element.66.own_k_ref, bf16[4,256,768]{2,1,0:T(8,128)(2,1)} %get-tuple-element.67.own_v_ref, bf16[4,256,768]{2,1,0:T(8,128)(2,1)} %collective-permute-done.10.left_ref, bf16[4,256,768]{2,1,0:T(8,128)(2,1)} %copy-done.1, ...), custom_call_target="tpu_custom_call" | custom-call | flops 1048576 | bytes 1048576 | tf_op jit(solution)/shard_map/project_halos/pallas_call | solution.py:660
  107.4 16.5 %attn_fwd.1 = (bf16[4,256,768]{2,1,0:T(8,128)(2,1)}, f32[4,6,2,256]{3,2,1,0:T(2,128)}) custom-call(bf16[4,256,768]{2,1,0:T(8,128)(2,1)} %get-tuple-element.65.q_ref.refs_0_, bf16[4,784,768]{2,1,0:T(8,128)(2,1)} %get-tuple-element.69.k_ref.refs_1_, bf16[4,784,768]{2,1,0:T(8,128)(2,1)} %get-tuple-element.70.v_ref.refs_2_, f32[16,768]{1,0:T(8,128)} %pad.25.w_ref.refs_3_, ...), custom_call_target="tpu_custom_call" | custom-call | flops 1048576 | bytes 1048576 | tf_op jit(solution)/shard_map/attn_fwd/pallas_call | solution.py:240
  124.0 55.2 %ffn.1 = (bf16[1024,768]{1,0:T(8,128)(2,1)}, f32[1024,768]{1,0:T(8,128)}, bf16[1024,768]{1,0:T(8,128)(2,1)}, f32[8,768]{1,0:T(8,128)}, f32[4,1,768]{2,1,0:T(1,128)}, /*index=5*/bf16[8,9,96,768]{3,2,1,0:T(8,128)(2,1)}) custom-call(bf16[1024,768]{1,0:T(8,128)(2,1)} %bitcast.120, bf16[1024,768]{1,0:T(8,128)(2,1)} %bitcast.136, bf16[1024,768]{1,0:T(8,128)(2,1)} %bitcast.135, ...), custom_call_target="tpu_custom_call" | custom-call | flops 1048576 | bytes 1048576 | tf_op jit(solution)/shard_map/ffn/pallas_call | solution.py:492
  179.2 28.8 %attn_bwd.1 = (bf16[4,256,768]{2,1,0:T(8,128)(2,1)}, bf16[4,784,768]{2,1,0:T(8,128)(2,1)}, bf16[4,784,768]{2,1,0:T(8,128)(2,1)}, f32[4,16,768]{2,1,0:T(8,128)}) custom-call(bf16[4,256,768]{2,1,0:T(8,128)(2,1)} %get-tuple-element.65.q_ref.refs_0_, bf16[4,784,768]{2,1,0:T(8,128)(2,1)} %get-tuple-element.69.k_ref.refs_1_, ...), custom_call_target="tpu_custom_call" | custom-call | flops 1048576 | bytes 1048576 | tf_op jit(solution)/shard_map/attn_bwd/pallas_call | solution.py:270
  208.0 14.6 %input_grads.1 = (bf16[4,256,768]{2,1,0:T(8,128)(2,1)}, bf16[4,256,768]{2,1,0:T(8,128)(2,1)}, bf16[4,1,768]{2,1,0:T(2,128)(2,1)}, f32[4,256,768]{2,1,0:T(8,128)}) custom-call(bf16[4,256,768]{2,1,0:T(8,128)(2,1)} %get-tuple-element.78.dq_ref, bf16[4,784,768]{2,1,0:T(8,128)(2,1)} %get-tuple-element.79.dk_ref, bf16[4,784,768]{2,1,0:T(8,128)(2,1)} %get-tuple-element.80.dv_ref, ...), custom_call_target="tpu_custom_call" | custom-call | flops 1048576 | bytes 1048576 | tf_op jit(solution)/shard_map/input_grads/pallas_call | solution.py:689
  222.6 3.7 %collective-permute-start.13 = (bf16[4,256,768]{2,1,0:T(8,128)(2,1)}, bf16[4,256,768]{2,1,0:T(8,128)(2,1)S(1)}, u32[]{:S(2)}, u32[]{:S(2)}) collective-permute-start(bf16[4,256,768]{2,1,0:T(8,128)(2,1)} %get-tuple-element.89), channel_id=1, source_target_pairs={{1,0},{2,1},{3,2},{5,4},{6,5},{7,6},{9,8},{10,9},{11,10},{13,12},{... | collective-permute-start | bytes 4718600 | tf_op jit(solution)/shard_map/ppermute | solution.py:954
  226.2 2.3 collective-permute-start.14
  228.7 1.3 collective-permute-start.15
  230.3 1.4 copy.51
  231.7 16.2 %weight_grads.1 = (bf16[4,352,768]{2,1,0:T(8,128)(2,1)}, bf16[4,352,768]{2,1,0:T(8,128)(2,1)}) custom-call(s32[1]{0:T(128)} %bitcast.41.core_ref, bf16[4,256,768]{2,1,0:T(8,128)(2,1)} %x_ref.2, bf16[4,256,768]{2,1,0:T(8,128)(2,1)} %collective-permute-done.10.left_ref, bf16[4,256,768]{2,1,0:T(8,128)(2,1)} %copy-done.1, bf16[4,1,768]{2,1,0:T(2,128)(2,1)} %copy-done.14, ...), custom_call_target="tpu_custom_call" | custom-call | flops 1048576 | bytes 1048576 | tf_op jit(solution)/shard_map/weight_grads/pallas_call | solution.py:774
  247.8 15.7 %collective-permute-done.15 = bf16[4,1,768]{2,1,0:T(2,128)(2,1)S(1)} collective-permute-done((bf16[4,1,768]{2,1,0:T(2,128)(2,1)}, bf16[4,1,768]{2,1,0:T(2,128)(2,1)S(1)}, u32[]{:S(2)}, u32[]{:S(2)}) %collective-permute-start.15) | collective-permute-done | bytes 6176 | tf_op jit(solution)/shard_map/ppermute | solution.py:954
  263.8 0.9 copy-done.6
  265.2 1.1 slice-done
  267.0 2.7 collective-permute-done.16
  270.7 2.6 collective-permute-start.18
  273.3 0.5 collective-permute-start.17
  273.9 1.9 collective-permute-start.20
  275.7 8.5 %collective-permute-done.22 = bf16[216,768]{1,0:T(8,128)(2,1)S(1)} collective-permute-done((bf16[216,768]{1,0:T(8,128)(2,1)S(1)}, bf16[216,768]{1,0:T(8,128)(2,1)S(1)}, u32[]{:S(2)}, u32[]{:S(2)}) %collective-permute-start.22) | collective-permute-done | bytes 331808 | tf_op jit(solution)/shard_map/ppermute | solution.py:912
  284.3 1.6 add_convert_fusion.1
  285.9 1.9 collective-permute-done.20
  287.8 10.8 %collective-permute-done.21 = bf16[216,768]{1,0:T(8,128)(2,1)S(1)} collective-permute-done((bf16[216,768]{1,0:T(8,128)(2,1)S(1)}, bf16[216,768]{1,0:T(8,128)(2,1)S(1)}, u32[]{:S(2)}, u32[]{:S(2)}) %collective-permute-start.21) | collective-permute-done | bytes 331808 | tf_op jit(solution)/shard_map/ppermute | solution.py:912
  298.8 0.6 slice.210
  299.9 0.6 collective-permute-start.25
  300.5 4.3 %collective-permute-start.23 = (bf16[88,768]{1,0:T(8,128)(2,1)S(1)}, bf16[88,768]{1,0:T(8,128)(2,1)S(1)}, u32[]{:S(2)}, u32[]{:S(2)}) collective-permute-start(bf16[88,768]{1,0:T(8,128)(2,1)S(1)} %get-tuple-element.116), channel_id=1, source_target_pairs={{0,1},{1,0},{2,3},{3,2},{4,5},{5,4},{6,7},{7,6},{8,9},{9,8},{10,11... | collective-permute-start | bytes 405512 | tf_op jit(solution)/shard_map/ppermute | solution.py:912
  304.8 0.8 fusion.26
  305.5 0.7 copy.57
  306.6 5.7 %collective-permute-done.23 = bf16[88,768]{1,0:T(8,128)(2,1)S(1)} collective-permute-done((bf16[88,768]{1,0:T(8,128)(2,1)S(1)}, bf16[88,768]{1,0:T(8,128)(2,1)S(1)}, u32[]{:S(2)}, u32[]{:S(2)}) %collective-permute-start.23) | collective-permute-done | bytes 135200 | tf_op jit(solution)/shard_map/ppermute | solution.py:912
  312.2 1.2 collective-permute-done.24
  313.5 0.5 slice_bitcast_fusion.3
  314.0 0.5 slice_bitcast_fusion
  314.6 0.6 slice.211
  315.2 0.7 fusion.28
  (131 shorter events, 8.2 us)
Async XLA Ops:
  7.2 42.6 %all-gather.5.cloned.1.call-start = ((), (), s32[]{:S(2)}) async-start(), calls=%async_computation.2 | async-start | bytes 1658880 | tf_op jit(solution)/shard_map/all_gather | solution.py:980
  8.8 12.5 %collective-permute-start.2 = (bf16[88,768]{1,0:T(8,128)(2,1)}, bf16[88,768]{1,0:T(8,128)(2,1)S(1)}, u32[]{:S(2)}, u32[]{:S(2)}) collective-permute-start(bf16[88,768]{1,0:T(8,128)(2,1)} %stack.76), channel_id=1, source_target_pairs={{0,3},{1,2},{2,1},{3,0},{4,7},{5,6},{6,5},{7,4},{8,11},{9,10},{10,... | collective-permute-start | bytes 405512 | tf_op jit(solution)/shard_map/ppermute | solution.py:856
  9.2 12.0 %collective-permute-start.1 = (bf16[88,768]{1,0:T(8,128)(2,1)}, bf16[88,768]{1,0:T(8,128)(2,1)S(1)}, u32[]{:S(2)}, u32[]{:S(2)}) collective-permute-start(bf16[88,768]{1,0:T(8,128)(2,1)} %stack.76), channel_id=1, source_target_pairs={{0,2},{1,3},{2,0},{3,1},{4,6},{5,7},{6,4},{7,5},{8,10},{9,11},{10,... | collective-permute-start | bytes 405512 | tf_op jit(solution)/shard_map/ppermute | solution.py:856
  12.7 8.6 %collective-permute-start = (bf16[88,768]{1,0:T(8,128)(2,1)}, bf16[88,768]{1,0:T(8,128)(2,1)S(1)}, u32[]{:S(2)}, u32[]{:S(2)}) collective-permute-start(bf16[88,768]{1,0:T(8,128)(2,1)} %stack.76), channel_id=1, source_target_pairs={{0,1},{1,0},{2,3},{3,2},{4,5},{5,4},{6,7},{7,6},{8,9},{9,8},{10,11... | collective-permute-start | bytes 405512 | tf_op jit(solution)/shard_map/ppermute | solution.py:856
  14.4 4.4 %copy-start.12 = (bf16[88,768]{1,0:T(8,128)(2,1)S(1)}, bf16[88,768]{1,0:T(8,128)(2,1)}, u32[]{:S(2)}) copy-start(bf16[88,768]{1,0:T(8,128)(2,1)} %stack.76) | copy-start | bytes 405508
  14.5 109.5 %all-gather.7.cloned.1.call-start = ((), (), s32[]{:S(2)}) async-start(), calls=%async_computation.3 | async-start | bytes 11943936 | tf_op jit(solution)/shard_map/all_gather | solution.py:993
  23.3 3.0 copy-start.5
  23.3 16.2 %collective-permute-start.8 = (bf16[352,768]{1,0:T(8,128)(2,1)S(1)}, bf16[352,768]{1,0:T(8,128)(2,1)S(1)}, u32[]{:S(2)}, u32[]{:S(2)}) collective-permute-start(bf16[352,768]{1,0:T(8,128)(2,1)S(1)} %pad_maximum_fusion.2.refs_1_), channel_id=1, source_target_pairs={{0,24},{8,16},{16,8},{24,0},{1,25},{9,17},{17,9},{25,1},{2,26},{10... | collective-permute-start | bytes 1622024 | tf_op jit(solution)/shard_map/ppermute | solution.py:868
  25.8 23.2 %collective-permute-start.6 = (bf16[352,768]{1,0:T(8,128)(2,1)S(1)}, bf16[352,768]{1,0:T(8,128)(2,1)S(1)}, u32[]{:S(2)}, u32[]{:S(2)}) collective-permute-start(bf16[352,768]{1,0:T(8,128)(2,1)S(1)} %pad_maximum_fusion.2.refs_1_), channel_id=1, source_target_pairs={{0,16},{8,24},{16,0},{24,8},{1,17},{9,25},{17,1},{25,9},{2,18},{10... | collective-permute-start | bytes 1622024 | tf_op jit(solution)/shard_map/ppermute | solution.py:868
  26.3 23.5 %collective-permute-start.4 = (bf16[352,768]{1,0:T(8,128)(2,1)S(1)}, bf16[352,768]{1,0:T(8,128)(2,1)}, u32[]{:S(2)}, u32[]{:S(2)}) collective-permute-start(bf16[352,768]{1,0:T(8,128)(2,1)S(1)} %pad_maximum_fusion.2.refs_1_), channel_id=1, source_target_pairs={{0,8},{8,0},{16,24},{24,16},{1,9},{9,1},{17,25},{25,17},{2,10},{10... | collective-permute-start | bytes 1622024 | tf_op jit(solution)/shard_map/ppermute | solution.py:868
  39.5 9.5 %copy-start.10 = (bf16[352,768]{1,0:T(8,128)(2,1)}, bf16[352,768]{1,0:T(8,128)(2,1)S(1)}, u32[]{:S(2)}) copy-start(bf16[352,768]{1,0:T(8,128)(2,1)S(1)} %collective-permute-done.8.refs_7_) | copy-start | bytes 1622020
  49.0 0.8 copy-start.11
  52.1 1.9 copy-start
  53.4 211.8 %reduce-scatter.2.cloned.1.call-start = ((), (), s32[]{:S(2)}) async-start(), calls=%async_computation.1 | async-start | bytes 11943936 | tf_op jit(solution)/shard_map/reduce_scatter | solution.py:1014
  54.0 39.3 %collective-permute-start.11 = (bf16[4,256,768]{2,1,0:T(8,128)(2,1)S(1)}, bf16[4,256,768]{2,1,0:T(8,128)(2,1)S(1)}, u32[]{:S(2)}, u32[]{:S(2)}) collective-permute-start(bf16[4,256,768]{2,1,0:T(8,128)(2,1)S(1)} %copy-done), channel_id=1, source_target_pairs={{1,0},{2,1},{3,2},{5,4},{6,5},{7,6},{9,8},{10,9},{11,10},{13,12},{... | collective-permute-start | bytes 4718600 | tf_op jit(solution)/shard_map/ppermute | solution.py:954
  57.3 38.8 %collective-permute-start.10 = (bf16[4,256,768]{2,1,0:T(8,128)(2,1)S(1)}, bf16[4,256,768]{2,1,0:T(8,128)(2,1)}, u32[]{:S(2)}, u32[]{:S(2)}) collective-permute-start(bf16[4,256,768]{2,1,0:T(8,128)(2,1)S(1)} %copy-done), channel_id=1, source_target_pairs={{0,1},{1,2},{2,3},{4,5},{5,6},{6,7},{8,9},{9,10},{10,11},{12,13},{... | collective-permute-start | bytes 4718600 | tf_op jit(solution)/shard_map/ppermute | solution.py:954
  60.5 2.3 collective-permute-start.3
  60.6 3.0 collective-permute-start.9
  61.1 8.2 %collective-permute-start.7 = (bf16[352,768]{1,0:T(8,128)(2,1)}, bf16[352,768]{1,0:T(8,128)(2,1)}, u32[]{:S(2)}, u32[]{:S(2)}) collective-permute-start(bf16[352,768]{1,0:T(8,128)(2,1)} %copy-done.11), channel_id=1, source_target_pairs={{0,4},{4,0},{1,5},{5,1},{2,6},{6,2},{3,7},{7,3},{8,12},{12,8},{9,1... | collective-permute-start | bytes 1622024 | tf_op jit(solution)/shard_map/ppermute | solution.py:890
  62.9 6.4 %collective-permute-start.5 = (bf16[352,768]{1,0:T(8,128)(2,1)}, bf16[352,768]{1,0:T(8,128)(2,1)}, u32[]{:S(2)}, u32[]{:S(2)}) collective-permute-start(bf16[352,768]{1,0:T(8,128)(2,1)} %collective-permute-done.4.refs_3_), channel_id=1, source_target_pairs={{0,4},{4,0},{1,5},{5,1},{2,6},{6,2},{3,7},{7,3},{8,12},{12,8},{9,1... | collective-permute-start | bytes 1622024 | tf_op jit(solution)/shard_map/ppermute | solution.py:890
  63.6 27.9 %collective-permute-start.12 = (bf16[4,1,768]{2,1,0:T(2,128)(2,1)S(1)}, bf16[4,1,768]{2,1,0:T(2,128)(2,1)S(1)}, u32[]{:S(2)}, u32[]{:S(2)}) collective-permute-start(bf16[4,1,768]{2,1,0:T(2,128)(2,1)S(1)} %slice.161), channel_id=1, source_target_pairs={{2,0},{3,1},{6,4},{7,5},{10,8},{11,9},{14,12},{15,13},{18,16},{19,... | collective-permute-start | bytes 18440 | tf_op jit(solution)/shard_map/ppermute | solution.py:954
  91.5 4.7 %copy-start.14 = (bf16[4,1,768]{2,1,0:T(2,128)(2,1)}, bf16[4,1,768]{2,1,0:T(2,128)(2,1)S(1)}, u32[]{:S(2)}) copy-start(bf16[4,1,768]{2,1,0:T(2,128)(2,1)S(1)} %collective-permute-done.12.far_ref) | copy-start | bytes 18436
  93.3 2.9 copy-start.1
  208.0 20.5 %copy-start.13 = (f32[4,16,768]{2,1,0:T(8,128)S(1)}, f32[4,16,768]{2,1,0:T(8,128)}, u32[]{:S(2)}) copy-start(f32[4,16,768]{2,1,0:T(8,128)} %get-tuple-element.84) | copy-start | bytes 589828
  208.0 20.6 %copy-start.15 = (f32[4,1,768]{2,1,0:T(1,128)S(1)}, f32[4,1,768]{2,1,0:T(1,128)}, u32[]{:S(2)}) copy-start(f32[4,1,768]{2,1,0:T(1,128)} %get-tuple-element.86) | copy-start | bytes 36868
  208.0 20.7 %copy-start.16 = (f32[8,768]{1,0:T(8,128)S(1)}, f32[8,768]{1,0:T(8,128)}, u32[]{:S(2)}) copy-start(f32[8,768]{1,0:T(8,128)} %get-tuple-element.85) | copy-start | bytes 73732
  222.6 41.0 %collective-permute-start.13 = (bf16[4,256,768]{2,1,0:T(8,128)(2,1)}, bf16[4,256,768]{2,1,0:T(8,128)(2,1)S(1)}, u32[]{:S(2)}, u32[]{:S(2)}) collective-permute-start(bf16[4,256,768]{2,1,0:T(8,128)(2,1)} %get-tuple-element.89), channel_id=1, source_target_pairs={{1,0},{2,1},{3,2},{5,4},{6,5},{7,6},{9,8},{10,9},{11,10},{13,12},{... | collective-permute-start | bytes 4718600 | tf_op jit(solution)/shard_map/ppermute | solution.py:954
  226.2 37.6 %collective-permute-start.14 = (bf16[4,256,768]{2,1,0:T(8,128)(2,1)}, bf16[4,256,768]{2,1,0:T(8,128)(2,1)S(1)}, u32[]{:S(2)}, u32[]{:S(2)}) collective-permute-start(bf16[4,256,768]{2,1,0:T(8,128)(2,1)} %get-tuple-element.90), channel_id=1, source_target_pairs={{0,1},{1,2},{2,3},{4,5},{5,6},{6,7},{8,9},{9,10},{10,11},{12,13},{... | collective-permute-start | bytes 4718600 | tf_op jit(solution)/shard_map/ppermute | solution.py:954
  228.7 34.8 %collective-permute-start.15 = (bf16[4,1,768]{2,1,0:T(2,128)(2,1)}, bf16[4,1,768]{2,1,0:T(2,128)(2,1)S(1)}, u32[]{:S(2)}, u32[]{:S(2)}) collective-permute-start(bf16[4,1,768]{2,1,0:T(2,128)(2,1)} %get-tuple-element.91), channel_id=1, source_target_pairs={{0,2},{1,3},{4,6},{5,7},{8,10},{9,11},{12,14},{13,15},{16,18},{17,... | collective-permute-start | bytes 18440 | tf_op jit(solution)/shard_map/ppermute | solution.py:954
  263.5 1.2 copy-start.6
  263.8 1.4 copy-start.8
  265.2 4.5 %collective-permute-start.16 = (bf16[4,352,768]{2,1,0:T(8,128)(2,1)}, bf16[4,352,768]{2,1,0:T(8,128)(2,1)S(1)}, u32[]{:S(2)}, u32[]{:S(2)}) collective-permute-start(bf16[4,352,768]{2,1,0:T(8,128)(2,1)} %get-tuple-element.96), channel_id=1, source_target_pairs={{0,4},{4,0},{1,5},{5,1},{2,6},{6,2},{3,7},{7,3},{8,12},{12,8},{9,1... | collective-permute-start | bytes 6488072 | tf_op jit(solution)/shard_map/ppermute | solution.py:1052
  265.2 1.1 slice-start
  265.2 1.6 copy-start.3
  266.7 2.9 copy-start.4
  266.9 17.4 %collective-permute-start.22 = (bf16[216,768]{1,0:T(8,128)(2,1)S(1)}, bf16[216,768]{1,0:T(8,128)(2,1)S(1)}, u32[]{:S(2)}, u32[]{:S(2)}) collective-permute-start(bf16[216,768]{1,0:T(8,128)(2,1)S(1)} %get-tuple-element.110), channel_id=1, source_target_pairs={{0,3},{1,2},{2,1},{3,0},{4,7},{5,6},{6,5},{7,4},{8,11},{9,10},{10,... | collective-permute-start | bytes 995336 | tf_op jit(solution)/shard_map/ppermute | solution.py:912
  269.7 14.6 %copy-start.7 = (bf16[4,256,768]{2,1,0:T(8,128)(2,1)S(1)}, bf16[4,256,768]{2,1,0:T(8,128)(2,1)}, u32[]{:S(2)}) copy-start(bf16[4,256,768]{2,1,0:T(8,128)(2,1)} %copy-done.6) | copy-start | bytes 4718596
  269.7 14.6 %copy-start.9 = (bf16[4,256,768]{2,1,0:T(8,128)(2,1)S(1)}, bf16[4,256,768]{2,1,0:T(8,128)(2,1)}, u32[]{:S(2)}) copy-start(bf16[4,256,768]{2,1,0:T(8,128)(2,1)} %copy-done.8) | copy-start | bytes 4718596
  270.2 14.1 %copy-start.2 = (f32[4,256,768]{2,1,0:T(8,128)S(1)}, f32[4,256,768]{2,1,0:T(8,128)}, u32[]{:S(2)}) copy-start(f32[4,256,768]{2,1,0:T(8,128)} %get-tuple-element.82) | copy-start | bytes 9437188
  270.3 29.1 %collective-permute-start.19 = (bf16[352,768]{1,0:T(8,128)(2,1)S(1)}, bf16[352,768]{1,0:T(8,128)(2,1)S(1)}, u32[]{:S(2)}, u32[]{:S(2)}) collective-permute-start(bf16[352,768]{1,0:T(8,128)(2,1)S(1)} %get-tuple-element.107), channel_id=1, source_target_pairs={{0,24},{8,16},{16,8},{24,0},{1,25},{9,17},{17,9},{25,1},{2,26},{10... | collective-permute-start | bytes 1622024 | tf_op jit(solution)/shard_map/ppermute | solution.py:912
  270.7 28.7 %collective-permute-start.18 = (bf16[352,768]{1,0:T(8,128)(2,1)S(1)}, bf16[352,768]{1,0:T(8,128)(2,1)S(1)}, u32[]{:S(2)}, u32[]{:S(2)}) collective-permute-start(bf16[352,768]{1,0:T(8,128)(2,1)S(1)} %get-tuple-element.108), channel_id=1, source_target_pairs={{0,16},{8,24},{16,0},{24,8},{1,17},{9,25},{17,1},{25,9},{2,18},{10... | collective-permute-start | bytes 1622024 | tf_op jit(solution)/shard_map/ppermute | solution.py:912
  273.3 26.1 %collective-permute-start.17 = (bf16[352,768]{1,0:T(8,128)(2,1)S(1)}, bf16[352,768]{1,0:T(8,128)(2,1)S(1)}, u32[]{:S(2)}, u32[]{:S(2)}) collective-permute-start(bf16[352,768]{1,0:T(8,128)(2,1)S(1)} %get-tuple-element.109), channel_id=1, source_target_pairs={{0,8},{8,0},{16,24},{24,16},{1,9},{9,1},{17,25},{25,17},{2,10},{10... | collective-permute-start | bytes 1622024 | tf_op jit(solution)/shard_map/ppermute | solution.py:912
  273.9 13.9 %collective-permute-start.20 = (bf16[216,768]{1,0:T(8,128)(2,1)S(1)}, bf16[216,768]{1,0:T(8,128)(2,1)S(1)}, u32[]{:S(2)}, u32[]{:S(2)}) collective-permute-start(bf16[216,768]{1,0:T(8,128)(2,1)S(1)} %get-tuple-element.111), channel_id=1, source_target_pairs={{0,1},{1,0},{2,3},{3,2},{4,5},{5,4},{6,7},{7,6},{8,9},{9,8},{10,11... | collective-permute-start | bytes 995336 | tf_op jit(solution)/shard_map/ppermute | solution.py:912
  284.3 14.3 %collective-permute-start.21 = (bf16[216,768]{1,0:T(8,128)(2,1)S(1)}, bf16[216,768]{1,0:T(8,128)(2,1)S(1)}, u32[]{:S(2)}, u32[]{:S(2)}) collective-permute-start(bf16[216,768]{1,0:T(8,128)(2,1)S(1)} %get-tuple-element.112), channel_id=1, source_target_pairs={{0,2},{1,3},{2,0},{3,1},{4,6},{5,7},{6,4},{7,5},{8,10},{9,11},{10,... | collective-permute-start | bytes 995336 | tf_op jit(solution)/shard_map/ppermute | solution.py:912
  299.9 6.7 %collective-permute-start.25 = (bf16[88,768]{1,0:T(8,128)(2,1)S(1)}, bf16[88,768]{1,0:T(8,128)(2,1)S(1)}, u32[]{:S(2)}, u32[]{:S(2)}) collective-permute-start(bf16[88,768]{1,0:T(8,128)(2,1)S(1)} %get-tuple-element.115), channel_id=1, source_target_pairs={{0,3},{1,2},{2,1},{3,0},{4,7},{5,6},{6,5},{7,4},{8,11},{9,10},{10,... | collective-permute-start | bytes 405512 | tf_op jit(solution)/shard_map/ppermute | solution.py:912
  300.5 11.8 %collective-permute-start.23 = (bf16[88,768]{1,0:T(8,128)(2,1)S(1)}, bf16[88,768]{1,0:T(8,128)(2,1)S(1)}, u32[]{:S(2)}, u32[]{:S(2)}) collective-permute-start(bf16[88,768]{1,0:T(8,128)(2,1)S(1)} %get-tuple-element.116), channel_id=1, source_target_pairs={{0,1},{1,0},{2,3},{3,2},{4,5},{5,4},{6,7},{7,6},{8,9},{9,8},{10,11... | collective-permute-start | bytes 405512 | tf_op jit(solution)/shard_map/ppermute | solution.py:912
  304.8 8.7 %collective-permute-start.24 = (bf16[88,768]{1,0:T(8,128)(2,1)S(1)}, bf16[88,768]{1,0:T(8,128)(2,1)S(1)}, u32[]{:S(2)}, u32[]{:S(2)}) collective-permute-start(bf16[88,768]{1,0:T(8,128)(2,1)S(1)} %get-tuple-element.117), channel_id=1, source_target_pairs={{0,2},{1,3},{2,0},{3,1},{4,6},{5,7},{6,4},{7,5},{8,10},{9,11},{10,... | collective-permute-start | bytes 405512 | tf_op jit(solution)/shard_map/ppermute | solution.py:912
Sparse Core Ops, SparseCore 0:
  14.6 33.4 all-gather.4
  53.5 65.8 all-gather.6
  179.3 81.6 reduce-scatter.1

commit v2 on v1

--- a/solution.py
+++ b/solution.py
@@ -349,13 +349,13 @@
 
     def in_copy(panel, slot):
         return pltpu.make_async_copy(
-            d_in_stage.at[slot], d_weights_ref.at[:, panels + panel], in_sems.at[slot]
+            d_in_stage.at[slot], d_weights_ref.at[:, :, panels + panel], in_sems.at[slot]
         )
 
     def out_copy(panel, slot):
         return pltpu.make_async_copy(
             d_out_stage.at[slot],
-            d_weights_ref.at[pl.ds(panel * some, some), pl.ds(0, panels)],
+            d_weights_ref.at[pl.ds(panel * some, some), :, pl.ds(0, panels)],
             out_sems.at[slot],
         )
 
@@ -394,7 +394,7 @@
             acc[rows, :] += nn(out, square(w_out_ref))
             return carry
 
-        lax.fori_loop(0, chunks, body, 0)
+        lax.fori_loop(0, chunks, body, 0, unroll=True)
 
     @pl.when(step == panels)
     def _():
@@ -477,7 +477,7 @@
 
 def feed_forward(x, mixed, cot, small, bias, weights):
     tokens, width = x.shape
-    units, groups, rows_in, _ = weights.shape
+    units, column, groups, share, _ = weights.shape
     panels = groups // 2
     panel = width
 
@@ -497,15 +497,18 @@
             whole(tokens, width),
             whole(tokens, width),
             pl.BlockSpec(
-                (units, 1, rows_in, width),
-                lambda j: (0, 2 * panels, 0, 0),
+                (units, column, 1, share, width),
+                lambda j: (0, 0, 2 * panels, 0, 0),
                 pipeline_mode=pl.Buffered(buffer_count=1),
             ),
             whole(8, width),
             pl.BlockSpec((1, 1, panel), lambda j: (lax.rem(j, panels), 0, 0)),
-            pl.BlockSpec((units, 1, rows_in, width), lambda j: (0, panels + lax.rem(j, panels), 0, 0)),
             pl.BlockSpec(
-                (units // panels, panels, rows_in, width), lambda j: (lax.rem(j, panels), 0, 0, 0)
+                (units, column, 1, share, width), lambda j: (0, 0, panels + lax.rem(j, panels), 0, 0)
+            ),
+            pl.BlockSpec(
+                (units // panels, column, panels, share, width),
+                lambda j: (lax.rem(j, panels), 0, 0, 0, 0),
             ),
         ],
         out_specs=[
@@ -531,8 +534,8 @@
             pltpu.VMEM((panels, tokens, panel), BF16),
             pltpu.VMEM((panels, tokens, panel), F32),
             pltpu.VMEM((tokens, panel), BF16),
-            pltpu.VMEM((2, units, rows_in, width), BF16),
-            pltpu.VMEM((2, units // panels, panels, rows_in, width), BF16),
+            pltpu.VMEM((2, units, column, share, width), BF16),
+            pltpu.VMEM((2, units // panels, column, panels, share, width), BF16),
             pltpu.SemaphoreType.DMA((2,)),
             pltpu.SemaphoreType.DMA((2,)),
         ],
@@ -980,18 +983,8 @@
     late_column = lax.all_gather(late, "seq", axis=0)
     late_column = after(late_column, [piece for piece, _ in early_pieces[1:]])
     outer_rows = panels * share
-    late_column = jnp.concatenate(
-        (
-            late_column[:, :outer_rows].reshape(-1, width),
-            late_column[:, outer_rows:]
-            .reshape(seq_count, panels + 1, share, width)
-            .swapaxes(0, 1)
-            .reshape(-1, width),
-        ),
-        axis=0,
-    )
     late = lax.all_gather(late_column, ("yx", "core"), axis=0)
-    late = late.reshape(units, 2 * panels + 1, seq_count * share, width)
+    late = late.reshape(units, seq_count, 2 * panels + 1, share, width)
     small = early[:, 3 * seq_count * share :].reshape(parts, SMALL, width)
     vectors = small[:, : SMALL - 1, :share].transpose(1, 0, 2).reshape(SMALL - 1, width).astype(F32)
     taps = jnp.pad(vectors[:10], ((0, 6), (0, 0)))
@@ -1030,7 +1023,8 @@
     left, right, far, own = input_grads(
         d_queries, d_keys, d_values, d_first.reshape(seqs, group, width), early
     )
-    back = (shift(left, -1), shift(right, 1), shift(far, 2))
+    from_far = shift(far, 2)
+    back = (from_far, shift(left, -1), shift(right, 1))
 
     d_taps = jnp.sum(d_taps, axis=0)[:10]
     d_vectors = jnp.concatenate((d_taps, d_small[:5]), axis=0)
@@ -1048,22 +1042,11 @@
         d_values,
         d_vectors,
     )
-    (mine, other), back = after(((mine, other), back))
+    (mine, other), back, late_sum = after(((mine, other), back, late_sum))
+    late_sum = lax.psum_scatter(late_sum, "seq", scatter_dimension=0, tiled=True).astype(F32)
     swapped = lax.ppermute(other, "core", [(0, 1), (1, 0)])
     early_sum = (mine.astype(F32) + swapped.astype(F32)).astype(BF16)
-    outer_all = seq_count * outer_rows
-    late_sum = jnp.concatenate(
-        (
-            late_sum[:outer_all].reshape(seq_count, outer_rows, width),
-            late_sum[outer_all:]
-            .reshape(panels + 1, seq_count, share, width)
-            .swapaxes(0, 1)
-            .reshape(seq_count, (panels + 1) * share, width),
-        ),
-        axis=1,
-    )
-    late_sum = exchange_sum(late_sum, "seq")
-    early_sum = exchange_sum(early_sum, "yx", late_sum).astype(BF16)
+    early_sum = exchange_sum(early_sum, "yx").astype(BF16)
     whole = 3 * seq_count * share
     early_sum = jnp.concatenate(
         [
@@ -1078,7 +1061,7 @@
     early_sum = exchange_sum(early_sum, "seq")
 
     edge = group - HALO
-    from_right, from_left, from_far = (part.astype(F32) for part in back)
+    from_far, from_right, from_left = (part.astype(F32) for part in back)
     d_input = own + jnp.pad(from_right, ((0, 0), (edge, 0), (0, 0)))
     d_input = d_input + jnp.pad(from_left, ((0, 0), (0, edge), (0, 0)))
     d_input = d_input + jnp.pad(from_far, ((0, 0), (0, group - 1), (0, 0)))

time: 326 us -> 322 us (0.988)
  other arithmetic: 8.15 us -> 13.2 us
  waiting for transfers between devices: 83.5 us -> 80 us
    ppermute x9 -> x6, waiting for transfers between devices: 28.4 us -> 24.4 us  [exchange_sum(): lax.ppermute(pick(pieces, met(me)[0]), axis, pairs)]
    slice x5 -> x0, local copies, waits for them, and re-layouts: 3.42 us -> none  [the longest x1 1.17 us: local(): late_column[:, outer_rows:].reshape(seq_count, panels + 1, share, width)]
    ppermute x9 -> x6, starting transfers between devices: 10.4 us -> 7.67 us  [exchange_sum(): lax.ppermute(pick(pieces, met(me)[0]), axis, pairs)]
  transfers between devices with their start and end apart: 29 -> 27, of which waited for: 16 -> 15; matrix products, arithmetic and copies ran while one was open for 6% -> 9% of each run, Pallas kernels for 31% -> 32%
where the time goes in v2:
time: 322 us; the launch traced here: 318 us
  Pallas kernels  157 us (49%)
  waiting for transfers between devices  80 us (25%)
  starting transfers between devices  35.5 us (11%)
  local copies, waits for them, and re-layouts  18.5 us (6%)
  between operations  14.4 us (4%)
  other arithmetic  13.2 us (4%)
    pallas_call x1, Pallas kernels, feed_forward(): pl.pallas_call(functools.partial(ffn_kernel, panels), grid=(2 * panels,),...  53.9 us
    pallas_call x1, Pallas kernels, attention_backward(): pl.pallas_call(kernel, grid=(count,), in_specs=attention_specs(ext, group...  29 us
    ppermute x6, waiting for transfers between devices, shift(): return lax.ppermute(value, 'seq', pairs)  27.4 us
    ppermute x6, waiting for transfers between devices, exchange_sum(): lax.ppermute(pick(pieces, met(me)[0]), axis, pairs)  24.4 us
    ppermute x3, waiting for transfers between devices, gather_yx(): pieces.append((lax.ppermute(column, 'yx', pairs), met(me)[1]))  22.1 us
    ppermute x6, starting transfers between devices, shift(): return lax.ppermute(value, 'seq', pairs)  19.4 us
    pallas_call x1, Pallas kernels, attention_forward(): pl.pallas_call(attn_fwd_kernel, grid=(seqs,), in_specs=attention_specs(ex...  16.6 us
    pallas_call x1, Pallas kernels, weight_grads(): pl.pallas_call(weight_grad_kernel, grid=(seqs,), in_specs=[pl.BlockSpec(m...  16.2 us
  transfers between devices with their start and end apart: 27, of which 15 were waited for; matrix products, arithmetic and copies ran while one was open for 9% of the time, Pallas kernels for 32%

profile of v2, /device:TPU:16, one launch (start us, length us, event | category | flops | bytes accessed | tf_op | source)
XLA Modules:
  0.0 318.1 jit_solution(13163851209818683575)
XLA Ops:
  7.2 1.5 stack.76
  8.8 0.4 collective-permute-start.2
  9.2 3.5 %collective-permute-start.1 = (bf16[88,768]{1,0:T(8,128)(2,1)}, bf16[88,768]{1,0:T(8,128)(2,1)S(1)}, u32[]{:S(2)}, u32[]{:S(2)}) collective-permute-start(bf16[88,768]{1,0:T(8,128)(2,1)} %stack.76), channel_id=1, source_target_pairs={{0,2},{1,3},{2,0},{3,1},{4,6},{5,7},{6,4},{7,5},{8,10},{9,11},{10,... | collective-permute-start | bytes 405512 | tf_op jit(solution)/shard_map/ppermute | solution.py:859
  12.7 1.7 pack.1
  14.6 0.8 select_reduce_fusion
  17.2 0.9 abs_compare_fusion.1
  18.9 1.4 pad_maximum_fusion.bias_ref.refs_5_
  20.2 1.0 collective-permute-done.2
  21.3 1.8 broadcast_in_dim.87.same_ref.refs_4_
  23.3 2.5 collective-permute-start.8
  25.8 0.5 collective-permute-start.6
  26.3 0.5 collective-permute-start.4
  26.8 12.7 %collective-permute-done.8.refs_7_ = bf16[352,768]{1,0:T(8,128)(2,1)S(1)} collective-permute-done((bf16[352,768]{1,0:T(8,128)(2,1)S(1)}, bf16[352,768]{1,0:T(8,128)(2,1)S(1)}, u32[]{:S(2)}, u32[]{:S(2)}) %collective-permute-start.8) | collective-permute-done | bytes 540704 | tf_op jit(solution)/shard_map/ppermute | solution.py:871
  39.5 9.5 %collective-permute-done.6.refs_5_ = bf16[352,768]{1,0:T(8,128)(2,1)S(1)} collective-permute-done((bf16[352,768]{1,0:T(8,128)(2,1)S(1)}, bf16[352,768]{1,0:T(8,128)(2,1)S(1)}, u32[]{:S(2)}, u32[]{:S(2)}) %collective-permute-start.6) | collective-permute-done | bytes 540704 | tf_op jit(solution)/shard_map/ppermute | solution.py:871
  49.0 0.8 copy-done.6
  49.9 3.3 %collective-permute-start.11 = (bf16[4,256,768]{2,1,0:T(8,128)(2,1)S(1)}, bf16[4,256,768]{2,1,0:T(8,128)(2,1)S(1)}, u32[]{:S(2)}, u32[]{:S(2)}) collective-permute-start(bf16[4,256,768]{2,1,0:T(8,128)(2,1)S(1)} %copy-done), channel_id=1, source_target_pairs={{1,0},{2,1},{3,2},{5,4},{6,5},{7,6},{9,8},{10,9},{11,10},{13,12},{... | collective-permute-start | bytes 4718600 | tf_op jit(solution)/shard_map/ppermute | solution.py:957
  53.2 3.2 %collective-permute-start.10 = (bf16[4,256,768]{2,1,0:T(8,128)(2,1)S(1)}, bf16[4,256,768]{2,1,0:T(8,128)(2,1)}, u32[]{:S(2)}, u32[]{:S(2)}) collective-permute-start(bf16[4,256,768]{2,1,0:T(8,128)(2,1)S(1)} %copy-done), channel_id=1, source_target_pairs={{0,1},{1,2},{2,3},{4,5},{5,6},{6,7},{8,9},{9,10},{10,11},{12,13},{... | collective-permute-start | bytes 4718600 | tf_op jit(solution)/shard_map/ppermute | solution.py:957
  56.5 0.5 collective-permute-start.9
  57.1 1.7 collective-permute-done.3.refs_2_
  58.9 0.6 stack.67.refs_0_
  59.5 5.7 %collective-permute-start.12 = (bf16[4,1,768]{2,1,0:T(2,128)(2,1)S(1)}, bf16[4,1,768]{2,1,0:T(2,128)(2,1)S(1)}, u32[]{:S(2)}, u32[]{:S(2)}) collective-permute-start(bf16[4,1,768]{2,1,0:T(2,128)(2,1)S(1)} %slice.149), channel_id=1, source_target_pairs={{2,0},{3,1},{6,4},{7,5},{10,8},{11,9},{14,12},{15,13},{18,16},{19,... | collective-permute-start | bytes 18440 | tf_op jit(solution)/shard_map/ppermute | solution.py:957
  65.2 4.2 %assemble.1.w_ref = bf16[8,352,768]{2,1,0:T(8,128)(2,1)} custom-call(s32[8]{0:T(128)} %stack.67.refs_0_, bf16[352,768]{1,0:T(8,128)(2,1)} %copy-done.2, bf16[352,768]{1,0:T(8,128)(2,1)} %collective-permute-done.3.refs_2_, bf16[352,768]{1,0:T(8,128)(2,1)} %collective-permute-done.4.refs_3_, bf16[352,768]{1,0:T(8,128)(2,1)} %collective-permute-done.5.refs_4_, ...), custom_call_target="tpu_custom_call" | custom-call | flops 1048576 | bytes 1048576 | tf_op jit(solution)/shard_map/assemble/pallas_call | solution.py:895
  69.4 1.2 slice.180
  70.8 0.7 reshape.289.bias_ref
  71.7 0.6 pad.25.w_ref.refs_3_
  72.3 0.6 pad.26.small_ref
  73.0 7.6 %project_own.1 = (bf16[4,256,768]{2,1,0:T(8,128)(2,1)}, bf16[4,256,768]{2,1,0:T(8,128)(2,1)}, bf16[4,256,768]{2,1,0:T(8,128)(2,1)}) custom-call(bf16[4,256,768]{2,1,0:T(8,128)(2,1)} %x_ref.2, bf16[8,352,768]{2,1,0:T(8,128)(2,1)} %assemble.1.w_ref), custom_call_target="tpu_custom_call" | custom-call | flops 1048576 | bytes 1048576 | tf_op jit(solution)/shard_map/project_own/pallas_call | solution.py:648
  80.5 6.9 %collective-permute-done.12.far_ref = bf16[4,1,768]{2,1,0:T(2,128)(2,1)S(1)} collective-permute-done((bf16[4,1,768]{2,1,0:T(2,128)(2,1)S(1)}, bf16[4,1,768]{2,1,0:T(2,128)(2,1)S(1)}, u32[]{:S(2)}, u32[]{:S(2)}) %collective-permute-start.12) | collective-permute-done | bytes 6176 | tf_op jit(solution)/shard_map/ppermute | solution.py:957
  87.4 1.8 collective-permute-done.11.right_ref
  89.2 2.9 collective-permute-done.10.left_ref
  92.0 11.2 %project_halos.1 = (bf16[4,784,768]{2,1,0:T(8,128)(2,1)}, bf16[4,784,768]{2,1,0:T(8,128)(2,1)}) custom-call(bf16[4,256,768]{2,1,0:T(8,128)(2,1)} %get-tuple-element.64.own_k_ref, bf16[4,256,768]{2,1,0:T(8,128)(2,1)} %get-tuple-element.65.own_v_ref, bf16[4,256,768]{2,1,0:T(8,128)(2,1)} %collective-permute-done.10.left_ref, bf16[4,256,768]{2,1,0:T(8,128)(2,1)} %copy-done.1, ...), custom_call_target="tpu_custom_call" | custom-call | flops 1048576 | bytes 1048576 | tf_op jit(solution)/shard_map/project_halos/pallas_call | solution.py:663
  103.3 16.6 %attn_fwd.1 = (bf16[4,256,768]{2,1,0:T(8,128)(2,1)}, f32[4,6,2,256]{3,2,1,0:T(2,128)}) custom-call(bf16[4,256,768]{2,1,0:T(8,128)(2,1)} %get-tuple-element.63.q_ref.refs_0_, bf16[4,784,768]{2,1,0:T(8,128)(2,1)} %get-tuple-element.67.k_ref.refs_1_, bf16[4,784,768]{2,1,0:T(8,128)(2,1)} %get-tuple-element.68.v_ref.refs_2_, f32[16,768]{1,0:T(8,128)} %pad.25.w_ref.refs_3_, ...), custom_call_target="tpu_custom_call" | custom-call | flops 1048576 | bytes 1048576 | tf_op jit(solution)/shard_map/attn_fwd/pallas_call | solution.py:240
  119.8 53.9 %ffn.1 = (bf16[1024,768]{1,0:T(8,128)(2,1)}, f32[1024,768]{1,0:T(8,128)}, bf16[1024,768]{1,0:T(8,128)(2,1)}, f32[8,768]{1,0:T(8,128)}, f32[4,1,768]{2,1,0:T(1,128)}, /*index=5*/bf16[8,4,9,24,768]{4,3,2,1,0:T(8,128)(2,1)}) custom-call(bf16[1024,768]{1,0:T(8,128)(2,1)} %bitcast.99, bf16[1024,768]{1,0:T(8,128)(2,1)} %bitcast.107, bf16[1024,768]{1,0:T(8,128)(2,1)} %bitcast.106, ...), custom_call_target="tpu_custom_call" | custom-call | flops 1048576 | bytes 1048576 | tf_op jit(solution)/shard_map/ffn/pallas_call | solution.py:492
  173.8 29.0 %attn_bwd.1 = (bf16[4,256,768]{2,1,0:T(8,128)(2,1)}, bf16[4,784,768]{2,1,0:T(8,128)(2,1)}, bf16[4,784,768]{2,1,0:T(8,128)(2,1)}, f32[4,16,768]{2,1,0:T(8,128)}) custom-call(bf16[4,256,768]{2,1,0:T(8,128)(2,1)} %get-tuple-element.63.q_ref.refs_0_, bf16[4,784,768]{2,1,0:T(8,128)(2,1)} %get-tuple-element.67.k_ref.refs_1_, ...), custom_call_target="tpu_custom_call" | custom-call | flops 1048576 | bytes 1048576 | tf_op jit(solution)/shard_map/attn_bwd/pallas_call | solution.py:270
  202.9 14.4 %input_grads.1 = (bf16[4,256,768]{2,1,0:T(8,128)(2,1)}, bf16[4,256,768]{2,1,0:T(8,128)(2,1)}, bf16[4,1,768]{2,1,0:T(2,128)(2,1)}, f32[4,256,768]{2,1,0:T(8,128)}) custom-call(bf16[4,256,768]{2,1,0:T(8,128)(2,1)} %get-tuple-element.76.dq_ref, bf16[4,784,768]{2,1,0:T(8,128)(2,1)} %get-tuple-element.77.dk_ref, bf16[4,784,768]{2,1,0:T(8,128)(2,1)} %get-tuple-element.78.dv_ref, ...), custom_call_target="tpu_custom_call" | custom-call | flops 1048576 | bytes 1048576 | tf_op jit(solution)/shard_map/input_grads/pallas_call | solution.py:692
  217.4 3.6 %collective-permute-start.14 = (bf16[4,256,768]{2,1,0:T(8,128)(2,1)}, bf16[4,256,768]{2,1,0:T(8,128)(2,1)S(1)}, u32[]{:S(2)}, u32[]{:S(2)}) collective-permute-start(bf16[4,256,768]{2,1,0:T(8,128)(2,1)} %get-tuple-element.88), channel_id=1, source_target_pairs={{1,0},{2,1},{3,2},{5,4},{6,5},{7,6},{9,8},{10,9},{11,10},{13,12},{... | collective-permute-start | bytes 4718600 | tf_op jit(solution)/shard_map/ppermute | solution.py:957
  220.9 2.4 collective-permute-start.15
  223.5 1.3 collective-permute-start.13
  225.1 1.3 copy.52
  226.4 16.2 %weight_grads.1 = (bf16[4,352,768]{2,1,0:T(8,128)(2,1)}, bf16[4,352,768]{2,1,0:T(8,128)(2,1)}) custom-call(s32[1]{0:T(128)} %bitcast.37.core_ref, bf16[4,256,768]{2,1,0:T(8,128)(2,1)} %x_ref.2, bf16[4,256,768]{2,1,0:T(8,128)(2,1)} %collective-permute-done.10.left_ref, bf16[4,256,768]{2,1,0:T(8,128)(2,1)} %copy-done.1, bf16[4,1,768]{2,1,0:T(2,128)(2,1)} %copy-done.9, ...), custom_call_target="tpu_custom_call" | custom-call | flops 1048576 | bytes 1048576 | tf_op jit(solution)/shard_map/weight_grads/pallas_call | solution.py:777
  242.7 15.6 %collective-permute-done.13 = bf16[4,1,768]{2,1,0:T(2,128)(2,1)S(1)} collective-permute-done((bf16[4,1,768]{2,1,0:T(2,128)(2,1)}, bf16[4,1,768]{2,1,0:T(2,128)(2,1)S(1)}, u32[]{:S(2)}, u32[]{:S(2)}) %collective-permute-start.13) | collective-permute-done | bytes 6176 | tf_op jit(solution)/shard_map/ppermute | solution.py:957
  258.3 0.3 collective-permute-done.15
  258.7 0.8 copy-done.3
  259.5 0.5 copy-done.4
  260.0 3.2 %collective-permute-done.16 = bf16[4,352,768]{2,1,0:T(8,128)(2,1)} collective-permute-done((bf16[4,352,768]{2,1,0:T(8,128)(2,1)}, bf16[4,352,768]{2,1,0:T(8,128)(2,1)}, u32[]{:S(2)}, u32[]{:S(2)}) %collective-permute-start.16) | collective-permute-done | bytes 2162720 | tf_op jit(solution)/shard_map/ppermute | solution.py:1047
  263.2 2.8 add_convert_fusion
  266.0 1.0 dynamic-slice_bitcast_fusion
  267.2 2.7 collective-permute-start.18
  269.9 0.5 collective-permute-start.17
  270.4 4.5 %add_convert_fusion.1 = bf16[4,256,768]{2,1,0:T(8,128)(2,1)} fusion(bf16[4,256,768]{2,1,0:T(8,128)(2,1)} %copy-done.4, f32[4,256,768]{2,1,0:T(8,128)} %get-tuple-element.80, bf16[4,256,768]{2,1,0:T(8,128)(2,1)} %copy-done.3, bf16[4,1,768]{2,1,0:T(2,128)(2,1)S(1)} %collective-permute-done.13), kind=kLoop, calls=%fused_computation.1 | loop fusion | flops 5505024 | bytes 7870464 | tf_op jit(solution)/shard_map/convert_element_type | solution.py:1073
  274.9 8.4 %collective-permute-done.19 = bf16[352,768]{1,0:T(8,128)(2,1)} collective-permute-done((bf16[352,768]{1,0:T(8,128)(2,1)}, bf16[352,768]{1,0:T(8,128)(2,1)}, u32[]{:S(2)}, u32[]{:S(2)}) %collective-permute-start.19) | collective-permute-done | bytes 540704 | tf_op jit(solution)/shard_map/ppermute | solution.py:915
  283.3 10.6 %collective-permute-done.18 = bf16[352,768]{1,0:T(8,128)(2,1)} collective-permute-done((bf16[352,768]{1,0:T(8,128)(2,1)S(1)}, bf16[352,768]{1,0:T(8,128)(2,1)}, u32[]{:S(2)}, u32[]{:S(2)}) %collective-permute-start.18) | collective-permute-done | bytes 540704 | tf_op jit(solution)/shard_map/ppermute | solution.py:915
  293.9 1.6 fusion.4
  295.8 1.8 collective-permute-start.20
  297.6 2.3 collective-permute-start.21
  299.9 1.7 fusion.17
  301.6 0.7 copy.57
  302.3 1.4 slice.192
  303.8 0.9 collective-permute-done.22
  304.9 4.3 %collective-permute-done.21 = bf16[88,768]{1,0:T(8,128)(2,1)S(1)} collective-permute-done((bf16[88,768]{1,0:T(8,128)(2,1)S(1)}, bf16[88,768]{1,0:T(8,128)(2,1)S(1)}, u32[]{:S(2)}, u32[]{:S(2)}) %collective-permute-start.21) | collective-permute-done | bytes 135200 | tf_op jit(solution)/shard_map/ppermute | solution.py:915
  309.2 0.5 slice_bitcast_fusion.3
  309.7 0.5 slice_bitcast_fusion
  310.3 0.6 slice.193
  310.9 0.7 fusion.18
  (108 shorter events, 4.6 us)
Async XLA Ops:
  7.2 42.6 %all-gather.5.cloned.1.call-start = ((), (), s32[]{:S(2)}) async-start(), calls=%async_computation.4 | async-start | bytes 1658880 | tf_op jit(solution)/shard_map/all_gather | solution.py:983
  8.8 12.5 %collective-permute-start.2 = (bf16[88,768]{1,0:T(8,128)(2,1)}, bf16[88,768]{1,0:T(8,128)(2,1)S(1)}, u32[]{:S(2)}, u32[]{:S(2)}) collective-permute-start(bf16[88,768]{1,0:T(8,128)(2,1)} %stack.76), channel_id=1, source_target_pairs={{0,3},{1,2},{2,1},{3,0},{4,7},{5,6},{6,5},{7,4},{8,11},{9,10},{10,... | collective-permute-start | bytes 405512 | tf_op jit(solution)/shard_map/ppermute | solution.py:859
  9.2 12.0 %collective-permute-start.1 = (bf16[88,768]{1,0:T(8,128)(2,1)}, bf16[88,768]{1,0:T(8,128)(2,1)S(1)}, u32[]{:S(2)}, u32[]{:S(2)}) collective-permute-start(bf16[88,768]{1,0:T(8,128)(2,1)} %stack.76), channel_id=1, source_target_pairs={{0,2},{1,3},{2,0},{3,1},{4,6},{5,7},{6,4},{7,5},{8,10},{9,11},{10,... | collective-permute-start | bytes 405512 | tf_op jit(solution)/shard_map/ppermute | solution.py:859
  12.7 8.6 %collective-permute-start = (bf16[88,768]{1,0:T(8,128)(2,1)}, bf16[88,768]{1,0:T(8,128)(2,1)S(1)}, u32[]{:S(2)}, u32[]{:S(2)}) collective-permute-start(bf16[88,768]{1,0:T(8,128)(2,1)} %stack.76), channel_id=1, source_target_pairs={{0,1},{1,0},{2,3},{3,2},{4,5},{5,4},{6,7},{7,6},{8,9},{9,8},{10,11... | collective-permute-start | bytes 405512 | tf_op jit(solution)/shard_map/ppermute | solution.py:859
  14.5 4.4 %copy-start.7 = (bf16[88,768]{1,0:T(8,128)(2,1)S(1)}, bf16[88,768]{1,0:T(8,128)(2,1)}, u32[]{:S(2)}) copy-start(bf16[88,768]{1,0:T(8,128)(2,1)} %stack.76) | copy-start | bytes 405508
  14.5 105.4 %all-gather.7.cloned.1.call-start = ((), (), s32[]{:S(2)}) async-start(), calls=%async_computation.5 | async-start | bytes 11943936 | tf_op jit(solution)/shard_map/all_gather | solution.py:986
  23.2 26.7 %copy-start = (bf16[4,256,768]{2,1,0:T(8,128)(2,1)S(1)}, bf16[4,256,768]{2,1,0:T(8,128)(2,1)}, u32[]{:S(2)}) copy-start(bf16[4,256,768]{2,1,0:T(8,128)(2,1)} %x_ref.2) | copy-start | bytes 4718596
  23.3 3.0 copy-start.2
  23.3 16.2 %collective-permute-start.8 = (bf16[352,768]{1,0:T(8,128)(2,1)S(1)}, bf16[352,768]{1,0:T(8,128)(2,1)S(1)}, u32[]{:S(2)}, u32[]{:S(2)}) collective-permute-start(bf16[352,768]{1,0:T(8,128)(2,1)S(1)} %pad_maximum_fusion.1.refs_1_), channel_id=1, source_target_pairs={{0,24},{8,16},{16,8},{24,0},{1,25},{9,17},{17,9},{25,1},{2,26},{10... | collective-permute-start | bytes 1622024 | tf_op jit(solution)/shard_map/ppermute | solution.py:871
  25.8 23.2 %collective-permute-start.6 = (bf16[352,768]{1,0:T(8,128)(2,1)S(1)}, bf16[352,768]{1,0:T(8,128)(2,1)S(1)}, u32[]{:S(2)}, u32[]{:S(2)}) collective-permute-start(bf16[352,768]{1,0:T(8,128)(2,1)S(1)} %pad_maximum_fusion.1.refs_1_), channel_id=1, source_target_pairs={{0,16},{8,24},{16,0},{24,8},{1,17},{9,25},{17,1},{25,9},{2,18},{10... | collective-permute-start | bytes 1622024 | tf_op jit(solution)/shard_map/ppermute | solution.py:871
  26.3 23.5 %collective-permute-start.4 = (bf16[352,768]{1,0:T(8,128)(2,1)S(1)}, bf16[352,768]{1,0:T(8,128)(2,1)}, u32[]{:S(2)}, u32[]{:S(2)}) collective-permute-start(bf16[352,768]{1,0:T(8,128)(2,1)S(1)} %pad_maximum_fusion.1.refs_1_), channel_id=1, source_target_pairs={{0,8},{8,0},{16,24},{24,16},{1,9},{9,1},{17,25},{25,17},{2,10},{10... | collective-permute-start | bytes 1622024 | tf_op jit(solution)/shard_map/ppermute | solution.py:871
  39.5 9.5 %copy-start.5 = (bf16[352,768]{1,0:T(8,128)(2,1)}, bf16[352,768]{1,0:T(8,128)(2,1)S(1)}, u32[]{:S(2)}) copy-start(bf16[352,768]{1,0:T(8,128)(2,1)S(1)} %collective-permute-done.8.refs_7_) | copy-start | bytes 1622020
  49.0 0.8 copy-start.6
  49.8 208.8 %reduce-scatter.3.cloned.1.call-start = ((), (), s32[]{:S(2)}) async-start(), calls=%async_computation.2 | async-start | bytes 11943936 | tf_op jit(solution)/shard_map/reduce_scatter | solution.py:1007
  49.9 39.3 %collective-permute-start.11 = (bf16[4,256,768]{2,1,0:T(8,128)(2,1)S(1)}, bf16[4,256,768]{2,1,0:T(8,128)(2,1)S(1)}, u32[]{:S(2)}, u32[]{:S(2)}) collective-permute-start(bf16[4,256,768]{2,1,0:T(8,128)(2,1)S(1)} %copy-done), channel_id=1, source_target_pairs={{1,0},{2,1},{3,2},{5,4},{6,5},{7,6},{9,8},{10,9},{11,10},{13,12},{... | collective-permute-start | bytes 4718600 | tf_op jit(solution)/shard_map/ppermute | solution.py:957
  53.2 38.8 %collective-permute-start.10 = (bf16[4,256,768]{2,1,0:T(8,128)(2,1)S(1)}, bf16[4,256,768]{2,1,0:T(8,128)(2,1)}, u32[]{:S(2)}, u32[]{:S(2)}) collective-permute-start(bf16[4,256,768]{2,1,0:T(8,128)(2,1)S(1)} %copy-done), channel_id=1, source_target_pairs={{0,1},{1,2},{2,3},{4,5},{5,6},{6,7},{8,9},{9,10},{10,11},{12,13},{... | collective-permute-start | bytes 4718600 | tf_op jit(solution)/shard_map/ppermute | solution.py:957
  56.4 2.3 collective-permute-start.3
  56.5 3.0 collective-permute-start.9
  57.0 8.2 %collective-permute-start.7 = (bf16[352,768]{1,0:T(8,128)(2,1)}, bf16[352,768]{1,0:T(8,128)(2,1)}, u32[]{:S(2)}, u32[]{:S(2)}) collective-permute-start(bf16[352,768]{1,0:T(8,128)(2,1)} %copy-done.6), channel_id=1, source_target_pairs={{0,4},{4,0},{1,5},{5,1},{2,6},{6,2},{3,7},{7,3},{8,12},{12,8},{9,1... | collective-permute-start | bytes 1622024 | tf_op jit(solution)/shard_map/ppermute | solution.py:893
  58.7 6.5 %collective-permute-start.5 = (bf16[352,768]{1,0:T(8,128)(2,1)}, bf16[352,768]{1,0:T(8,128)(2,1)}, u32[]{:S(2)}, u32[]{:S(2)}) collective-permute-start(bf16[352,768]{1,0:T(8,128)(2,1)} %collective-permute-done.4.refs_3_), channel_id=1, source_target_pairs={{0,4},{4,0},{1,5},{5,1},{2,6},{6,2},{3,7},{7,3},{8,12},{12,8},{9,1... | collective-permute-start | bytes 1622024 | tf_op jit(solution)/shard_map/ppermute | solution.py:893
  59.5 27.9 %collective-permute-start.12 = (bf16[4,1,768]{2,1,0:T(2,128)(2,1)S(1)}, bf16[4,1,768]{2,1,0:T(2,128)(2,1)S(1)}, u32[]{:S(2)}, u32[]{:S(2)}) collective-permute-start(bf16[4,1,768]{2,1,0:T(2,128)(2,1)S(1)} %slice.149), channel_id=1, source_target_pairs={{2,0},{3,1},{6,4},{7,5},{10,8},{11,9},{14,12},{15,13},{18,16},{19,... | collective-permute-start | bytes 18440 | tf_op jit(solution)/shard_map/ppermute | solution.py:957
  87.4 4.7 %copy-start.9 = (bf16[4,1,768]{2,1,0:T(2,128)(2,1)}, bf16[4,1,768]{2,1,0:T(2,128)(2,1)S(1)}, u32[]{:S(2)}) copy-start(bf16[4,1,768]{2,1,0:T(2,128)(2,1)S(1)} %collective-permute-done.12.far_ref) | copy-start | bytes 18436
  89.2 2.9 copy-start.1
  173.8 126.1 %reduce-scatter.5.cloned.1.call-start = ((), (), s32[]{:S(2)}) async-start(), calls=%async_computation.3 | async-start | bytes 1658880 | tf_op jit(solution)/shard_map/reduce_scatter | solution.py:1046
  202.9 20.4 %copy-start.8 = (f32[4,16,768]{2,1,0:T(8,128)S(1)}, f32[4,16,768]{2,1,0:T(8,128)}, u32[]{:S(2)}) copy-start(f32[4,16,768]{2,1,0:T(8,128)} %get-tuple-element.82) | copy-start | bytes 589828
  202.9 20.4 %copy-start.10 = (f32[4,1,768]{2,1,0:T(1,128)S(1)}, f32[4,1,768]{2,1,0:T(1,128)}, u32[]{:S(2)}) copy-start(f32[4,1,768]{2,1,0:T(1,128)} %get-tuple-element.84) | copy-start | bytes 36868
  202.9 20.6 %copy-start.11 = (f32[8,768]{1,0:T(8,128)S(1)}, f32[8,768]{1,0:T(8,128)}, u32[]{:S(2)}) copy-start(f32[8,768]{1,0:T(8,128)} %get-tuple-element.83) | copy-start | bytes 73732
  217.4 41.0 %collective-permute-start.14 = (bf16[4,256,768]{2,1,0:T(8,128)(2,1)}, bf16[4,256,768]{2,1,0:T(8,128)(2,1)S(1)}, u32[]{:S(2)}, u32[]{:S(2)}) collective-permute-start(bf16[4,256,768]{2,1,0:T(8,128)(2,1)} %get-tuple-element.88), channel_id=1, source_target_pairs={{1,0},{2,1},{3,2},{5,4},{6,5},{7,6},{9,8},{10,9},{11,10},{13,12},{... | collective-permute-start | bytes 4718600 | tf_op jit(solution)/shard_map/ppermute | solution.py:957
  220.9 37.7 %collective-permute-start.15 = (bf16[4,256,768]{2,1,0:T(8,128)(2,1)}, bf16[4,256,768]{2,1,0:T(8,128)(2,1)S(1)}, u32[]{:S(2)}, u32[]{:S(2)}) collective-permute-start(bf16[4,256,768]{2,1,0:T(8,128)(2,1)} %get-tuple-element.89), channel_id=1, source_target_pairs={{0,1},{1,2},{2,3},{4,5},{5,6},{6,7},{8,9},{9,10},{10,11},{12,13},{... | collective-permute-start | bytes 4718600 | tf_op jit(solution)/shard_map/ppermute | solution.py:957
  223.5 34.8 %collective-permute-start.13 = (bf16[4,1,768]{2,1,0:T(2,128)(2,1)}, bf16[4,1,768]{2,1,0:T(2,128)(2,1)S(1)}, u32[]{:S(2)}, u32[]{:S(2)}) collective-permute-start(bf16[4,1,768]{2,1,0:T(2,128)(2,1)} %get-tuple-element.87), channel_id=1, source_target_pairs={{0,2},{1,3},{4,6},{5,7},{8,10},{9,11},{12,14},{13,15},{16,18},{17,... | collective-permute-start | bytes 18440 | tf_op jit(solution)/shard_map/ppermute | solution.py:957
  258.3 1.2 copy-start.3
  258.6 1.4 copy-start.4
  258.6 4.6 %collective-permute-start.16 = (bf16[4,352,768]{2,1,0:T(8,128)(2,1)}, bf16[4,352,768]{2,1,0:T(8,128)(2,1)}, u32[]{:S(2)}, u32[]{:S(2)}) collective-permute-start(bf16[4,352,768]{2,1,0:T(8,128)(2,1)} %get-tuple-element.95), channel_id=1, source_target_pairs={{0,4},{4,0},{1,5},{5,1},{2,6},{6,2},{3,7},{7,3},{8,12},{12,8},{9,1... | collective-permute-start | bytes 6488072 | tf_op jit(solution)/shard_map/ppermute | solution.py:1047
  266.9 16.4 %collective-permute-start.19 = (bf16[352,768]{1,0:T(8,128)(2,1)}, bf16[352,768]{1,0:T(8,128)(2,1)}, u32[]{:S(2)}, u32[]{:S(2)}) collective-permute-start(bf16[352,768]{1,0:T(8,128)(2,1)} %get-tuple-element.103), channel_id=1, source_target_pairs={{0,24},{8,16},{16,8},{24,0},{1,25},{9,17},{17,9},{25,1},{2,26},{10... | collective-permute-start | bytes 1622024 | tf_op jit(solution)/shard_map/ppermute | solution.py:915
  267.2 26.7 %collective-permute-start.18 = (bf16[352,768]{1,0:T(8,128)(2,1)S(1)}, bf16[352,768]{1,0:T(8,128)(2,1)}, u32[]{:S(2)}, u32[]{:S(2)}) collective-permute-start(bf16[352,768]{1,0:T(8,128)(2,1)S(1)} %get-tuple-element.104), channel_id=1, source_target_pairs={{0,16},{8,24},{16,0},{24,8},{1,17},{9,25},{17,1},{25,9},{2,18},{10... | collective-permute-start | bytes 1622024 | tf_op jit(solution)/shard_map/ppermute | solution.py:915
  269.9 24.0 %collective-permute-start.17 = (bf16[352,768]{1,0:T(8,128)(2,1)S(1)}, bf16[352,768]{1,0:T(8,128)(2,1)}, u32[]{:S(2)}, u32[]{:S(2)}) collective-permute-start(bf16[352,768]{1,0:T(8,128)(2,1)S(1)} %get-tuple-element.105), channel_id=1, source_target_pairs={{0,8},{8,0},{16,24},{24,16},{1,9},{9,1},{17,25},{25,17},{2,10},{10... | collective-permute-start | bytes 1622024 | tf_op jit(solution)/shard_map/ppermute | solution.py:915
  295.7 9.0 %collective-permute-start.22 = (bf16[88,768]{1,0:T(8,128)(2,1)S(1)}, bf16[88,768]{1,0:T(8,128)(2,1)S(1)}, u32[]{:S(2)}, u32[]{:S(2)}) collective-permute-start(bf16[88,768]{1,0:T(8,128)(2,1)S(1)} %get-tuple-element.106), channel_id=1, source_target_pairs={{0,3},{1,2},{2,1},{3,0},{4,7},{5,6},{6,5},{7,4},{8,11},{9,10},{10,... | collective-permute-start | bytes 405512 | tf_op jit(solution)/shard_map/ppermute | solution.py:915
  295.8 9.1 %collective-permute-start.20 = (bf16[88,768]{1,0:T(8,128)(2,1)S(1)}, bf16[88,768]{1,0:T(8,128)(2,1)S(1)}, u32[]{:S(2)}, u32[]{:S(2)}) collective-permute-start(bf16[88,768]{1,0:T(8,128)(2,1)S(1)} %get-tuple-element.107), channel_id=1, source_target_pairs={{0,1},{1,0},{2,3},{3,2},{4,5},{5,4},{6,7},{7,6},{8,9},{9,8},{10,11... | collective-permute-start | bytes 405512 | tf_op jit(solution)/shard_map/ppermute | solution.py:915
  297.6 11.6 %collective-permute-start.21 = (bf16[88,768]{1,0:T(8,128)(2,1)S(1)}, bf16[88,768]{1,0:T(8,128)(2,1)S(1)}, u32[]{:S(2)}, u32[]{:S(2)}) collective-permute-start(bf16[88,768]{1,0:T(8,128)(2,1)S(1)} %get-tuple-element.108), channel_id=1, source_target_pairs={{0,2},{1,3},{2,0},{3,1},{4,6},{5,7},{6,4},{7,5},{8,10},{9,11},{10,... | collective-permute-start | bytes 405512 | tf_op jit(solution)/shard_map/ppermute | solution.py:915
Sparse Core Ops, SparseCore 0:
  14.6 33.4 all-gather.4
  50.0 65.7 all-gather.6
  173.9 81.5 reduce-scatter.2
  258.8 30.8 reduce-scatter.4

commit v3 on v2

--- a/solution.py
+++ b/solution.py
@@ -674,37 +674,69 @@
     )(own_keys, own_values, left, right, far, weights)
 
 
-def input_grad_kernel(
-    dq_ref, dk_ref, dv_ref, first_ref, w_ref, left_ref, right_ref, far_ref, own_ref
-):
-    right = HALO + dq_ref.shape[1]
-    grad = nt(dk_ref[0], square_of(w_ref, 1)) + nt(dv_ref[0], square_of(w_ref, 2))
+def halo_grad_kernel(dk_ref, dv_ref, wk_ref, wv_ref, left_ref, right_ref, far_ref, dk, dv):
+    right = dk_ref.shape[1] - HALO - PAD
+    width = dk_ref.shape[2]
+    for rows, ref in ((dk, dk_ref), (dv, dv_ref)):
+        rows[:HALO, :] = ref[0, :HALO, :]
+        rows[HALO:, :] = ref[0, right:, :]
+    grad = nt(dk[...], wk_ref[...].reshape(width, width)) + nt(
+        dv[...], wv_ref[...].reshape(width, width)
+    )
     left_ref[0] = grad[:HALO].astype(BF16)
-    right_ref[0] = grad[right : right + HALO].astype(BF16)
-    far_ref[0] = grad[right + HALO : right + HALO + 1].astype(BF16)
-    own_ref[0] = grad[HALO:right] + nt(dq_ref[0], square_of(w_ref, 0)) + first_ref[0]
-
-
-def input_grads(d_queries, d_keys, d_values, d_first, weights):
+    right_ref[0] = grad[HALO : 2 * HALO].astype(BF16)
+    far_ref[0] = grad[2 * HALO : 2 * HALO + 1].astype(BF16)
+
+
+def halo_grads(d_keys, d_values, weights):
+    seqs, ext, width = d_keys.shape
+    units = weights.shape[0]
+
+    def part(place):
+        return pl.BlockSpec(
+            (units, width // units, width),
+            lambda s: (0, place, 0),
+            pipeline_mode=pl.Buffered(buffer_count=1),
+        )
+
+    rows = (HALO, HALO, 1)
+    kept = pltpu.VMEM((2 * HALO + PAD, width), BF16)
+    return pl.pallas_call(
+        halo_grad_kernel,
+        grid=(seqs,),
+        in_specs=[by_seq(ext, width), by_seq(ext, width), part(1), part(2)],
+        out_specs=[by_seq(n, width) for n in rows],
+        out_shape=[jax.ShapeDtypeStruct((seqs, n, width), BF16) for n in rows],
+        scratch_shapes=[kept, kept],
+        compiler_params=pltpu.CompilerParams(vmem_limit_bytes=60 << 20),
+        cost_estimate=QUICK,
+        name="halo_grads",
+    )(d_keys, d_values, weights, weights)
+
+
+def own_grad_kernel(dq_ref, dk_ref, dv_ref, first_ref, w_ref, own_ref):
+    grad = nt(dq_ref[0], square_of(w_ref, 0)) + nt(dk_ref[0], square_of(w_ref, 1))
+    own_ref[0] = grad + nt(dv_ref[0], square_of(w_ref, 2)) + first_ref[0]
+
+
+def own_grads(d_queries, d_keys, d_values, d_first, weights):
     seqs, group, width = d_queries.shape
-    ext = d_keys.shape[1]
-    rows = (HALO, HALO)
+    middle = pl.BlockSpec((1, group, width), lambda s: (s, HALO // group, 0))
     return pl.pallas_call(
-        input_grad_kernel,
+        own_grad_kernel,
         grid=(seqs,),
         in_specs=[
             by_seq(group, width),
-            by_seq(ext, width),
-            by_seq(ext, width),
+            middle,
+            middle,
             by_seq(group, width),
             resident(*weights.shape),
         ],
-        out_specs=[by_seq(n, width) for n in rows + (1, group)],
-        out_shape=[jax.ShapeDtypeStruct((seqs, n, width), BF16) for n in rows + (1,)]
-        + [jax.ShapeDtypeStruct((seqs, group, width), F32)],
+        out_specs=by_seq(group, width),
+        out_shape=jax.ShapeDtypeStruct((seqs, group, width), F32),
         compiler_params=pltpu.CompilerParams(vmem_limit_bytes=60 << 20),
         cost_estimate=QUICK,
-        name="input_grads",
+        name="own_grads",
     )(d_queries, d_keys, d_values, d_first, weights)
 
 
@@ -1020,9 +1052,7 @@
         seqs,
         (),
     )
-    left, right, far, own = input_grads(
-        d_queries, d_keys, d_values, d_first.reshape(seqs, group, width), early
-    )
+    left, right, far = halo_grads(d_keys, d_values, early)
     from_far = shift(far, 2)
     back = (from_far, shift(left, -1), shift(right, 1))
 
@@ -1035,14 +1065,20 @@
     d_vectors = d_vectors.reshape(units, seq_count * SMALL, width)
     mine, other = weight_grads(
         core.astype(jnp.int32).reshape(1),
-        after(tokens, own),
+        after(tokens, left),
         *came,
         d_queries,
         d_keys,
         d_values,
         d_vectors,
     )
-    (mine, other), back, late_sum = after(((mine, other), back, late_sum))
+    own = own_grads(
+        d_queries,
+        *after((d_keys, d_values), mine),
+        d_first.reshape(seqs, group, width),
+        early,
+    )
+    (mine, other), back, late_sum, own = after(((mine, other), back, late_sum, own))
     late_sum = lax.psum_scatter(late_sum, "seq", scatter_dimension=0, tiled=True).astype(F32)
     swapped = lax.ppermute(other, "core", [(0, 1), (1, 0)])
     early_sum = (mine.astype(F32) + swapped.astype(F32)).astype(BF16)

time: 322 us -> 320 us (level)
  waiting for transfers between devices: 80 us -> 74.8 us
  Pallas kernels: 157 us -> 161 us
    ppermute x6, waiting for transfers between devices: 27.4 us -> 17.1 us  [shift(): return lax.ppermute(value, 'seq', pairs)]
    pallas_call x1 -> x2, Pallas kernels: 14.4 us -> 19.3 us  [the longest x1 9.73 us: halo_grads(): pl.pallas_call(halo_grad_kernel, grid=(seqs,), in_specs=[by_seq(ext, widt...]
  transfers between devices with their start and end apart: 27 -> 27, of which waited for: 15 -> 15; matrix products, arithmetic and copies ran while one was open for 9% -> 8% of each run, Pallas kernels for 32% -> 34%
where the time goes in v3:
time: 320 us; the launch traced here: 316 us
  Pallas kernels  161 us (50%)
  waiting for transfers between devices  74.8 us (23%)
  starting transfers between devices  35.1 us (11%)
  local copies, waits for them, and re-layouts  18.2 us (6%)
  between operations  14.4 us (4%)
  other arithmetic  11.7 us (4%)
    pallas_call x1, Pallas kernels, feed_forward(): pl.pallas_call(functools.partial(ffn_kernel, panels), grid=(2 * panels,),...  53.9 us
    pallas_call x1, Pallas kernels, attention_backward(): pl.pallas_call(kernel, grid=(count,), in_specs=attention_specs(ext, group...  29.1 us
    ppermute x6, waiting for transfers between devices, exchange_sum(): lax.ppermute(pick(pieces, met(me)[0]), axis, pairs)  25.6 us
    ppermute x3, waiting for transfers between devices, gather_yx(): pieces.append((lax.ppermute(column, 'yx', pairs), met(me)[1]))  22.1 us
    ppermute x6, starting transfers between devices, shift(): return lax.ppermute(value, 'seq', pairs)  19.3 us
    ppermute x6, waiting for transfers between devices, shift(): return lax.ppermute(value, 'seq', pairs)  17.1 us
    pallas_call x1, Pallas kernels, attention_forward(): pl.pallas_call(attn_fwd_kernel, grid=(seqs,), in_specs=attention_specs(ex...  16.6 us
    pallas_call x1, Pallas kernels, weight_grads(): pl.pallas_call(weight_grad_kernel, grid=(seqs,), in_specs=[pl.BlockSpec(m...  16.2 us
  transfers between devices with their start and end apart: 27, of which 15 were waited for; matrix products, arithmetic and copies ran while one was open for 8% of the time, Pallas kernels for 34%

profile of v3, /device:TPU:16, one launch (start us, length us, event | category | flops | bytes accessed | tf_op | source)
XLA Modules:
  0.0 315.6 jit_solution(6569355533635719217)
XLA Ops:
  7.2 1.5 stack.76
  9.2 3.5 %collective-permute-start.1 = (bf16[88,768]{1,0:T(8,128)(2,1)}, bf16[88,768]{1,0:T(8,128)(2,1)S(1)}, u32[]{:S(2)}, u32[]{:S(2)}) collective-permute-start(bf16[88,768]{1,0:T(8,128)(2,1)} %stack.76), channel_id=1, source_target_pairs={{0,2},{1,3},{2,0},{3,1},{4,6},{5,7},{6,4},{7,5},{8,10},{9,11},{10,... | collective-permute-start | bytes 405512 | tf_op jit(solution)/shard_map/ppermute | solution.py:891
  12.7 1.8 pack.1
  14.6 0.8 select_reduce_fusion
  17.2 0.9 abs_compare_fusion.1
  18.9 1.4 pad_maximum_fusion.bias_ref.refs_5_
  20.2 1.0 collective-permute-done.2
  21.3 1.8 broadcast_in_dim.87.same_ref.refs_4_
  23.3 2.5 collective-permute-start.8
  26.3 0.5 collective-permute-start.4
  26.8 12.7 %collective-permute-done.8.refs_7_ = bf16[352,768]{1,0:T(8,128)(2,1)S(1)} collective-permute-done((bf16[352,768]{1,0:T(8,128)(2,1)S(1)}, bf16[352,768]{1,0:T(8,128)(2,1)S(1)}, u32[]{:S(2)}, u32[]{:S(2)}) %collective-permute-start.8) | collective-permute-done | bytes 540704 | tf_op jit(solution)/shard_map/ppermute | solution.py:903
  39.5 9.5 %collective-permute-done.6.refs_5_ = bf16[352,768]{1,0:T(8,128)(2,1)S(1)} collective-permute-done((bf16[352,768]{1,0:T(8,128)(2,1)S(1)}, bf16[352,768]{1,0:T(8,128)(2,1)S(1)}, u32[]{:S(2)}, u32[]{:S(2)}) %collective-permute-start.6) | collective-permute-done | bytes 540704 | tf_op jit(solution)/shard_map/ppermute | solution.py:903
  49.0 0.8 copy-done.7
  49.9 3.3 %collective-permute-start.11 = (bf16[4,256,768]{2,1,0:T(8,128)(2,1)S(1)}, bf16[4,256,768]{2,1,0:T(8,128)(2,1)S(1)}, u32[]{:S(2)}, u32[]{:S(2)}) collective-permute-start(bf16[4,256,768]{2,1,0:T(8,128)(2,1)S(1)} %copy-done), channel_id=1, source_target_pairs={{1,0},{2,1},{3,2},{5,4},{6,5},{7,6},{9,8},{10,9},{11,10},{13,12},{... | collective-permute-start | bytes 4718600 | tf_op jit(solution)/shard_map/ppermute | solution.py:989
  53.2 3.2 %collective-permute-start.10 = (bf16[4,256,768]{2,1,0:T(8,128)(2,1)S(1)}, bf16[4,256,768]{2,1,0:T(8,128)(2,1)}, u32[]{:S(2)}, u32[]{:S(2)}) collective-permute-start(bf16[4,256,768]{2,1,0:T(8,128)(2,1)S(1)} %copy-done), channel_id=1, source_target_pairs={{0,1},{1,2},{2,3},{4,5},{5,6},{6,7},{8,9},{9,10},{10,11},{12,13},{... | collective-permute-start | bytes 4718600 | tf_op jit(solution)/shard_map/ppermute | solution.py:989
  57.0 1.7 collective-permute-done.3.refs_2_
  58.9 0.6 stack.67.refs_0_
  59.5 5.7 %collective-permute-start.12 = (bf16[4,1,768]{2,1,0:T(2,128)(2,1)S(1)}, bf16[4,1,768]{2,1,0:T(2,128)(2,1)S(1)}, u32[]{:S(2)}, u32[]{:S(2)}) collective-permute-start(bf16[4,1,768]{2,1,0:T(2,128)(2,1)S(1)} %slice.149), channel_id=1, source_target_pairs={{2,0},{3,1},{6,4},{7,5},{10,8},{11,9},{14,12},{15,13},{18,16},{19,... | collective-permute-start | bytes 18440 | tf_op jit(solution)/shard_map/ppermute | solution.py:989
  65.2 4.3 %assemble.1.w_ref.wk_ref.wv_ref = bf16[8,352,768]{2,1,0:T(8,128)(2,1)} custom-call(s32[8]{0:T(128)} %stack.67.refs_0_, bf16[352,768]{1,0:T(8,128)(2,1)} %copy-done.5, bf16[352,768]{1,0:T(8,128)(2,1)} %collective-permute-done.3.refs_2_, bf16[352,768]{1,0:T(8,128)(2,1)} %collective-permute-done.4.refs_3_, bf16[352,768]{1,0:T(8,128)(2,1)} %collective-permute-done.5.refs_4_, ...), custom_call_target="tpu_custom_call" | custom-call | flops 1048576 | bytes 1048576 | tf_op jit(solution)/shard_map/assemble/pallas_call | solution.py:927
  69.4 1.2 slice.180
  70.8 0.7 reshape.289.bias_ref
  71.7 0.6 pad.25.w_ref.refs_3_
  72.3 0.6 pad.26.small_ref
  73.0 7.6 %project_own.1 = (bf16[4,256,768]{2,1,0:T(8,128)(2,1)}, bf16[4,256,768]{2,1,0:T(8,128)(2,1)}, bf16[4,256,768]{2,1,0:T(8,128)(2,1)}) custom-call(bf16[4,256,768]{2,1,0:T(8,128)(2,1)} %x_ref.2, bf16[8,352,768]{2,1,0:T(8,128)(2,1)} %assemble.1.w_ref.wk_ref.wv_ref), custom_call_target="tpu_custom_call" | custom-call | flops 1048576 | bytes 1048576 | tf_op jit(solution)/shard_map/project_own/pallas_call | solution.py:648
  80.5 6.9 %collective-permute-done.12.far_ref = bf16[4,1,768]{2,1,0:T(2,128)(2,1)S(1)} collective-permute-done((bf16[4,1,768]{2,1,0:T(2,128)(2,1)S(1)}, bf16[4,1,768]{2,1,0:T(2,128)(2,1)S(1)}, u32[]{:S(2)}, u32[]{:S(2)}) %collective-permute-start.12) | collective-permute-done | bytes 6176 | tf_op jit(solution)/shard_map/ppermute | solution.py:989
  87.4 1.8 collective-permute-done.11.right_ref
  89.2 2.9 collective-permute-done.10.left_ref
  92.0 11.2 %project_halos.1 = (bf16[4,784,768]{2,1,0:T(8,128)(2,1)}, bf16[4,784,768]{2,1,0:T(8,128)(2,1)}) custom-call(bf16[4,256,768]{2,1,0:T(8,128)(2,1)} %get-tuple-element.66.own_k_ref, bf16[4,256,768]{2,1,0:T(8,128)(2,1)} %get-tuple-element.67.own_v_ref, bf16[4,256,768]{2,1,0:T(8,128)(2,1)} %collective-permute-done.10.left_ref, bf16[4,256,768]{2,1,0:T(8,128)(2,1)} %copy-done.3, ...), custom_call_target="tpu_custom_call" | custom-call | flops 1048576 | bytes 1048576 | tf_op jit(solution)/shard_map/project_halos/pallas_call | solution.py:663
  103.3 16.6 %attn_fwd.1 = (bf16[4,256,768]{2,1,0:T(8,128)(2,1)}, f32[4,6,2,256]{3,2,1,0:T(2,128)}) custom-call(bf16[4,256,768]{2,1,0:T(8,128)(2,1)} %get-tuple-element.65.q_ref.refs_0_, bf16[4,784,768]{2,1,0:T(8,128)(2,1)} %get-tuple-element.69.k_ref.refs_1_, bf16[4,784,768]{2,1,0:T(8,128)(2,1)} %get-tuple-element.70.v_ref.refs_2_, f32[16,768]{1,0:T(8,128)} %pad.25.w_ref.refs_3_, ...), custom_call_target="tpu_custom_call" | custom-call | flops 1048576 | bytes 1048576 | tf_op jit(solution)/shard_map/attn_fwd/pallas_call | solution.py:240
  119.9 53.9 %ffn.1 = (bf16[1024,768]{1,0:T(8,128)(2,1)}, f32[1024,768]{1,0:T(8,128)}, bf16[1024,768]{1,0:T(8,128)(2,1)}, f32[8,768]{1,0:T(8,128)}, f32[4,1,768]{2,1,0:T(1,128)}, /*index=5*/bf16[8,4,9,24,768]{4,3,2,1,0:T(8,128)(2,1)}) custom-call(bf16[1024,768]{1,0:T(8,128)(2,1)} %bitcast.99, bf16[1024,768]{1,0:T(8,128)(2,1)} %bitcast.107, bf16[1024,768]{1,0:T(8,128)(2,1)} %bitcast.106, ...), custom_call_target="tpu_custom_call" | custom-call | flops 1048576 | bytes 1048576 | tf_op jit(solution)/shard_map/ffn/pallas_call | solution.py:492
  173.8 29.1 %attn_bwd.1 = (bf16[4,256,768]{2,1,0:T(8,128)(2,1)}, bf16[4,784,768]{2,1,0:T(8,128)(2,1)}, bf16[4,784,768]{2,1,0:T(8,128)(2,1)}, f32[4,16,768]{2,1,0:T(8,128)}) custom-call(bf16[4,256,768]{2,1,0:T(8,128)(2,1)} %get-tuple-element.65.q_ref.refs_0_, bf16[4,784,768]{2,1,0:T(8,128)(2,1)} %get-tuple-element.69.k_ref.refs_1_, ...), custom_call_target="tpu_custom_call" | custom-call | flops 1048576 | bytes 1048576 | tf_op jit(solution)/shard_map/attn_bwd/pallas_call | solution.py:270
  202.9 9.7 %halo_grads.1 = (bf16[4,256,768]{2,1,0:T(8,128)(2,1)}, bf16[4,256,768]{2,1,0:T(8,128)(2,1)}, bf16[4,1,768]{2,1,0:T(2,128)(2,1)}) custom-call(bf16[4,784,768]{2,1,0:T(8,128)(2,1)} %get-tuple-element.91.dk_ref, bf16[4,784,768]{2,1,0:T(8,128)(2,1)} %get-tuple-element.92.dv_ref, bf16[8,352,768]{2,1,0:T(8,128)(2,1)} %assemble.1.w_ref.wk_ref.wv_ref, ...), custom_call_target="tpu_custom_call" | custom-call | flops 1048576 | bytes 1048576 | tf_op jit(solution)/shard_map/halo_grads/pallas_call | solution.py:704
  212.7 2.9 collective-permute-start.15
  215.6 3.0 collective-permute-start.14
  218.9 1.3 collective-permute-start.13
  220.3 1.3 copy.52
  221.7 16.2 %weight_grads.1 = (bf16[4,352,768]{2,1,0:T(8,128)(2,1)}, bf16[4,352,768]{2,1,0:T(8,128)(2,1)}) custom-call(s32[1]{0:T(128)} %bitcast.35.core_ref, bf16[4,256,768]{2,1,0:T(8,128)(2,1)} %x_ref.2, bf16[4,256,768]{2,1,0:T(8,128)(2,1)} %collective-permute-done.10.left_ref, bf16[4,256,768]{2,1,0:T(8,128)(2,1)} %copy-done.3, bf16[4,1,768]{2,1,0:T(2,128)(2,1)} %copy-done.10, ...), custom_call_target="tpu_custom_call" | custom-call | flops 1048576 | bytes 1048576 | tf_op jit(solution)/shard_map/weight_grads/pallas_call | solution.py:809
  237.8 9.5 %own_grads.1 = f32[4,256,768]{2,1,0:T(8,128)} custom-call(bf16[4,256,768]{2,1,0:T(8,128)(2,1)} %get-tuple-element.82.dq_ref, bf16[4,784,768]{2,1,0:T(8,128)(2,1)} %get-tuple-element.91.dk_ref, bf16[4,784,768]{2,1,0:T(8,128)(2,1)} %get-tuple-element.92.dv_ref, f32[4,256,768]{2,1,0:T(8,128)} %bitcast.104, bf16[8,352,768]{2,1,0:T(8,128)(2,1)} %assemble.1.w_ref.wk_ref.wv_ref), custom_call_target="tpu_custom_call" | custom-call | flops 1048576 | bytes 1048576 | tf_op jit(solution)/shard_map/own_grads/pallas_call | solution.py:725
  247.4 4.0 %collective-permute-done.13 = bf16[4,1,768]{2,1,0:T(2,128)(2,1)S(1)} collective-permute-done((bf16[4,1,768]{2,1,0:T(2,128)(2,1)}, bf16[4,1,768]{2,1,0:T(2,128)(2,1)S(1)}, u32[]{:S(2)}, u32[]{:S(2)}) %collective-permute-start.13) | collective-permute-done | bytes 6176 | tf_op jit(solution)/shard_map/ppermute | solution.py:989
  251.3 1.7 collective-permute-done.14
  253.0 2.6 reduce-scatter.3.cloned.1.call-done
  255.6 4.5 %collective-permute-done.16 = bf16[4,352,768]{2,1,0:T(8,128)(2,1)} collective-permute-done((bf16[4,352,768]{2,1,0:T(8,128)(2,1)}, bf16[4,352,768]{2,1,0:T(8,128)(2,1)}, u32[]{:S(2)}, u32[]{:S(2)}) %collective-permute-start.16) | collective-permute-done | bytes 2162720 | tf_op jit(solution)/shard_map/ppermute | solution.py:1083
  260.1 2.1 add_convert_fusion
  262.3 1.2 dynamic-slice_bitcast_fusion
  263.5 0.7 copy-done.2
  264.2 1.4 collective-permute-start.19
  265.7 1.4 collective-permute-start.18
  267.0 0.7 collective-permute-start.17
  267.7 3.5 %add_convert_fusion.1 = bf16[4,256,768]{2,1,0:T(8,128)(2,1)} fusion(bf16[4,256,768]{2,1,0:T(8,128)(2,1)} %collective-permute-done.15, f32[4,256,768]{2,1,0:T(8,128)S(1)} %copy-done.1, bf16[4,256,768]{2,1,0:T(8,128)(2,1)} %collective-permute-done.14, bf16[4,1,768]{2,1,0:T(2,128)(2,1)S(1)} %collective-permute-done.13), kind=kLoop, calls=%fused_computation.1 | loop fusion | flops 5505024 | bytes 7870464 | tf_op jit(solution)/shard_map/convert_element_type | solution.py:1109
  271.2 9.3 %collective-permute-done.19 = bf16[352,768]{1,0:T(8,128)(2,1)} collective-permute-done((bf16[352,768]{1,0:T(8,128)(2,1)}, bf16[352,768]{1,0:T(8,128)(2,1)}, u32[]{:S(2)}, u32[]{:S(2)}) %collective-permute-start.19) | collective-permute-done | bytes 540704 | tf_op jit(solution)/shard_map/ppermute | solution.py:947
  280.6 10.7 %collective-permute-done.18 = bf16[352,768]{1,0:T(8,128)(2,1)} collective-permute-done((bf16[352,768]{1,0:T(8,128)(2,1)}, bf16[352,768]{1,0:T(8,128)(2,1)}, u32[]{:S(2)}, u32[]{:S(2)}) %collective-permute-start.18) | collective-permute-done | bytes 540704 | tf_op jit(solution)/shard_map/ppermute | solution.py:947
  291.3 1.8 fusion.4
  293.3 0.6 collective-permute-start.22
  293.9 1.4 collective-permute-start.20
  295.3 1.9 collective-permute-start.21
  297.2 1.7 fusion.17
  298.9 0.7 copy.57
  299.7 1.4 slice.192
  301.1 1.6 collective-permute-done.22
  302.7 3.9 %collective-permute-done.21 = bf16[88,768]{1,0:T(8,128)(2,1)S(1)} collective-permute-done((bf16[88,768]{1,0:T(8,128)(2,1)S(1)}, bf16[88,768]{1,0:T(8,128)(2,1)S(1)}, u32[]{:S(2)}, u32[]{:S(2)}) %collective-permute-start.21) | collective-permute-done | bytes 135200 | tf_op jit(solution)/shard_map/ppermute | solution.py:947
  306.7 0.5 slice_bitcast_fusion.3
  307.2 0.5 slice_bitcast_fusion
  307.7 0.6 slice.193
  308.3 0.7 fusion.18
  (111 shorter events, 5.5 us)
Async XLA Ops:
  7.2 42.6 %all-gather.5.cloned.1.call-start = ((), (), s32[]{:S(2)}) async-start(), calls=%async_computation.4 | async-start | bytes 1658880 | tf_op jit(solution)/shard_map/all_gather | solution.py:1015
  8.8 12.5 %collective-permute-start.2 = (bf16[88,768]{1,0:T(8,128)(2,1)}, bf16[88,768]{1,0:T(8,128)(2,1)S(1)}, u32[]{:S(2)}, u32[]{:S(2)}) collective-permute-start(bf16[88,768]{1,0:T(8,128)(2,1)} %stack.76), channel_id=1, source_target_pairs={{0,3},{1,2},{2,1},{3,0},{4,7},{5,6},{6,5},{7,4},{8,11},{9,10},{10,... | collective-permute-start | bytes 405512 | tf_op jit(solution)/shard_map/ppermute | solution.py:891
  9.2 12.0 %collective-permute-start.1 = (bf16[88,768]{1,0:T(8,128)(2,1)}, bf16[88,768]{1,0:T(8,128)(2,1)S(1)}, u32[]{:S(2)}, u32[]{:S(2)}) collective-permute-start(bf16[88,768]{1,0:T(8,128)(2,1)} %stack.76), channel_id=1, source_target_pairs={{0,2},{1,3},{2,0},{3,1},{4,6},{5,7},{6,4},{7,5},{8,10},{9,11},{10,... | collective-permute-start | bytes 405512 | tf_op jit(solution)/shard_map/ppermute | solution.py:891
  12.7 8.6 %collective-permute-start = (bf16[88,768]{1,0:T(8,128)(2,1)}, bf16[88,768]{1,0:T(8,128)(2,1)S(1)}, u32[]{:S(2)}, u32[]{:S(2)}) collective-permute-start(bf16[88,768]{1,0:T(8,128)(2,1)} %stack.76), channel_id=1, source_target_pairs={{0,1},{1,0},{2,3},{3,2},{4,5},{5,4},{6,7},{7,6},{8,9},{9,8},{10,11... | collective-permute-start | bytes 405512 | tf_op jit(solution)/shard_map/ppermute | solution.py:891
  14.5 4.4 %copy-start.8 = (bf16[88,768]{1,0:T(8,128)(2,1)S(1)}, bf16[88,768]{1,0:T(8,128)(2,1)}, u32[]{:S(2)}) copy-start(bf16[88,768]{1,0:T(8,128)(2,1)} %stack.76) | copy-start | bytes 405508
  14.5 105.4 %all-gather.7.cloned.1.call-start = ((), (), s32[]{:S(2)}) async-start(), calls=%async_computation.5 | async-start | bytes 11943936 | tf_op jit(solution)/shard_map/all_gather | solution.py:1018
  23.2 26.7 %copy-start = (bf16[4,256,768]{2,1,0:T(8,128)(2,1)S(1)}, bf16[4,256,768]{2,1,0:T(8,128)(2,1)}, u32[]{:S(2)}) copy-start(bf16[4,256,768]{2,1,0:T(8,128)(2,1)} %x_ref.2) | copy-start | bytes 4718596
  23.3 3.0 copy-start.5
  23.3 16.2 %collective-permute-start.8 = (bf16[352,768]{1,0:T(8,128)(2,1)S(1)}, bf16[352,768]{1,0:T(8,128)(2,1)S(1)}, u32[]{:S(2)}, u32[]{:S(2)}) collective-permute-start(bf16[352,768]{1,0:T(8,128)(2,1)S(1)} %pad_maximum_fusion.1.refs_1_), channel_id=1, source_target_pairs={{0,24},{8,16},{16,8},{24,0},{1,25},{9,17},{17,9},{25,1},{2,26},{10... | collective-permute-start | bytes 1622024 | tf_op jit(solution)/shard_map/ppermute | solution.py:903
  25.8 23.2 %collective-permute-start.6 = (bf16[352,768]{1,0:T(8,128)(2,1)S(1)}, bf16[352,768]{1,0:T(8,128)(2,1)S(1)}, u32[]{:S(2)}, u32[]{:S(2)}) collective-permute-start(bf16[352,768]{1,0:T(8,128)(2,1)S(1)} %pad_maximum_fusion.1.refs_1_), channel_id=1, source_target_pairs={{0,16},{8,24},{16,0},{24,8},{1,17},{9,25},{17,1},{25,9},{2,18},{10... | collective-permute-start | bytes 1622024 | tf_op jit(solution)/shard_map/ppermute | solution.py:903
  26.3 23.5 %collective-permute-start.4 = (bf16[352,768]{1,0:T(8,128)(2,1)S(1)}, bf16[352,768]{1,0:T(8,128)(2,1)}, u32[]{:S(2)}, u32[]{:S(2)}) collective-permute-start(bf16[352,768]{1,0:T(8,128)(2,1)S(1)} %pad_maximum_fusion.1.refs_1_), channel_id=1, source_target_pairs={{0,8},{8,0},{16,24},{24,16},{1,9},{9,1},{17,25},{25,17},{2,10},{10... | collective-permute-start | bytes 1622024 | tf_op jit(solution)/shard_map/ppermute | solution.py:903
  39.5 9.5 %copy-start.6 = (bf16[352,768]{1,0:T(8,128)(2,1)}, bf16[352,768]{1,0:T(8,128)(2,1)S(1)}, u32[]{:S(2)}) copy-start(bf16[352,768]{1,0:T(8,128)(2,1)S(1)} %collective-permute-done.8.refs_7_) | copy-start | bytes 1622020
  49.0 0.8 copy-start.7
  49.8 205.7 %reduce-scatter.3.cloned.1.call-start = ((), (), s32[]{:S(2)}) async-start(), calls=%async_computation.2 | async-start | bytes 11943936 | tf_op jit(solution)/shard_map/reduce_scatter | solution.py:1039
  49.9 39.3 %collective-permute-start.11 = (bf16[4,256,768]{2,1,0:T(8,128)(2,1)S(1)}, bf16[4,256,768]{2,1,0:T(8,128)(2,1)S(1)}, u32[]{:S(2)}, u32[]{:S(2)}) collective-permute-start(bf16[4,256,768]{2,1,0:T(8,128)(2,1)S(1)} %copy-done), channel_id=1, source_target_pairs={{1,0},{2,1},{3,2},{5,4},{6,5},{7,6},{9,8},{10,9},{11,10},{13,12},{... | collective-permute-start | bytes 4718600 | tf_op jit(solution)/shard_map/ppermute | solution.py:989
  53.2 38.8 %collective-permute-start.10 = (bf16[4,256,768]{2,1,0:T(8,128)(2,1)S(1)}, bf16[4,256,768]{2,1,0:T(8,128)(2,1)}, u32[]{:S(2)}, u32[]{:S(2)}) collective-permute-start(bf16[4,256,768]{2,1,0:T(8,128)(2,1)S(1)} %copy-done), channel_id=1, source_target_pairs={{0,1},{1,2},{2,3},{4,5},{5,6},{6,7},{8,9},{9,10},{10,11},{12,13},{... | collective-permute-start | bytes 4718600 | tf_op jit(solution)/shard_map/ppermute | solution.py:989
  56.4 2.3 collective-permute-start.3
  56.5 3.0 collective-permute-start.9
  57.0 8.2 %collective-permute-start.7 = (bf16[352,768]{1,0:T(8,128)(2,1)}, bf16[352,768]{1,0:T(8,128)(2,1)}, u32[]{:S(2)}, u32[]{:S(2)}) collective-permute-start(bf16[352,768]{1,0:T(8,128)(2,1)} %copy-done.7), channel_id=1, source_target_pairs={{0,4},{4,0},{1,5},{5,1},{2,6},{6,2},{3,7},{7,3},{8,12},{12,8},{9,1... | collective-permute-start | bytes 1622024 | tf_op jit(solution)/shard_map/ppermute | solution.py:925
  58.7 6.4 %collective-permute-start.5 = (bf16[352,768]{1,0:T(8,128)(2,1)}, bf16[352,768]{1,0:T(8,128)(2,1)}, u32[]{:S(2)}, u32[]{:S(2)}) collective-permute-start(bf16[352,768]{1,0:T(8,128)(2,1)} %collective-permute-done.4.refs_3_), channel_id=1, source_target_pairs={{0,4},{4,0},{1,5},{5,1},{2,6},{6,2},{3,7},{7,3},{8,12},{12,8},{9,1... | collective-permute-start | bytes 1622024 | tf_op jit(solution)/shard_map/ppermute | solution.py:925
  59.5 27.9 %collective-permute-start.12 = (bf16[4,1,768]{2,1,0:T(2,128)(2,1)S(1)}, bf16[4,1,768]{2,1,0:T(2,128)(2,1)S(1)}, u32[]{:S(2)}, u32[]{:S(2)}) collective-permute-start(bf16[4,1,768]{2,1,0:T(2,128)(2,1)S(1)} %slice.149), channel_id=1, source_target_pairs={{2,0},{3,1},{6,4},{7,5},{10,8},{11,9},{14,12},{15,13},{18,16},{19,... | collective-permute-start | bytes 18440 | tf_op jit(solution)/shard_map/ppermute | solution.py:989
  87.4 4.7 %copy-start.10 = (bf16[4,1,768]{2,1,0:T(2,128)(2,1)}, bf16[4,1,768]{2,1,0:T(2,128)(2,1)S(1)}, u32[]{:S(2)}) copy-start(bf16[4,1,768]{2,1,0:T(2,128)(2,1)S(1)} %collective-permute-done.12.far_ref) | copy-start | bytes 18436
  89.2 2.9 copy-start.3
  173.8 123.4 %reduce-scatter.5.cloned.1.call-start = ((), (), s32[]{:S(2)}) async-start(), calls=%async_computation.3 | async-start | bytes 1658880 | tf_op jit(solution)/shard_map/reduce_scatter | solution.py:1082
  202.9 15.6 %copy-start.9 = (f32[4,16,768]{2,1,0:T(8,128)S(1)}, f32[4,16,768]{2,1,0:T(8,128)}, u32[]{:S(2)}) copy-start(f32[4,16,768]{2,1,0:T(8,128)} %get-tuple-element.83) | copy-start | bytes 589828
  202.9 15.6 %copy-start.11 = (f32[4,1,768]{2,1,0:T(1,128)S(1)}, f32[4,1,768]{2,1,0:T(1,128)}, u32[]{:S(2)}) copy-start(f32[4,1,768]{2,1,0:T(1,128)} %get-tuple-element.85) | copy-start | bytes 36868
  202.9 15.8 %copy-start.12 = (f32[8,768]{1,0:T(8,128)S(1)}, f32[8,768]{1,0:T(8,128)}, u32[]{:S(2)}) copy-start(f32[8,768]{1,0:T(8,128)} %get-tuple-element.84) | copy-start | bytes 73732
  212.7 38.6 %collective-permute-start.15 = (bf16[4,256,768]{2,1,0:T(8,128)(2,1)}, bf16[4,256,768]{2,1,0:T(8,128)(2,1)}, u32[]{:S(2)}, u32[]{:S(2)}) collective-permute-start(bf16[4,256,768]{2,1,0:T(8,128)(2,1)} %get-tuple-element.89), channel_id=1, source_target_pairs={{0,1},{1,2},{2,3},{4,5},{5,6},{6,7},{8,9},{9,10},{10,11},{12,13},{... | collective-permute-start | bytes 4718600 | tf_op jit(solution)/shard_map/ppermute | solution.py:989
  215.6 37.4 %collective-permute-start.14 = (bf16[4,256,768]{2,1,0:T(8,128)(2,1)}, bf16[4,256,768]{2,1,0:T(8,128)(2,1)}, u32[]{:S(2)}, u32[]{:S(2)}) collective-permute-start(bf16[4,256,768]{2,1,0:T(8,128)(2,1)} %get-tuple-element.80), channel_id=1, source_target_pairs={{1,0},{2,1},{3,2},{5,4},{6,5},{7,6},{9,8},{10,9},{11,10},{13,12},{... | collective-permute-start | bytes 4718600 | tf_op jit(solution)/shard_map/ppermute | solution.py:989
  218.9 32.4 %collective-permute-start.13 = (bf16[4,1,768]{2,1,0:T(2,128)(2,1)}, bf16[4,1,768]{2,1,0:T(2,128)(2,1)S(1)}, u32[]{:S(2)}, u32[]{:S(2)}) collective-permute-start(bf16[4,1,768]{2,1,0:T(2,128)(2,1)} %get-tuple-element.88), channel_id=1, source_target_pairs={{0,2},{1,3},{4,6},{5,7},{8,10},{9,11},{12,14},{13,15},{16,18},{17,... | collective-permute-start | bytes 18440 | tf_op jit(solution)/shard_map/ppermute | solution.py:989
  237.8 22.3 %copy-start.4 = (bf16[4,352,768]{2,1,0:T(8,128)(2,1)S(1)}, bf16[4,352,768]{2,1,0:T(8,128)(2,1)}, u32[]{:S(2)}) copy-start(bf16[4,352,768]{2,1,0:T(8,128)(2,1)} %get-tuple-element.98) | copy-start | bytes 6488068
  255.5 4.6 %collective-permute-start.16 = (bf16[4,352,768]{2,1,0:T(8,128)(2,1)}, bf16[4,352,768]{2,1,0:T(8,128)(2,1)}, u32[]{:S(2)}, u32[]{:S(2)}) collective-permute-start(bf16[4,352,768]{2,1,0:T(8,128)(2,1)} %get-tuple-element.99), channel_id=1, source_target_pairs={{0,4},{4,0},{1,5},{5,1},{2,6},{6,2},{3,7},{7,3},{8,12},{12,8},{9,1... | collective-permute-start | bytes 6488072 | tf_op jit(solution)/shard_map/ppermute | solution.py:1083
  262.3 2.0 copy-start.2
  262.3 5.4 %copy-start.1 = (f32[4,256,768]{2,1,0:T(8,128)S(1)}, f32[4,256,768]{2,1,0:T(8,128)}, u32[]{:S(2)}) copy-start(f32[4,256,768]{2,1,0:T(8,128)} %own_grads.1) | copy-start | bytes 9437188
  264.2 16.4 %collective-permute-start.19 = (bf16[352,768]{1,0:T(8,128)(2,1)}, bf16[352,768]{1,0:T(8,128)(2,1)}, u32[]{:S(2)}, u32[]{:S(2)}) collective-permute-start(bf16[352,768]{1,0:T(8,128)(2,1)} %get-tuple-element.107), channel_id=1, source_target_pairs={{0,24},{8,16},{16,8},{24,0},{1,25},{9,17},{17,9},{25,1},{2,26},{10... | collective-permute-start | bytes 1622024 | tf_op jit(solution)/shard_map/ppermute | solution.py:947
  265.7 25.7 %collective-permute-start.18 = (bf16[352,768]{1,0:T(8,128)(2,1)}, bf16[352,768]{1,0:T(8,128)(2,1)}, u32[]{:S(2)}, u32[]{:S(2)}) collective-permute-start(bf16[352,768]{1,0:T(8,128)(2,1)} %get-tuple-element.108), channel_id=1, source_target_pairs={{0,16},{8,24},{16,0},{24,8},{1,17},{9,25},{17,1},{25,9},{2,18},{10... | collective-permute-start | bytes 1622024 | tf_op jit(solution)/shard_map/ppermute | solution.py:947
  267.0 24.3 %collective-permute-start.17 = (bf16[352,768]{1,0:T(8,128)(2,1)}, bf16[352,768]{1,0:T(8,128)(2,1)}, u32[]{:S(2)}, u32[]{:S(2)}) collective-permute-start(bf16[352,768]{1,0:T(8,128)(2,1)} %get-tuple-element.109), channel_id=1, source_target_pairs={{0,8},{8,0},{16,24},{24,16},{1,9},{9,1},{17,25},{25,17},{2,10},{10... | collective-permute-start | bytes 1622024 | tf_op jit(solution)/shard_map/ppermute | solution.py:947
  293.3 9.4 %collective-permute-start.22 = (bf16[88,768]{1,0:T(8,128)(2,1)S(1)}, bf16[88,768]{1,0:T(8,128)(2,1)S(1)}, u32[]{:S(2)}, u32[]{:S(2)}) collective-permute-start(bf16[88,768]{1,0:T(8,128)(2,1)S(1)} %get-tuple-element.110), channel_id=1, source_target_pairs={{0,3},{1,2},{2,1},{3,0},{4,7},{5,6},{6,5},{7,4},{8,11},{9,10},{10,... | collective-permute-start | bytes 405512 | tf_op jit(solution)/shard_map/ppermute | solution.py:947
  293.9 8.8 %collective-permute-start.20 = (bf16[88,768]{1,0:T(8,128)(2,1)S(1)}, bf16[88,768]{1,0:T(8,128)(2,1)S(1)}, u32[]{:S(2)}, u32[]{:S(2)}) collective-permute-start(bf16[88,768]{1,0:T(8,128)(2,1)S(1)} %get-tuple-element.111), channel_id=1, source_target_pairs={{0,1},{1,0},{2,3},{3,2},{4,5},{5,4},{6,7},{7,6},{8,9},{9,8},{10,11... | collective-permute-start | bytes 405512 | tf_op jit(solution)/shard_map/ppermute | solution.py:947
  295.3 11.3 %collective-permute-start.21 = (bf16[88,768]{1,0:T(8,128)(2,1)S(1)}, bf16[88,768]{1,0:T(8,128)(2,1)S(1)}, u32[]{:S(2)}, u32[]{:S(2)}) collective-permute-start(bf16[88,768]{1,0:T(8,128)(2,1)S(1)} %get-tuple-element.112), channel_id=1, source_target_pairs={{0,2},{1,3},{2,0},{3,1},{4,6},{5,7},{6,4},{7,5},{8,10},{9,11},{10,... | collective-permute-start | bytes 405512 | tf_op jit(solution)/shard_map/ppermute | solution.py:947
Sparse Core Ops, SparseCore 0:
  14.6 33.4 all-gather.4
  50.0 65.7 all-gather.6
  173.9 81.5 reduce-scatter.2
  257.7 30.4 reduce-scatter.4

commit v4 on v3

--- a/solution.py
+++ b/solution.py
@@ -335,6 +335,8 @@
     hidden,
     slope,
     d_inner,
+    cot,
+    y_all,
     d_in_stage,
     d_out_stage,
     in_sems,
@@ -365,6 +367,13 @@
     gain_one, shift_one, outer_bias, gain_two, shift_two = (
         small_ref[i : i + 1, :] for i in range(5)
     )
+
+    piece = cot_ref.shape[0]
+    piece_rows = pl.ds(pl.multiple_of(lax.rem(step, panels) * piece, piece), piece)
+
+    @pl.when(step < panels)
+    def _():
+        cot[piece_rows, :] = cot_ref[...]
 
     @pl.when(step == 0)
     def _():
@@ -402,8 +411,8 @@
             d_gain, d_shift, d_bias = carry
             rows = pl.ds(pl.multiple_of(i * ROWS, ROWS), ROWS)
             normed, inv = normalize(acc[rows, :])
-            y_ref[rows, :] = (normed * gain_two + shift_two).astype(BF16)
-            grad = cot_ref[rows, :].astype(F32)
+            y_all[rows, :] = (normed * gain_two + shift_two).astype(BF16)
+            grad = cot[rows, :].astype(F32)
             d_second = normalize_back(grad * gain_two, normed, inv)
             low_grad = d_second.astype(BF16)
             acc[rows, :] = d_second
@@ -424,6 +433,7 @@
     @pl.when(step >= panels)
     def _():
         panel = step - panels
+        y_ref[...] = y_all[piece_rows, :]
 
         def body(i, d_bias):
             rows = pl.ds(pl.multiple_of(i * ROWS, ROWS), ROWS)
@@ -495,7 +505,7 @@
         in_specs=[
             whole(tokens, width),
             whole(tokens, width),
-            whole(tokens, width),
+            pl.BlockSpec((tokens // panels, width), lambda j: (jnp.minimum(j, panels - 1), 0)),
             pl.BlockSpec(
                 (units, column, 1, share, width),
                 lambda j: (0, 0, 2 * panels, 0, 0),
@@ -512,7 +522,7 @@
             ),
         ],
         out_specs=[
-            whole(tokens, width),
+            pl.BlockSpec((tokens // panels, width), lambda j: (later(j), 0)),
             whole(tokens, width),
             whole(tokens, width),
             whole(8, width),
@@ -534,6 +544,8 @@
             pltpu.VMEM((panels, tokens, panel), BF16),
             pltpu.VMEM((panels, tokens, panel), F32),
             pltpu.VMEM((tokens, panel), BF16),
+            pltpu.VMEM((tokens, width), BF16),
+            pltpu.VMEM((tokens, width), BF16),
             pltpu.VMEM((2, units, column, share, width), BF16),
             pltpu.VMEM((2, units // panels, column, panels, share, width), BF16),
             pltpu.SemaphoreType.DMA((2,)),
@@ -616,15 +628,15 @@
 
 
 def project_halos_kernel(
-    own_k_ref, own_v_ref, left_ref, right_ref, far_ref, w_ref, k_ref, v_ref, halos
+    own_k_ref, own_v_ref, left_ref, right_ref, far_ref, wk_ref, wv_ref, k_ref, v_ref, halos
 ):
     group, width = own_k_ref.shape[1:]
     right = HALO + group
     halos[:HALO, :] = left_ref[0]
     halos[HALO : 2 * HALO, :] = right_ref[0]
     halos[2 * HALO :, :] = padded(far_ref)
-    for place, own_ref, ref in ((1, own_k_ref, k_ref), (2, own_v_ref, v_ref)):
-        rows = nn(halos[...], square_of(w_ref, place)).astype(BF16)
+    for w_ref, own_ref, ref in ((wk_ref, own_k_ref, k_ref), (wv_ref, own_v_ref, v_ref)):
+        rows = nn(halos[...], w_ref[...].reshape(width, width)).astype(BF16)
         ref[0, :HALO, :] = rows[:HALO]
         ref[0, HALO:right, :] = own_ref[0]
         ref[0, right:, :] = rows[HALO:]
@@ -640,6 +652,15 @@
 def resident(*shape):
     return pl.BlockSpec(
         shape, lambda s: (0,) * len(shape), pipeline_mode=pl.Buffered(buffer_count=1)
+    )
+
+
+def one_of(weights, place):
+    units, _, width = weights.shape
+    return pl.BlockSpec(
+        (units, width // units, width),
+        lambda s: (0, place, 0),
+        pipeline_mode=pl.Buffered(buffer_count=1),
     )
 
 
@@ -664,14 +685,15 @@
         project_halos_kernel,
         grid=(seqs,),
         in_specs=[by_seq(group, width)] * 2
-        + [by_seq(HALO, width), by_seq(HALO, width), by_seq(1, width), resident(*weights.shape)],
+        + [by_seq(HALO, width), by_seq(HALO, width), by_seq(1, width)]
+        + [one_of(weights, 1), one_of(weights, 2)],
         out_specs=[by_seq(ext, width)] * 2,
         out_shape=[jax.ShapeDtypeStruct((seqs, ext, width), BF16)] * 2,
         scratch_shapes=[pltpu.VMEM((2 * HALO + PAD, width), BF16)],
         compiler_params=pltpu.CompilerParams(vmem_limit_bytes=60 << 20),
         cost_estimate=QUICK,
         name="project_halos",
-    )(own_keys, own_values, left, right, far, weights)
+    )(own_keys, own_values, left, right, far, weights, weights)
 
 
 def halo_grad_kernel(dk_ref, dv_ref, wk_ref, wv_ref, left_ref, right_ref, far_ref, dk, dv):
@@ -690,21 +712,12 @@
 
 def halo_grads(d_keys, d_values, weights):
     seqs, ext, width = d_keys.shape
-    units = weights.shape[0]
-
-    def part(place):
-        return pl.BlockSpec(
-            (units, width // units, width),
-            lambda s: (0, place, 0),
-            pipeline_mode=pl.Buffered(buffer_count=1),
-        )
-
     rows = (HALO, HALO, 1)
     kept = pltpu.VMEM((2 * HALO + PAD, width), BF16)
     return pl.pallas_call(
         halo_grad_kernel,
         grid=(seqs,),
-        in_specs=[by_seq(ext, width), by_seq(ext, width), part(1), part(2)],
+        in_specs=[by_seq(ext, width), by_seq(ext, width), one_of(weights, 1), one_of(weights, 2)],
         out_specs=[by_seq(n, width) for n in rows],
         out_shape=[jax.ShapeDtypeStruct((seqs, n, width), BF16) for n in rows],
         scratch_shapes=[kept, kept],
@@ -795,9 +808,10 @@
             at = slice(place * part, (place + 1) * part)
             mine_ref[:, at, :] = mine.astype(BF16)
             other_ref[:, at, :] = other.astype(BF16)
-        mine, other = split_cores(small_ref[...], core)
-        mine_ref[:, 3 * part :, :] = mine.astype(BF16)
-        other_ref[:, 3 * part :, :] = other.astype(BF16)
+        used = small_ref.shape[2]
+        for ref, half in zip((mine_ref, other_ref), split_cores(small_ref[...], core)):
+            ref[:, 3 * part :, :used] = half.astype(BF16)
+            ref[:, 3 * part :, used:] = jnp.zeros(half.shape[:2] + (width - used,), BF16)
 
 
 def weight_grads(core, x, left, right, far, d_queries, d_keys, d_values, small):
@@ -1059,10 +1073,10 @@
     d_taps = jnp.sum(d_taps, axis=0)[:10]
     d_vectors = jnp.concatenate((d_taps, d_small[:5]), axis=0)
     d_vectors = d_vectors.reshape(SMALL - 1, parts, share).transpose(1, 0, 2)
-    d_vectors = jnp.pad(d_vectors, ((0, 0), (0, 0), (0, width - share)))
-    d_bias = jnp.pad(d_bias.reshape(parts, 1, -1), ((0, 0), (0, 0), (0, width - ff // parts)))
-    d_vectors = jnp.concatenate((d_vectors, d_bias), axis=1).astype(BF16)
-    d_vectors = d_vectors.reshape(units, seq_count * SMALL, width)
+    d_vectors = jnp.pad(d_vectors, ((0, 0), (0, 0), (0, LANES - share)))
+    d_bias = jnp.pad(d_bias.reshape(parts, 1, -1), ((0, 0), (0, 0), (0, LANES - ff // parts)))
+    d_vectors = jnp.concatenate((d_vectors, d_bias), axis=1)
+    d_vectors = d_vectors.reshape(units, seq_count * SMALL, LANES)
     mine, other = weight_grads(
         core.astype(jnp.int32).reshape(1),
         after(tokens, left),

time: 320 us -> 318 us (level)
  transfers between devices with their start and end apart: 27 -> 27, of which waited for: 15 -> 16; matrix products, arithmetic and copies ran while one was open for 8% -> 8% of each run, Pallas kernels for 34% -> 33%
where the time goes in v4:
time: 318 us; the launch traced here: 314 us
  Pallas kernels  160 us (50%)
  waiting for transfers between devices  75 us (24%)
  starting transfers between devices  35.1 us (11%)
  local copies, waits for them, and re-layouts  17.7 us (6%)
  between operations  14.4 us (5%)
  other arithmetic  11.7 us (4%)
    pallas_call x1, Pallas kernels, feed_forward(): pl.pallas_call(functools.partial(ffn_kernel, panels), grid=(2 * panels,),...  53.6 us
    pallas_call x1, Pallas kernels, attention_backward(): pl.pallas_call(kernel, grid=(count,), in_specs=attention_specs(ext, group...  29.1 us
    ppermute x6, waiting for transfers between devices, exchange_sum(): lax.ppermute(pick(pieces, met(me)[0]), axis, pairs)  25.6 us
    ppermute x3, waiting for transfers between devices, gather_yx(): pieces.append((lax.ppermute(column, 'yx', pairs), met(me)[1]))  22.1 us
    ppermute x6, starting transfers between devices, shift(): return lax.ppermute(value, 'seq', pairs)  19.3 us
    ppermute x6, waiting for transfers between devices, shift(): return lax.ppermute(value, 'seq', pairs)  17.3 us
    pallas_call x1, Pallas kernels, attention_forward(): pl.pallas_call(attn_fwd_kernel, grid=(seqs,), in_specs=attention_specs(ex...  16.6 us
    pallas_call x1, Pallas kernels, weight_grads(): pl.pallas_call(weight_grad_kernel, grid=(seqs,), in_specs=[pl.BlockSpec(m...  16 us
  transfers between devices with their start and end apart: 27, of which 16 were waited for; matrix products, arithmetic and copies ran while one was open for 8% of the time, Pallas kernels for 33%

profile of v4, /device:TPU:16, one launch (start us, length us, event | category | flops | bytes accessed | tf_op | source)
XLA Modules:
  0.0 314.1 jit_solution(1766676709427626902)
XLA Ops:
  7.2 1.5 stack.76
  9.2 3.5 %collective-permute-start.1 = (bf16[88,768]{1,0:T(8,128)(2,1)}, bf16[88,768]{1,0:T(8,128)(2,1)S(1)}, u32[]{:S(2)}, u32[]{:S(2)}) collective-permute-start(bf16[88,768]{1,0:T(8,128)(2,1)} %stack.76), channel_id=1, source_target_pairs={{0,2},{1,3},{2,0},{3,1},{4,6},{5,7},{6,4},{7,5},{8,10},{9,11},{10,... | collective-permute-start | bytes 405512 | tf_op jit(solution)/shard_map/ppermute | solution.py:905
  12.7 1.8 pack.1
  14.6 0.8 select_reduce_fusion
  17.2 0.9 abs_compare_fusion.1
  18.9 1.4 pad_maximum_fusion.bias_ref.refs_5_
  20.2 1.0 collective-permute-done.2
  21.3 1.8 broadcast_in_dim.87.same_ref.refs_4_
  23.3 2.5 collective-permute-start.8
  26.3 0.5 collective-permute-start.4
  26.8 12.7 %collective-permute-done.8.refs_7_ = bf16[352,768]{1,0:T(8,128)(2,1)S(1)} collective-permute-done((bf16[352,768]{1,0:T(8,128)(2,1)S(1)}, bf16[352,768]{1,0:T(8,128)(2,1)S(1)}, u32[]{:S(2)}, u32[]{:S(2)}) %collective-permute-start.8) | collective-permute-done | bytes 540704 | tf_op jit(solution)/shard_map/ppermute | solution.py:917
  39.5 9.5 %collective-permute-done.6.refs_5_ = bf16[352,768]{1,0:T(8,128)(2,1)S(1)} collective-permute-done((bf16[352,768]{1,0:T(8,128)(2,1)S(1)}, bf16[352,768]{1,0:T(8,128)(2,1)S(1)}, u32[]{:S(2)}, u32[]{:S(2)}) %collective-permute-start.6) | collective-permute-done | bytes 540704 | tf_op jit(solution)/shard_map/ppermute | solution.py:917
  49.0 0.8 copy-done.7
  49.9 3.3 %collective-permute-start.11 = (bf16[4,256,768]{2,1,0:T(8,128)(2,1)S(1)}, bf16[4,256,768]{2,1,0:T(8,128)(2,1)S(1)}, u32[]{:S(2)}, u32[]{:S(2)}) collective-permute-start(bf16[4,256,768]{2,1,0:T(8,128)(2,1)S(1)} %copy-done), channel_id=1, source_target_pairs={{1,0},{2,1},{3,2},{5,4},{6,5},{7,6},{9,8},{10,9},{11,10},{13,12},{... | collective-permute-start | bytes 4718600 | tf_op jit(solution)/shard_map/ppermute | solution.py:1003
  53.2 3.2 %collective-permute-start.10 = (bf16[4,256,768]{2,1,0:T(8,128)(2,1)S(1)}, bf16[4,256,768]{2,1,0:T(8,128)(2,1)}, u32[]{:S(2)}, u32[]{:S(2)}) collective-permute-start(bf16[4,256,768]{2,1,0:T(8,128)(2,1)S(1)} %copy-done), channel_id=1, source_target_pairs={{0,1},{1,2},{2,3},{4,5},{5,6},{6,7},{8,9},{9,10},{10,11},{12,13},{... | collective-permute-start | bytes 4718600 | tf_op jit(solution)/shard_map/ppermute | solution.py:1003
  57.0 1.7 collective-permute-done.3.refs_2_
  58.9 0.6 stack.67.refs_0_
  59.5 5.7 %collective-permute-start.12 = (bf16[4,1,768]{2,1,0:T(2,128)(2,1)S(1)}, bf16[4,1,768]{2,1,0:T(2,128)(2,1)S(1)}, u32[]{:S(2)}, u32[]{:S(2)}) collective-permute-start(bf16[4,1,768]{2,1,0:T(2,128)(2,1)S(1)} %slice.147), channel_id=1, source_target_pairs={{2,0},{3,1},{6,4},{7,5},{10,8},{11,9},{14,12},{15,13},{18,16},{19,... | collective-permute-start | bytes 18440 | tf_op jit(solution)/shard_map/ppermute | solution.py:1003
  65.2 4.3 %assemble.1.w_ref.wk_ref.wv_ref = bf16[8,352,768]{2,1,0:T(8,128)(2,1)} custom-call(s32[8]{0:T(128)} %stack.67.refs_0_, bf16[352,768]{1,0:T(8,128)(2,1)} %copy-done.5, bf16[352,768]{1,0:T(8,128)(2,1)} %collective-permute-done.3.refs_2_, bf16[352,768]{1,0:T(8,128)(2,1)} %collective-permute-done.4.refs_3_, bf16[352,768]{1,0:T(8,128)(2,1)} %collective-permute-done.5.refs_4_, ...), custom_call_target="tpu_custom_call" | custom-call | flops 1048576 | bytes 1048576 | tf_op jit(solution)/shard_map/assemble/pallas_call | solution.py:941
  69.4 1.2 slice.178
  70.8 0.7 reshape.288.bias_ref
  71.7 0.6 pad.23.w_ref.refs_3_
  72.3 0.6 pad.24.small_ref
  73.0 7.6 %project_own.1 = (bf16[4,256,768]{2,1,0:T(8,128)(2,1)}, bf16[4,256,768]{2,1,0:T(8,128)(2,1)}, bf16[4,256,768]{2,1,0:T(8,128)(2,1)}) custom-call(bf16[4,256,768]{2,1,0:T(8,128)(2,1)} %x_ref.2, bf16[8,352,768]{2,1,0:T(8,128)(2,1)} %assemble.1.w_ref.wk_ref.wv_ref), custom_call_target="tpu_custom_call" | custom-call | flops 1048576 | bytes 1048576 | tf_op jit(solution)/shard_map/project_own/pallas_call | solution.py:669
  80.5 6.9 %collective-permute-done.12.far_ref = bf16[4,1,768]{2,1,0:T(2,128)(2,1)S(1)} collective-permute-done((bf16[4,1,768]{2,1,0:T(2,128)(2,1)S(1)}, bf16[4,1,768]{2,1,0:T(2,128)(2,1)S(1)}, u32[]{:S(2)}, u32[]{:S(2)}) %collective-permute-start.12) | collective-permute-done | bytes 6176 | tf_op jit(solution)/shard_map/ppermute | solution.py:1003
  87.4 1.8 collective-permute-done.11.right_ref
  89.2 2.9 collective-permute-done.10.left_ref
  92.0 10.3 %project_halos.1 = (bf16[4,784,768]{2,1,0:T(8,128)(2,1)}, bf16[4,784,768]{2,1,0:T(8,128)(2,1)}) custom-call(bf16[4,256,768]{2,1,0:T(8,128)(2,1)} %get-tuple-element.66.own_k_ref, bf16[4,256,768]{2,1,0:T(8,128)(2,1)} %get-tuple-element.67.own_v_ref, bf16[4,256,768]{2,1,0:T(8,128)(2,1)} %collective-permute-done.10.left_ref, bf16[4,256,768]{2,1,0:T(8,128)(2,1)} %copy-done.3, ...), custom_call_target="tpu_custom_call" | custom-call | flops 1048576 | bytes 1048576 | tf_op jit(solution)/shard_map/project_halos/pallas_call | solution.py:684
  102.3 16.6 %attn_fwd.1 = (bf16[4,256,768]{2,1,0:T(8,128)(2,1)}, f32[4,6,2,256]{3,2,1,0:T(2,128)}) custom-call(bf16[4,256,768]{2,1,0:T(8,128)(2,1)} %get-tuple-element.65.q_ref.refs_0_, bf16[4,784,768]{2,1,0:T(8,128)(2,1)} %get-tuple-element.69.k_ref.refs_1_, bf16[4,784,768]{2,1,0:T(8,128)(2,1)} %get-tuple-element.70.v_ref.refs_2_, f32[16,768]{1,0:T(8,128)} %pad.23.w_ref.refs_3_, ...), custom_call_target="tpu_custom_call" | custom-call | flops 1048576 | bytes 1048576 | tf_op jit(solution)/shard_map/attn_fwd/pallas_call | solution.py:240
  118.9 53.6 %ffn.1 = (bf16[1024,768]{1,0:T(8,128)(2,1)}, f32[1024,768]{1,0:T(8,128)}, bf16[1024,768]{1,0:T(8,128)(2,1)}, f32[8,768]{1,0:T(8,128)}, f32[4,1,768]{2,1,0:T(1,128)}, /*index=5*/bf16[8,4,9,24,768]{4,3,2,1,0:T(8,128)(2,1)}) custom-call(bf16[1024,768]{1,0:T(8,128)(2,1)} %bitcast.100, bf16[1024,768]{1,0:T(8,128)(2,1)} %bitcast.107, bf16[1024,768]{1,0:T(8,128)(2,1)} %bitcast.106, ...), custom_call_target="tpu_custom_call" | custom-call | flops 1048576 | bytes 1048576 | tf_op jit(solution)/shard_map/ffn/pallas_call | solution.py:502
  172.6 29.1 %attn_bwd.1 = (bf16[4,256,768]{2,1,0:T(8,128)(2,1)}, bf16[4,784,768]{2,1,0:T(8,128)(2,1)}, bf16[4,784,768]{2,1,0:T(8,128)(2,1)}, f32[4,16,768]{2,1,0:T(8,128)}) custom-call(bf16[4,256,768]{2,1,0:T(8,128)(2,1)} %get-tuple-element.65.q_ref.refs_0_, bf16[4,784,768]{2,1,0:T(8,128)(2,1)} %get-tuple-element.69.k_ref.refs_1_, ...), custom_call_target="tpu_custom_call" | custom-call | flops 1048576 | bytes 1048576 | tf_op jit(solution)/shard_map/attn_bwd/pallas_call | solution.py:270
  201.7 9.7 %halo_grads.1 = (bf16[4,256,768]{2,1,0:T(8,128)(2,1)}, bf16[4,256,768]{2,1,0:T(8,128)(2,1)}, bf16[4,1,768]{2,1,0:T(2,128)(2,1)}) custom-call(bf16[4,784,768]{2,1,0:T(8,128)(2,1)} %get-tuple-element.91.dk_ref, bf16[4,784,768]{2,1,0:T(8,128)(2,1)} %get-tuple-element.92.dv_ref, bf16[8,352,768]{2,1,0:T(8,128)(2,1)} %assemble.1.w_ref.wk_ref.wv_ref, ...), custom_call_target="tpu_custom_call" | custom-call | flops 1048576 | bytes 1048576 | tf_op jit(solution)/shard_map/halo_grads/pallas_call | solution.py:717
  211.3 2.7 collective-permute-start.15
  214.1 3.1 collective-permute-start.14
  217.6 1.3 collective-permute-start.13
  218.9 0.9 copy.52
  219.7 16.0 %weight_grads.1 = (bf16[4,352,768]{2,1,0:T(8,128)(2,1)}, bf16[4,352,768]{2,1,0:T(8,128)(2,1)}) custom-call(s32[1]{0:T(128)} %bitcast.35.core_ref, bf16[4,256,768]{2,1,0:T(8,128)(2,1)} %x_ref.2, bf16[4,256,768]{2,1,0:T(8,128)(2,1)} %collective-permute-done.10.left_ref, bf16[4,256,768]{2,1,0:T(8,128)(2,1)} %copy-done.3, bf16[4,1,768]{2,1,0:T(2,128)(2,1)} %copy-done.10, ...), custom_call_target="tpu_custom_call" | custom-call | flops 1048576 | bytes 1048576 | tf_op jit(solution)/shard_map/weight_grads/pallas_call | solution.py:823
  235.7 10.0 %own_grads.1 = f32[4,256,768]{2,1,0:T(8,128)} custom-call(bf16[4,256,768]{2,1,0:T(8,128)(2,1)} %get-tuple-element.82.dq_ref, bf16[4,784,768]{2,1,0:T(8,128)(2,1)} %get-tuple-element.91.dk_ref, bf16[4,784,768]{2,1,0:T(8,128)(2,1)} %get-tuple-element.92.dv_ref, f32[4,256,768]{2,1,0:T(8,128)} %bitcast.104, bf16[8,352,768]{2,1,0:T(8,128)(2,1)} %assemble.1.w_ref.wk_ref.wv_ref), custom_call_target="tpu_custom_call" | custom-call | flops 1048576 | bytes 1048576 | tf_op jit(solution)/shard_map/own_grads/pallas_call | solution.py:738
  245.8 4.3 %collective-permute-done.13 = bf16[4,1,768]{2,1,0:T(2,128)(2,1)S(1)} collective-permute-done((bf16[4,1,768]{2,1,0:T(2,128)(2,1)}, bf16[4,1,768]{2,1,0:T(2,128)(2,1)S(1)}, u32[]{:S(2)}, u32[]{:S(2)}) %collective-permute-start.13) | collective-permute-done | bytes 6176 | tf_op jit(solution)/shard_map/ppermute | solution.py:1003
  250.1 1.5 collective-permute-done.14
  251.5 2.6 reduce-scatter.3.cloned.1.call-done
  254.2 4.5 %collective-permute-done.16 = bf16[4,352,768]{2,1,0:T(8,128)(2,1)} collective-permute-done((bf16[4,352,768]{2,1,0:T(8,128)(2,1)}, bf16[4,352,768]{2,1,0:T(8,128)(2,1)}, u32[]{:S(2)}, u32[]{:S(2)}) %collective-permute-start.16) | collective-permute-done | bytes 2162720 | tf_op jit(solution)/shard_map/ppermute | solution.py:1097
  258.7 2.1 add_convert_fusion
  260.9 1.2 dynamic-slice_bitcast_fusion
  262.1 0.7 copy-done.2
  262.8 1.5 collective-permute-start.19
  264.3 1.4 collective-permute-start.18
  265.6 0.7 collective-permute-start.17
  266.3 3.5 %add_convert_fusion.1 = bf16[4,256,768]{2,1,0:T(8,128)(2,1)} fusion(bf16[4,256,768]{2,1,0:T(8,128)(2,1)} %collective-permute-done.15, f32[4,256,768]{2,1,0:T(8,128)S(1)} %copy-done.1, bf16[4,256,768]{2,1,0:T(8,128)(2,1)} %collective-permute-done.14, bf16[4,1,768]{2,1,0:T(2,128)(2,1)S(1)} %collective-permute-done.13), kind=kLoop, calls=%fused_computation.1 | loop fusion | flops 5505024 | bytes 7870464 | tf_op jit(solution)/shard_map/convert_element_type | solution.py:1123
  269.8 9.3 %collective-permute-done.19 = bf16[352,768]{1,0:T(8,128)(2,1)} collective-permute-done((bf16[352,768]{1,0:T(8,128)(2,1)}, bf16[352,768]{1,0:T(8,128)(2,1)}, u32[]{:S(2)}, u32[]{:S(2)}) %collective-permute-start.19) | collective-permute-done | bytes 540704 | tf_op jit(solution)/shard_map/ppermute | solution.py:961
  279.2 10.7 %collective-permute-done.18 = bf16[352,768]{1,0:T(8,128)(2,1)} collective-permute-done((bf16[352,768]{1,0:T(8,128)(2,1)}, bf16[352,768]{1,0:T(8,128)(2,1)}, u32[]{:S(2)}, u32[]{:S(2)}) %collective-permute-start.18) | collective-permute-done | bytes 540704 | tf_op jit(solution)/shard_map/ppermute | solution.py:961
  289.9 1.8 fusion.2
  291.9 0.6 collective-permute-start.22
  292.5 1.6 collective-permute-start.20
  294.1 1.7 collective-permute-start.21
  295.8 1.7 fusion.14
  297.5 0.7 copy.57
  298.2 1.4 slice.189
  299.7 1.6 collective-permute-done.22
  301.4 3.8 %collective-permute-done.21 = bf16[88,768]{1,0:T(8,128)(2,1)S(1)} collective-permute-done((bf16[88,768]{1,0:T(8,128)(2,1)S(1)}, bf16[88,768]{1,0:T(8,128)(2,1)S(1)}, u32[]{:S(2)}, u32[]{:S(2)}) %collective-permute-start.21) | collective-permute-done | bytes 135200 | tf_op jit(solution)/shard_map/ppermute | solution.py:961
  305.3 0.5 slice_bitcast_fusion.3
  305.8 0.5 slice_bitcast_fusion
  306.3 0.6 slice.190
  306.9 0.7 fusion.15
  (110 shorter events, 5.6 us)
Async XLA Ops:
  7.2 42.6 %all-gather.5.cloned.1.call-start = ((), (), s32[]{:S(2)}) async-start(), calls=%async_computation.4 | async-start | bytes 1658880 | tf_op jit(solution)/shard_map/all_gather | solution.py:1029
  8.8 12.5 %collective-permute-start.2 = (bf16[88,768]{1,0:T(8,128)(2,1)}, bf16[88,768]{1,0:T(8,128)(2,1)S(1)}, u32[]{:S(2)}, u32[]{:S(2)}) collective-permute-start(bf16[88,768]{1,0:T(8,128)(2,1)} %stack.76), channel_id=1, source_target_pairs={{0,3},{1,2},{2,1},{3,0},{4,7},{5,6},{6,5},{7,4},{8,11},{9,10},{10,... | collective-permute-start | bytes 405512 | tf_op jit(solution)/shard_map/ppermute | solution.py:905
  9.2 12.0 %collective-permute-start.1 = (bf16[88,768]{1,0:T(8,128)(2,1)}, bf16[88,768]{1,0:T(8,128)(2,1)S(1)}, u32[]{:S(2)}, u32[]{:S(2)}) collective-permute-start(bf16[88,768]{1,0:T(8,128)(2,1)} %stack.76), channel_id=1, source_target_pairs={{0,2},{1,3},{2,0},{3,1},{4,6},{5,7},{6,4},{7,5},{8,10},{9,11},{10,... | collective-permute-start | bytes 405512 | tf_op jit(solution)/shard_map/ppermute | solution.py:905
  12.7 8.6 %collective-permute-start = (bf16[88,768]{1,0:T(8,128)(2,1)}, bf16[88,768]{1,0:T(8,128)(2,1)S(1)}, u32[]{:S(2)}, u32[]{:S(2)}) collective-permute-start(bf16[88,768]{1,0:T(8,128)(2,1)} %stack.76), channel_id=1, source_target_pairs={{0,1},{1,0},{2,3},{3,2},{4,5},{5,4},{6,7},{7,6},{8,9},{9,8},{10,11... | collective-permute-start | bytes 405512 | tf_op jit(solution)/shard_map/ppermute | solution.py:905
  14.5 4.4 %copy-start.8 = (bf16[88,768]{1,0:T(8,128)(2,1)S(1)}, bf16[88,768]{1,0:T(8,128)(2,1)}, u32[]{:S(2)}) copy-start(bf16[88,768]{1,0:T(8,128)(2,1)} %stack.76) | copy-start | bytes 405508
  14.5 104.4 %all-gather.7.cloned.1.call-start = ((), (), s32[]{:S(2)}) async-start(), calls=%async_computation.5 | async-start | bytes 11943936 | tf_op jit(solution)/shard_map/all_gather | solution.py:1032
  23.2 26.7 %copy-start = (bf16[4,256,768]{2,1,0:T(8,128)(2,1)S(1)}, bf16[4,256,768]{2,1,0:T(8,128)(2,1)}, u32[]{:S(2)}) copy-start(bf16[4,256,768]{2,1,0:T(8,128)(2,1)} %x_ref.2) | copy-start | bytes 4718596
  23.3 3.0 copy-start.5
  23.3 16.2 %collective-permute-start.8 = (bf16[352,768]{1,0:T(8,128)(2,1)S(1)}, bf16[352,768]{1,0:T(8,128)(2,1)S(1)}, u32[]{:S(2)}, u32[]{:S(2)}) collective-permute-start(bf16[352,768]{1,0:T(8,128)(2,1)S(1)} %pad_maximum_fusion.1.refs_1_), channel_id=1, source_target_pairs={{0,24},{8,16},{16,8},{24,0},{1,25},{9,17},{17,9},{25,1},{2,26},{10... | collective-permute-start | bytes 1622024 | tf_op jit(solution)/shard_map/ppermute | solution.py:917
  25.8 23.2 %collective-permute-start.6 = (bf16[352,768]{1,0:T(8,128)(2,1)S(1)}, bf16[352,768]{1,0:T(8,128)(2,1)S(1)}, u32[]{:S(2)}, u32[]{:S(2)}) collective-permute-start(bf16[352,768]{1,0:T(8,128)(2,1)S(1)} %pad_maximum_fusion.1.refs_1_), channel_id=1, source_target_pairs={{0,16},{8,24},{16,0},{24,8},{1,17},{9,25},{17,1},{25,9},{2,18},{10... | collective-permute-start | bytes 1622024 | tf_op jit(solution)/shard_map/ppermute | solution.py:917
  26.3 23.5 %collective-permute-start.4 = (bf16[352,768]{1,0:T(8,128)(2,1)S(1)}, bf16[352,768]{1,0:T(8,128)(2,1)}, u32[]{:S(2)}, u32[]{:S(2)}) collective-permute-start(bf16[352,768]{1,0:T(8,128)(2,1)S(1)} %pad_maximum_fusion.1.refs_1_), channel_id=1, source_target_pairs={{0,8},{8,0},{16,24},{24,16},{1,9},{9,1},{17,25},{25,17},{2,10},{10... | collective-permute-start | bytes 1622024 | tf_op jit(solution)/shard_map/ppermute | solution.py:917
  39.5 9.5 %copy-start.6 = (bf16[352,768]{1,0:T(8,128)(2,1)}, bf16[352,768]{1,0:T(8,128)(2,1)S(1)}, u32[]{:S(2)}) copy-start(bf16[352,768]{1,0:T(8,128)(2,1)S(1)} %collective-permute-done.8.refs_7_) | copy-start | bytes 1622020
  49.0 0.8 copy-start.7
  49.8 204.3 %reduce-scatter.3.cloned.1.call-start = ((), (), s32[]{:S(2)}) async-start(), calls=%async_computation.2 | async-start | bytes 11943936 | tf_op jit(solution)/shard_map/reduce_scatter | solution.py:1053
  49.9 39.3 %collective-permute-start.11 = (bf16[4,256,768]{2,1,0:T(8,128)(2,1)S(1)}, bf16[4,256,768]{2,1,0:T(8,128)(2,1)S(1)}, u32[]{:S(2)}, u32[]{:S(2)}) collective-permute-start(bf16[4,256,768]{2,1,0:T(8,128)(2,1)S(1)} %copy-done), channel_id=1, source_target_pairs={{1,0},{2,1},{3,2},{5,4},{6,5},{7,6},{9,8},{10,9},{11,10},{13,12},{... | collective-permute-start | bytes 4718600 | tf_op jit(solution)/shard_map/ppermute | solution.py:1003
  53.2 38.8 %collective-permute-start.10 = (bf16[4,256,768]{2,1,0:T(8,128)(2,1)S(1)}, bf16[4,256,768]{2,1,0:T(8,128)(2,1)}, u32[]{:S(2)}, u32[]{:S(2)}) collective-permute-start(bf16[4,256,768]{2,1,0:T(8,128)(2,1)S(1)} %copy-done), channel_id=1, source_target_pairs={{0,1},{1,2},{2,3},{4,5},{5,6},{6,7},{8,9},{9,10},{10,11},{12,13},{... | collective-permute-start | bytes 4718600 | tf_op jit(solution)/shard_map/ppermute | solution.py:1003
  56.4 2.3 collective-permute-start.3
  56.5 3.0 collective-permute-start.9
  57.0 8.2 %collective-permute-start.7 = (bf16[352,768]{1,0:T(8,128)(2,1)}, bf16[352,768]{1,0:T(8,128)(2,1)}, u32[]{:S(2)}, u32[]{:S(2)}) collective-permute-start(bf16[352,768]{1,0:T(8,128)(2,1)} %copy-done.7), channel_id=1, source_target_pairs={{0,4},{4,0},{1,5},{5,1},{2,6},{6,2},{3,7},{7,3},{8,12},{12,8},{9,1... | collective-permute-start | bytes 1622024 | tf_op jit(solution)/shard_map/ppermute | solution.py:939
  58.7 6.4 %collective-permute-start.5 = (bf16[352,768]{1,0:T(8,128)(2,1)}, bf16[352,768]{1,0:T(8,128)(2,1)}, u32[]{:S(2)}, u32[]{:S(2)}) collective-permute-start(bf16[352,768]{1,0:T(8,128)(2,1)} %collective-permute-done.4.refs_3_), channel_id=1, source_target_pairs={{0,4},{4,0},{1,5},{5,1},{2,6},{6,2},{3,7},{7,3},{8,12},{12,8},{9,1... | collective-permute-start | bytes 1622024 | tf_op jit(solution)/shard_map/ppermute | solution.py:939
  59.5 27.9 %collective-permute-start.12 = (bf16[4,1,768]{2,1,0:T(2,128)(2,1)S(1)}, bf16[4,1,768]{2,1,0:T(2,128)(2,1)S(1)}, u32[]{:S(2)}, u32[]{:S(2)}) collective-permute-start(bf16[4,1,768]{2,1,0:T(2,128)(2,1)S(1)} %slice.147), channel_id=1, source_target_pairs={{2,0},{3,1},{6,4},{7,5},{10,8},{11,9},{14,12},{15,13},{18,16},{19,... | collective-permute-start | bytes 18440 | tf_op jit(solution)/shard_map/ppermute | solution.py:1003
  87.4 4.7 %copy-start.10 = (bf16[4,1,768]{2,1,0:T(2,128)(2,1)}, bf16[4,1,768]{2,1,0:T(2,128)(2,1)S(1)}, u32[]{:S(2)}) copy-start(bf16[4,1,768]{2,1,0:T(2,128)(2,1)S(1)} %collective-permute-done.12.far_ref) | copy-start | bytes 18436
  89.2 2.9 copy-start.3
  172.5 123.3 %reduce-scatter.5.cloned.1.call-start = ((), (), s32[]{:S(2)}) async-start(), calls=%async_computation.3 | async-start | bytes 1658880 | tf_op jit(solution)/shard_map/reduce_scatter | solution.py:1096
  201.6 15.6 %copy-start.9 = (f32[4,16,768]{2,1,0:T(8,128)S(1)}, f32[4,16,768]{2,1,0:T(8,128)}, u32[]{:S(2)}) copy-start(f32[4,16,768]{2,1,0:T(8,128)} %get-tuple-element.83) | copy-start | bytes 589828
  201.6 15.6 %copy-start.12 = (f32[4,1,768]{2,1,0:T(1,128)S(1)}, f32[4,1,768]{2,1,0:T(1,128)}, u32[]{:S(2)}) copy-start(f32[4,1,768]{2,1,0:T(1,128)} %get-tuple-element.85) | copy-start | bytes 36868
  201.7 15.7 %copy-start.11 = (f32[8,768]{1,0:T(8,128)S(1)}, f32[8,768]{1,0:T(8,128)}, u32[]{:S(2)}) copy-start(f32[8,768]{1,0:T(8,128)} %get-tuple-element.84) | copy-start | bytes 73732
  211.3 38.7 %collective-permute-start.15 = (bf16[4,256,768]{2,1,0:T(8,128)(2,1)}, bf16[4,256,768]{2,1,0:T(8,128)(2,1)}, u32[]{:S(2)}, u32[]{:S(2)}) collective-permute-start(bf16[4,256,768]{2,1,0:T(8,128)(2,1)} %get-tuple-element.89), channel_id=1, source_target_pairs={{0,1},{1,2},{2,3},{4,5},{5,6},{6,7},{8,9},{9,10},{10,11},{12,13},{... | collective-permute-start | bytes 4718600 | tf_op jit(solution)/shard_map/ppermute | solution.py:1003
  214.1 37.5 %collective-permute-start.14 = (bf16[4,256,768]{2,1,0:T(8,128)(2,1)}, bf16[4,256,768]{2,1,0:T(8,128)(2,1)}, u32[]{:S(2)}, u32[]{:S(2)}) collective-permute-start(bf16[4,256,768]{2,1,0:T(8,128)(2,1)} %get-tuple-element.80), channel_id=1, source_target_pairs={{1,0},{2,1},{3,2},{5,4},{6,5},{7,6},{9,8},{10,9},{11,10},{13,12},{... | collective-permute-start | bytes 4718600 | tf_op jit(solution)/shard_map/ppermute | solution.py:1003
  217.6 32.5 %collective-permute-start.13 = (bf16[4,1,768]{2,1,0:T(2,128)(2,1)}, bf16[4,1,768]{2,1,0:T(2,128)(2,1)S(1)}, u32[]{:S(2)}, u32[]{:S(2)}) collective-permute-start(bf16[4,1,768]{2,1,0:T(2,128)(2,1)} %get-tuple-element.88), channel_id=1, source_target_pairs={{0,2},{1,3},{4,6},{5,7},{8,10},{9,11},{12,14},{13,15},{16,18},{17,... | collective-permute-start | bytes 18440 | tf_op jit(solution)/shard_map/ppermute | solution.py:1003
  235.7 23.0 %copy-start.4 = (bf16[4,352,768]{2,1,0:T(8,128)(2,1)S(1)}, bf16[4,352,768]{2,1,0:T(8,128)(2,1)}, u32[]{:S(2)}) copy-start(bf16[4,352,768]{2,1,0:T(8,128)(2,1)} %get-tuple-element.98) | copy-start | bytes 6488068
  254.1 4.6 %collective-permute-start.16 = (bf16[4,352,768]{2,1,0:T(8,128)(2,1)}, bf16[4,352,768]{2,1,0:T(8,128)(2,1)}, u32[]{:S(2)}, u32[]{:S(2)}) collective-permute-start(bf16[4,352,768]{2,1,0:T(8,128)(2,1)} %get-tuple-element.99), channel_id=1, source_target_pairs={{0,4},{4,0},{1,5},{5,1},{2,6},{6,2},{3,7},{7,3},{8,12},{12,8},{9,1... | collective-permute-start | bytes 6488072 | tf_op jit(solution)/shard_map/ppermute | solution.py:1097
  260.8 2.0 copy-start.2
  260.8 5.4 %copy-start.1 = (f32[4,256,768]{2,1,0:T(8,128)S(1)}, f32[4,256,768]{2,1,0:T(8,128)}, u32[]{:S(2)}) copy-start(f32[4,256,768]{2,1,0:T(8,128)} %own_grads.1) | copy-start | bytes 9437188
  262.8 16.4 %collective-permute-start.19 = (bf16[352,768]{1,0:T(8,128)(2,1)}, bf16[352,768]{1,0:T(8,128)(2,1)}, u32[]{:S(2)}, u32[]{:S(2)}) collective-permute-start(bf16[352,768]{1,0:T(8,128)(2,1)} %get-tuple-element.107), channel_id=1, source_target_pairs={{0,24},{8,16},{16,8},{24,0},{1,25},{9,17},{17,9},{25,1},{2,26},{10... | collective-permute-start | bytes 1622024 | tf_op jit(solution)/shard_map/ppermute | solution.py:961
  264.3 25.7 %collective-permute-start.18 = (bf16[352,768]{1,0:T(8,128)(2,1)}, bf16[352,768]{1,0:T(8,128)(2,1)}, u32[]{:S(2)}, u32[]{:S(2)}) collective-permute-start(bf16[352,768]{1,0:T(8,128)(2,1)} %get-tuple-element.108), channel_id=1, source_target_pairs={{0,16},{8,24},{16,0},{24,8},{1,17},{9,25},{17,1},{25,9},{2,18},{10... | collective-permute-start | bytes 1622024 | tf_op jit(solution)/shard_map/ppermute | solution.py:961
  265.6 24.3 %collective-permute-start.17 = (bf16[352,768]{1,0:T(8,128)(2,1)}, bf16[352,768]{1,0:T(8,128)(2,1)}, u32[]{:S(2)}, u32[]{:S(2)}) collective-permute-start(bf16[352,768]{1,0:T(8,128)(2,1)} %get-tuple-element.109), channel_id=1, source_target_pairs={{0,8},{8,0},{16,24},{24,16},{1,9},{9,1},{17,25},{25,17},{2,10},{10... | collective-permute-start | bytes 1622024 | tf_op jit(solution)/shard_map/ppermute | solution.py:961
  291.9 9.4 %collective-permute-start.22 = (bf16[88,768]{1,0:T(8,128)(2,1)S(1)}, bf16[88,768]{1,0:T(8,128)(2,1)S(1)}, u32[]{:S(2)}, u32[]{:S(2)}) collective-permute-start(bf16[88,768]{1,0:T(8,128)(2,1)S(1)} %get-tuple-element.110), channel_id=1, source_target_pairs={{0,3},{1,2},{2,1},{3,0},{4,7},{5,6},{6,5},{7,4},{8,11},{9,10},{10,... | collective-permute-start | bytes 405512 | tf_op jit(solution)/shard_map/ppermute | solution.py:961
  292.5 8.9 %collective-permute-start.20 = (bf16[88,768]{1,0:T(8,128)(2,1)S(1)}, bf16[88,768]{1,0:T(8,128)(2,1)S(1)}, u32[]{:S(2)}, u32[]{:S(2)}) collective-permute-start(bf16[88,768]{1,0:T(8,128)(2,1)S(1)} %get-tuple-element.111), channel_id=1, source_target_pairs={{0,1},{1,0},{2,3},{3,2},{4,5},{5,4},{6,7},{7,6},{8,9},{9,8},{10,11... | collective-permute-start | bytes 405512 | tf_op jit(solution)/shard_map/ppermute | solution.py:961
  294.1 11.1 %collective-permute-start.21 = (bf16[88,768]{1,0:T(8,128)(2,1)S(1)}, bf16[88,768]{1,0:T(8,128)(2,1)S(1)}, u32[]{:S(2)}, u32[]{:S(2)}) collective-permute-start(bf16[88,768]{1,0:T(8,128)(2,1)S(1)} %get-tuple-element.112), channel_id=1, source_target_pairs={{0,2},{1,3},{2,0},{3,1},{4,6},{5,7},{6,4},{7,5},{8,10},{9,11},{10,... | collective-permute-start | bytes 405512 | tf_op jit(solution)/shard_map/ppermute | solution.py:961
Sparse Core Ops, SparseCore 0:
  14.6 33.4 all-gather.4
  50.0 65.7 all-gather.6
  172.6 81.4 reduce-scatter.2
  256.3 30.4 reduce-scatter.4

commit v5 on v4

--- a/solution.py
+++ b/solution.py
@@ -443,7 +443,8 @@
             acc[rows, :] += nt(grad, square(w_in_ref))
             return d_bias + row_sum(grad.astype(F32))
 
-        d_bias_ref[0] = lax.fori_loop(0, chunks, body, jnp.zeros(d_bias_ref.shape[1:], F32))
+        zero = jnp.zeros(d_bias_ref.shape[1:], F32)
+        d_bias_ref[0] = lax.fori_loop(0, chunks, body, zero, unroll=True)
         slot = lax.rem(panel, 2)
 
         @pl.when(panel >= 2)

time: 318 us -> 317 us (level)
  transfers between devices with their start and end apart: 27 -> 27, of which waited for: 16 -> 16; matrix products, arithmetic and copies ran while one was open for 8% -> 8% of each run, Pallas kernels for 33% -> 34%
where the time goes in v5:
time: 317 us; the launch traced here: 313 us
  Pallas kernels  159 us (50%)
  waiting for transfers between devices  75 us (24%)
  starting transfers between devices  35.4 us (11%)
  local copies, waits for them, and re-layouts  17.7 us (6%)
  between operations  14.4 us (5%)
  other arithmetic  11.7 us (4%)
    pallas_call x1, Pallas kernels, feed_forward(): pl.pallas_call(functools.partial(ffn_kernel, panels), grid=(2 * panels,),...  52.1 us
    pallas_call x1, Pallas kernels, attention_backward(): pl.pallas_call(kernel, grid=(count,), in_specs=attention_specs(ext, group...  28.8 us
    ppermute x6, waiting for transfers between devices, exchange_sum(): lax.ppermute(pick(pieces, met(me)[0]), axis, pairs)  25.6 us
    ppermute x3, waiting for transfers between devices, gather_yx(): pieces.append((lax.ppermute(column, 'yx', pairs), met(me)[1]))  22.1 us
    ppermute x6, starting transfers between devices, shift(): return lax.ppermute(value, 'seq', pairs)  19.3 us
    ppermute x6, waiting for transfers between devices, shift(): return lax.ppermute(value, 'seq', pairs)  17.3 us
    pallas_call x1, Pallas kernels, attention_forward(): pl.pallas_call(attn_fwd_kernel, grid=(seqs,), in_specs=attention_specs(ex...  16.6 us
    pallas_call x1, Pallas kernels, weight_grads(): pl.pallas_call(weight_grad_kernel, grid=(seqs,), in_specs=[pl.BlockSpec(m...  16 us
  transfers between devices with their start and end apart: 27, of which 16 were waited for; matrix products, arithmetic and copies ran while one was open for 8% of the time, Pallas kernels for 34%

profile of v5, /device:TPU:16, one launch (start us, length us, event | category | flops | bytes accessed | tf_op | source)
XLA Modules:
  0.0 312.7 jit_solution(16958537348139375133)
XLA Ops:
  7.2 1.5 stack.76
  9.2 3.5 %collective-permute-start.1 = (bf16[88,768]{1,0:T(8,128)(2,1)}, bf16[88,768]{1,0:T(8,128)(2,1)S(1)}, u32[]{:S(2)}, u32[]{:S(2)}) collective-permute-start(bf16[88,768]{1,0:T(8,128)(2,1)} %stack.76), channel_id=1, source_target_pairs={{0,2},{1,3},{2,0},{3,1},{4,6},{5,7},{6,4},{7,5},{8,10},{9,11},{10,... | collective-permute-start | bytes 405512 | tf_op jit(solution)/shard_map/ppermute | solution.py:906
  12.7 1.8 pack.1
  14.6 0.8 select_reduce_fusion
  17.2 0.9 abs_compare_fusion.1
  18.9 1.4 pad_maximum_fusion.bias_ref.refs_5_
  20.2 1.0 collective-permute-done.2
  21.3 1.8 broadcast_in_dim.87.same_ref.refs_4_
  23.3 2.5 collective-permute-start.8
  26.3 0.5 collective-permute-start.4
  26.8 12.7 %collective-permute-done.8.refs_7_ = bf16[352,768]{1,0:T(8,128)(2,1)S(1)} collective-permute-done((bf16[352,768]{1,0:T(8,128)(2,1)S(1)}, bf16[352,768]{1,0:T(8,128)(2,1)S(1)}, u32[]{:S(2)}, u32[]{:S(2)}) %collective-permute-start.8) | collective-permute-done | bytes 540704 | tf_op jit(solution)/shard_map/ppermute | solution.py:918
  39.5 9.5 %collective-permute-done.6.refs_5_ = bf16[352,768]{1,0:T(8,128)(2,1)S(1)} collective-permute-done((bf16[352,768]{1,0:T(8,128)(2,1)S(1)}, bf16[352,768]{1,0:T(8,128)(2,1)S(1)}, u32[]{:S(2)}, u32[]{:S(2)}) %collective-permute-start.6) | collective-permute-done | bytes 540704 | tf_op jit(solution)/shard_map/ppermute | solution.py:918
  49.0 0.8 copy-done.7
  49.9 3.3 %collective-permute-start.11 = (bf16[4,256,768]{2,1,0:T(8,128)(2,1)S(1)}, bf16[4,256,768]{2,1,0:T(8,128)(2,1)S(1)}, u32[]{:S(2)}, u32[]{:S(2)}) collective-permute-start(bf16[4,256,768]{2,1,0:T(8,128)(2,1)S(1)} %copy-done), channel_id=1, source_target_pairs={{1,0},{2,1},{3,2},{5,4},{6,5},{7,6},{9,8},{10,9},{11,10},{13,12},{... | collective-permute-start | bytes 4718600 | tf_op jit(solution)/shard_map/ppermute | solution.py:1004
  53.2 3.2 %collective-permute-start.10 = (bf16[4,256,768]{2,1,0:T(8,128)(2,1)S(1)}, bf16[4,256,768]{2,1,0:T(8,128)(2,1)}, u32[]{:S(2)}, u32[]{:S(2)}) collective-permute-start(bf16[4,256,768]{2,1,0:T(8,128)(2,1)S(1)} %copy-done), channel_id=1, source_target_pairs={{0,1},{1,2},{2,3},{4,5},{5,6},{6,7},{8,9},{9,10},{10,11},{12,13},{... | collective-permute-start | bytes 4718600 | tf_op jit(solution)/shard_map/ppermute | solution.py:1004
  57.0 1.7 collective-permute-done.3.refs_2_
  58.9 0.6 stack.67.refs_0_
  59.5 5.7 %collective-permute-start.12 = (bf16[4,1,768]{2,1,0:T(2,128)(2,1)S(1)}, bf16[4,1,768]{2,1,0:T(2,128)(2,1)S(1)}, u32[]{:S(2)}, u32[]{:S(2)}) collective-permute-start(bf16[4,1,768]{2,1,0:T(2,128)(2,1)S(1)} %slice.147), channel_id=1, source_target_pairs={{2,0},{3,1},{6,4},{7,5},{10,8},{11,9},{14,12},{15,13},{18,16},{19,... | collective-permute-start | bytes 18440 | tf_op jit(solution)/shard_map/ppermute | solution.py:1004
  65.2 4.3 %assemble.1.w_ref.wk_ref.wv_ref = bf16[8,352,768]{2,1,0:T(8,128)(2,1)} custom-call(s32[8]{0:T(128)} %stack.67.refs_0_, bf16[352,768]{1,0:T(8,128)(2,1)} %copy-done.5, bf16[352,768]{1,0:T(8,128)(2,1)} %collective-permute-done.3.refs_2_, bf16[352,768]{1,0:T(8,128)(2,1)} %collective-permute-done.4.refs_3_, bf16[352,768]{1,0:T(8,128)(2,1)} %collective-permute-done.5.refs_4_, ...), custom_call_target="tpu_custom_call" | custom-call | flops 1048576 | bytes 1048576 | tf_op jit(solution)/shard_map/assemble/pallas_call | solution.py:942
  69.4 1.2 slice.178
  70.8 0.7 reshape.288.bias_ref
  71.7 0.6 pad.23.w_ref.refs_3_
  72.3 0.6 pad.24.small_ref
  73.0 7.6 %project_own.1 = (bf16[4,256,768]{2,1,0:T(8,128)(2,1)}, bf16[4,256,768]{2,1,0:T(8,128)(2,1)}, bf16[4,256,768]{2,1,0:T(8,128)(2,1)}) custom-call(bf16[4,256,768]{2,1,0:T(8,128)(2,1)} %x_ref.2, bf16[8,352,768]{2,1,0:T(8,128)(2,1)} %assemble.1.w_ref.wk_ref.wv_ref), custom_call_target="tpu_custom_call" | custom-call | flops 1048576 | bytes 1048576 | tf_op jit(solution)/shard_map/project_own/pallas_call | solution.py:670
  80.5 6.9 %collective-permute-done.12.far_ref = bf16[4,1,768]{2,1,0:T(2,128)(2,1)S(1)} collective-permute-done((bf16[4,1,768]{2,1,0:T(2,128)(2,1)S(1)}, bf16[4,1,768]{2,1,0:T(2,128)(2,1)S(1)}, u32[]{:S(2)}, u32[]{:S(2)}) %collective-permute-start.12) | collective-permute-done | bytes 6176 | tf_op jit(solution)/shard_map/ppermute | solution.py:1004
  87.4 1.8 collective-permute-done.11.right_ref
  89.2 2.9 collective-permute-done.10.left_ref
  92.0 10.3 %project_halos.1 = (bf16[4,784,768]{2,1,0:T(8,128)(2,1)}, bf16[4,784,768]{2,1,0:T(8,128)(2,1)}) custom-call(bf16[4,256,768]{2,1,0:T(8,128)(2,1)} %get-tuple-element.66.own_k_ref, bf16[4,256,768]{2,1,0:T(8,128)(2,1)} %get-tuple-element.67.own_v_ref, bf16[4,256,768]{2,1,0:T(8,128)(2,1)} %collective-permute-done.10.left_ref, bf16[4,256,768]{2,1,0:T(8,128)(2,1)} %copy-done.3, ...), custom_call_target="tpu_custom_call" | custom-call | flops 1048576 | bytes 1048576 | tf_op jit(solution)/shard_map/project_halos/pallas_call | solution.py:685
  102.3 16.6 %attn_fwd.1 = (bf16[4,256,768]{2,1,0:T(8,128)(2,1)}, f32[4,6,2,256]{3,2,1,0:T(2,128)}) custom-call(bf16[4,256,768]{2,1,0:T(8,128)(2,1)} %get-tuple-element.65.q_ref.refs_0_, bf16[4,784,768]{2,1,0:T(8,128)(2,1)} %get-tuple-element.69.k_ref.refs_1_, bf16[4,784,768]{2,1,0:T(8,128)(2,1)} %get-tuple-element.70.v_ref.refs_2_, f32[16,768]{1,0:T(8,128)} %pad.23.w_ref.refs_3_, ...), custom_call_target="tpu_custom_call" | custom-call | flops 1048576 | bytes 1048576 | tf_op jit(solution)/shard_map/attn_fwd/pallas_call | solution.py:240
  118.9 52.1 %ffn.1 = (bf16[1024,768]{1,0:T(8,128)(2,1)}, f32[1024,768]{1,0:T(8,128)}, bf16[1024,768]{1,0:T(8,128)(2,1)}, f32[8,768]{1,0:T(8,128)}, f32[4,1,768]{2,1,0:T(1,128)}, /*index=5*/bf16[8,4,9,24,768]{4,3,2,1,0:T(8,128)(2,1)}) custom-call(bf16[1024,768]{1,0:T(8,128)(2,1)} %bitcast.100, bf16[1024,768]{1,0:T(8,128)(2,1)} %bitcast.107, bf16[1024,768]{1,0:T(8,128)(2,1)} %bitcast.106, ...), custom_call_target="tpu_custom_call" | custom-call | flops 1048576 | bytes 1048576 | tf_op jit(solution)/shard_map/ffn/pallas_call | solution.py:503
  171.3 28.8 %attn_bwd.1 = (bf16[4,256,768]{2,1,0:T(8,128)(2,1)}, bf16[4,784,768]{2,1,0:T(8,128)(2,1)}, bf16[4,784,768]{2,1,0:T(8,128)(2,1)}, f32[4,16,768]{2,1,0:T(8,128)}) custom-call(bf16[4,256,768]{2,1,0:T(8,128)(2,1)} %get-tuple-element.65.q_ref.refs_0_, bf16[4,784,768]{2,1,0:T(8,128)(2,1)} %get-tuple-element.69.k_ref.refs_1_, ...), custom_call_target="tpu_custom_call" | custom-call | flops 1048576 | bytes 1048576 | tf_op jit(solution)/shard_map/attn_bwd/pallas_call | solution.py:270
  200.2 9.7 %halo_grads.1 = (bf16[4,256,768]{2,1,0:T(8,128)(2,1)}, bf16[4,256,768]{2,1,0:T(8,128)(2,1)}, bf16[4,1,768]{2,1,0:T(2,128)(2,1)}) custom-call(bf16[4,784,768]{2,1,0:T(8,128)(2,1)} %get-tuple-element.91.dk_ref, bf16[4,784,768]{2,1,0:T(8,128)(2,1)} %get-tuple-element.92.dv_ref, bf16[8,352,768]{2,1,0:T(8,128)(2,1)} %assemble.1.w_ref.wk_ref.wv_ref, ...), custom_call_target="tpu_custom_call" | custom-call | flops 1048576 | bytes 1048576 | tf_op jit(solution)/shard_map/halo_grads/pallas_call | solution.py:718
  209.9 2.7 collective-permute-start.15
  212.6 3.1 collective-permute-start.14
  216.1 1.3 collective-permute-start.13
  217.4 0.9 copy.52
  218.3 16.0 %weight_grads.1 = (bf16[4,352,768]{2,1,0:T(8,128)(2,1)}, bf16[4,352,768]{2,1,0:T(8,128)(2,1)}) custom-call(s32[1]{0:T(128)} %bitcast.35.core_ref, bf16[4,256,768]{2,1,0:T(8,128)(2,1)} %x_ref.2, bf16[4,256,768]{2,1,0:T(8,128)(2,1)} %collective-permute-done.10.left_ref, bf16[4,256,768]{2,1,0:T(8,128)(2,1)} %copy-done.3, bf16[4,1,768]{2,1,0:T(2,128)(2,1)} %copy-done.10, ...), custom_call_target="tpu_custom_call" | custom-call | flops 1048576 | bytes 1048576 | tf_op jit(solution)/shard_map/weight_grads/pallas_call | solution.py:824
  234.2 10.0 %own_grads.1 = f32[4,256,768]{2,1,0:T(8,128)} custom-call(bf16[4,256,768]{2,1,0:T(8,128)(2,1)} %get-tuple-element.82.dq_ref, bf16[4,784,768]{2,1,0:T(8,128)(2,1)} %get-tuple-element.91.dk_ref, bf16[4,784,768]{2,1,0:T(8,128)(2,1)} %get-tuple-element.92.dv_ref, f32[4,256,768]{2,1,0:T(8,128)} %bitcast.104, bf16[8,352,768]{2,1,0:T(8,128)(2,1)} %assemble.1.w_ref.wk_ref.wv_ref), custom_call_target="tpu_custom_call" | custom-call | flops 1048576 | bytes 1048576 | tf_op jit(solution)/shard_map/own_grads/pallas_call | solution.py:739
  244.3 4.3 %collective-permute-done.13 = bf16[4,1,768]{2,1,0:T(2,128)(2,1)S(1)} collective-permute-done((bf16[4,1,768]{2,1,0:T(2,128)(2,1)}, bf16[4,1,768]{2,1,0:T(2,128)(2,1)S(1)}, u32[]{:S(2)}, u32[]{:S(2)}) %collective-permute-start.13) | collective-permute-done | bytes 6176 | tf_op jit(solution)/shard_map/ppermute | solution.py:1004
  248.6 1.5 collective-permute-done.14
  250.1 2.6 reduce-scatter.3.cloned.1.call-done
  252.7 4.5 %collective-permute-done.16 = bf16[4,352,768]{2,1,0:T(8,128)(2,1)} collective-permute-done((bf16[4,352,768]{2,1,0:T(8,128)(2,1)}, bf16[4,352,768]{2,1,0:T(8,128)(2,1)}, u32[]{:S(2)}, u32[]{:S(2)}) %collective-permute-start.16) | collective-permute-done | bytes 2162720 | tf_op jit(solution)/shard_map/ppermute | solution.py:1098
  257.3 2.1 add_convert_fusion
  259.4 1.2 dynamic-slice_bitcast_fusion
  260.6 0.7 copy-done.2
  261.3 1.5 collective-permute-start.19
  262.8 1.4 collective-permute-start.18
  264.1 0.7 collective-permute-start.17
  264.8 3.5 %add_convert_fusion.1 = bf16[4,256,768]{2,1,0:T(8,128)(2,1)} fusion(bf16[4,256,768]{2,1,0:T(8,128)(2,1)} %collective-permute-done.15, f32[4,256,768]{2,1,0:T(8,128)S(1)} %copy-done.1, bf16[4,256,768]{2,1,0:T(8,128)(2,1)} %collective-permute-done.14, bf16[4,1,768]{2,1,0:T(2,128)(2,1)S(1)} %collective-permute-done.13), kind=kLoop, calls=%fused_computation.1 | loop fusion | flops 5505024 | bytes 7870464 | tf_op jit(solution)/shard_map/convert_element_type | solution.py:1124
  268.4 9.3 %collective-permute-done.19 = bf16[352,768]{1,0:T(8,128)(2,1)} collective-permute-done((bf16[352,768]{1,0:T(8,128)(2,1)}, bf16[352,768]{1,0:T(8,128)(2,1)}, u32[]{:S(2)}, u32[]{:S(2)}) %collective-permute-start.19) | collective-permute-done | bytes 540704 | tf_op jit(solution)/shard_map/ppermute | solution.py:962
  277.7 10.7 %collective-permute-done.18 = bf16[352,768]{1,0:T(8,128)(2,1)} collective-permute-done((bf16[352,768]{1,0:T(8,128)(2,1)}, bf16[352,768]{1,0:T(8,128)(2,1)}, u32[]{:S(2)}, u32[]{:S(2)}) %collective-permute-start.18) | collective-permute-done | bytes 540704 | tf_op jit(solution)/shard_map/ppermute | solution.py:962
  288.4 1.8 fusion.2
  290.4 0.6 collective-permute-start.22
  291.0 1.6 collective-permute-start.20
  292.6 1.7 collective-permute-start.21
  294.3 1.7 fusion.14
  296.0 0.7 copy.57
  296.8 1.4 slice.189
  298.2 1.6 collective-permute-done.22
  299.9 3.8 %collective-permute-done.21 = bf16[88,768]{1,0:T(8,128)(2,1)S(1)} collective-permute-done((bf16[88,768]{1,0:T(8,128)(2,1)S(1)}, bf16[88,768]{1,0:T(8,128)(2,1)S(1)}, u32[]{:S(2)}, u32[]{:S(2)}) %collective-permute-start.21) | collective-permute-done | bytes 135200 | tf_op jit(solution)/shard_map/ppermute | solution.py:962
  303.8 0.5 slice_bitcast_fusion.3
  304.3 0.5 slice_bitcast_fusion
  304.8 0.6 slice.190
  305.4 0.7 fusion.15
  (110 shorter events, 5.8 us)
Async XLA Ops:
  7.2 42.6 %all-gather.5.cloned.1.call-start = ((), (), s32[]{:S(2)}) async-start(), calls=%async_computation.4 | async-start | bytes 1658880 | tf_op jit(solution)/shard_map/all_gather | solution.py:1030
  8.8 12.5 %collective-permute-start.2 = (bf16[88,768]{1,0:T(8,128)(2,1)}, bf16[88,768]{1,0:T(8,128)(2,1)S(1)}, u32[]{:S(2)}, u32[]{:S(2)}) collective-permute-start(bf16[88,768]{1,0:T(8,128)(2,1)} %stack.76), channel_id=1, source_target_pairs={{0,3},{1,2},{2,1},{3,0},{4,7},{5,6},{6,5},{7,4},{8,11},{9,10},{10,... | collective-permute-start | bytes 405512 | tf_op jit(solution)/shard_map/ppermute | solution.py:906
  9.2 12.0 %collective-permute-start.1 = (bf16[88,768]{1,0:T(8,128)(2,1)}, bf16[88,768]{1,0:T(8,128)(2,1)S(1)}, u32[]{:S(2)}, u32[]{:S(2)}) collective-permute-start(bf16[88,768]{1,0:T(8,128)(2,1)} %stack.76), channel_id=1, source_target_pairs={{0,2},{1,3},{2,0},{3,1},{4,6},{5,7},{6,4},{7,5},{8,10},{9,11},{10,... | collective-permute-start | bytes 405512 | tf_op jit(solution)/shard_map/ppermute | solution.py:906
  12.7 8.6 %collective-permute-start = (bf16[88,768]{1,0:T(8,128)(2,1)}, bf16[88,768]{1,0:T(8,128)(2,1)S(1)}, u32[]{:S(2)}, u32[]{:S(2)}) collective-permute-start(bf16[88,768]{1,0:T(8,128)(2,1)} %stack.76), channel_id=1, source_target_pairs={{0,1},{1,0},{2,3},{3,2},{4,5},{5,4},{6,7},{7,6},{8,9},{9,8},{10,11... | collective-permute-start | bytes 405512 | tf_op jit(solution)/shard_map/ppermute | solution.py:906
  14.5 4.4 %copy-start.8 = (bf16[88,768]{1,0:T(8,128)(2,1)S(1)}, bf16[88,768]{1,0:T(8,128)(2,1)}, u32[]{:S(2)}) copy-start(bf16[88,768]{1,0:T(8,128)(2,1)} %stack.76) | copy-start | bytes 405508
  14.5 104.4 %all-gather.7.cloned.1.call-start = ((), (), s32[]{:S(2)}) async-start(), calls=%async_computation.5 | async-start | bytes 11943936 | tf_op jit(solution)/shard_map/all_gather | solution.py:1033
  23.2 26.7 %copy-start = (bf16[4,256,768]{2,1,0:T(8,128)(2,1)S(1)}, bf16[4,256,768]{2,1,0:T(8,128)(2,1)}, u32[]{:S(2)}) copy-start(bf16[4,256,768]{2,1,0:T(8,128)(2,1)} %x_ref.2) | copy-start | bytes 4718596
  23.3 3.0 copy-start.5
  23.3 16.2 %collective-permute-start.8 = (bf16[352,768]{1,0:T(8,128)(2,1)S(1)}, bf16[352,768]{1,0:T(8,128)(2,1)S(1)}, u32[]{:S(2)}, u32[]{:S(2)}) collective-permute-start(bf16[352,768]{1,0:T(8,128)(2,1)S(1)} %pad_maximum_fusion.1.refs_1_), channel_id=1, source_target_pairs={{0,24},{8,16},{16,8},{24,0},{1,25},{9,17},{17,9},{25,1},{2,26},{10... | collective-permute-start | bytes 1622024 | tf_op jit(solution)/shard_map/ppermute | solution.py:918
  25.8 23.2 %collective-permute-start.6 = (bf16[352,768]{1,0:T(8,128)(2,1)S(1)}, bf16[352,768]{1,0:T(8,128)(2,1)S(1)}, u32[]{:S(2)}, u32[]{:S(2)}) collective-permute-start(bf16[352,768]{1,0:T(8,128)(2,1)S(1)} %pad_maximum_fusion.1.refs_1_), channel_id=1, source_target_pairs={{0,16},{8,24},{16,0},{24,8},{1,17},{9,25},{17,1},{25,9},{2,18},{10... | collective-permute-start | bytes 1622024 | tf_op jit(solution)/shard_map/ppermute | solution.py:918
  26.3 23.5 %collective-permute-start.4 = (bf16[352,768]{1,0:T(8,128)(2,1)S(1)}, bf16[352,768]{1,0:T(8,128)(2,1)}, u32[]{:S(2)}, u32[]{:S(2)}) collective-permute-start(bf16[352,768]{1,0:T(8,128)(2,1)S(1)} %pad_maximum_fusion.1.refs_1_), channel_id=1, source_target_pairs={{0,8},{8,0},{16,24},{24,16},{1,9},{9,1},{17,25},{25,17},{2,10},{10... | collective-permute-start | bytes 1622024 | tf_op jit(solution)/shard_map/ppermute | solution.py:918
  39.5 9.5 %copy-start.6 = (bf16[352,768]{1,0:T(8,128)(2,1)}, bf16[352,768]{1,0:T(8,128)(2,1)S(1)}, u32[]{:S(2)}) copy-start(bf16[352,768]{1,0:T(8,128)(2,1)S(1)} %collective-permute-done.8.refs_7_) | copy-start | bytes 1622020
  49.0 0.8 copy-start.7
  49.8 202.8 %reduce-scatter.3.cloned.1.call-start = ((), (), s32[]{:S(2)}) async-start(), calls=%async_computation.2 | async-start | bytes 11943936 | tf_op jit(solution)/shard_map/reduce_scatter | solution.py:1054
  49.9 39.3 %collective-permute-start.11 = (bf16[4,256,768]{2,1,0:T(8,128)(2,1)S(1)}, bf16[4,256,768]{2,1,0:T(8,128)(2,1)S(1)}, u32[]{:S(2)}, u32[]{:S(2)}) collective-permute-start(bf16[4,256,768]{2,1,0:T(8,128)(2,1)S(1)} %copy-done), channel_id=1, source_target_pairs={{1,0},{2,1},{3,2},{5,4},{6,5},{7,6},{9,8},{10,9},{11,10},{13,12},{... | collective-permute-start | bytes 4718600 | tf_op jit(solution)/shard_map/ppermute | solution.py:1004
  53.2 38.8 %collective-permute-start.10 = (bf16[4,256,768]{2,1,0:T(8,128)(2,1)S(1)}, bf16[4,256,768]{2,1,0:T(8,128)(2,1)}, u32[]{:S(2)}, u32[]{:S(2)}) collective-permute-start(bf16[4,256,768]{2,1,0:T(8,128)(2,1)S(1)} %copy-done), channel_id=1, source_target_pairs={{0,1},{1,2},{2,3},{4,5},{5,6},{6,7},{8,9},{9,10},{10,11},{12,13},{... | collective-permute-start | bytes 4718600 | tf_op jit(solution)/shard_map/ppermute | solution.py:1004
  56.4 2.3 collective-permute-start.3
  56.5 3.0 collective-permute-start.9
  57.0 8.2 %collective-permute-start.7 = (bf16[352,768]{1,0:T(8,128)(2,1)}, bf16[352,768]{1,0:T(8,128)(2,1)}, u32[]{:S(2)}, u32[]{:S(2)}) collective-permute-start(bf16[352,768]{1,0:T(8,128)(2,1)} %copy-done.7), channel_id=1, source_target_pairs={{0,4},{4,0},{1,5},{5,1},{2,6},{6,2},{3,7},{7,3},{8,12},{12,8},{9,1... | collective-permute-start | bytes 1622024 | tf_op jit(solution)/shard_map/ppermute | solution.py:940
  58.7 6.4 %collective-permute-start.5 = (bf16[352,768]{1,0:T(8,128)(2,1)}, bf16[352,768]{1,0:T(8,128)(2,1)}, u32[]{:S(2)}, u32[]{:S(2)}) collective-permute-start(bf16[352,768]{1,0:T(8,128)(2,1)} %collective-permute-done.4.refs_3_), channel_id=1, source_target_pairs={{0,4},{4,0},{1,5},{5,1},{2,6},{6,2},{3,7},{7,3},{8,12},{12,8},{9,1... | collective-permute-start | bytes 1622024 | tf_op jit(solution)/shard_map/ppermute | solution.py:940
  59.5 27.9 %collective-permute-start.12 = (bf16[4,1,768]{2,1,0:T(2,128)(2,1)S(1)}, bf16[4,1,768]{2,1,0:T(2,128)(2,1)S(1)}, u32[]{:S(2)}, u32[]{:S(2)}) collective-permute-start(bf16[4,1,768]{2,1,0:T(2,128)(2,1)S(1)} %slice.147), channel_id=1, source_target_pairs={{2,0},{3,1},{6,4},{7,5},{10,8},{11,9},{14,12},{15,13},{18,16},{19,... | collective-permute-start | bytes 18440 | tf_op jit(solution)/shard_map/ppermute | solution.py:1004
  87.4 4.7 %copy-start.10 = (bf16[4,1,768]{2,1,0:T(2,128)(2,1)}, bf16[4,1,768]{2,1,0:T(2,128)(2,1)S(1)}, u32[]{:S(2)}) copy-start(bf16[4,1,768]{2,1,0:T(2,128)(2,1)S(1)} %collective-permute-done.12.far_ref) | copy-start | bytes 18436
  89.2 2.9 copy-start.3
  171.0 123.3 %reduce-scatter.5.cloned.1.call-start = ((), (), s32[]{:S(2)}) async-start(), calls=%async_computation.3 | async-start | bytes 1658880 | tf_op jit(solution)/shard_map/reduce_scatter | solution.py:1097
  200.2 15.6 %copy-start.9 = (f32[4,16,768]{2,1,0:T(8,128)S(1)}, f32[4,16,768]{2,1,0:T(8,128)}, u32[]{:S(2)}) copy-start(f32[4,16,768]{2,1,0:T(8,128)} %get-tuple-element.83) | copy-start | bytes 589828
  200.2 15.6 %copy-start.12 = (f32[4,1,768]{2,1,0:T(1,128)S(1)}, f32[4,1,768]{2,1,0:T(1,128)}, u32[]{:S(2)}) copy-start(f32[4,1,768]{2,1,0:T(1,128)} %get-tuple-element.85) | copy-start | bytes 36868
  200.2 15.7 %copy-start.11 = (f32[8,768]{1,0:T(8,128)S(1)}, f32[8,768]{1,0:T(8,128)}, u32[]{:S(2)}) copy-start(f32[8,768]{1,0:T(8,128)} %get-tuple-element.84) | copy-start | bytes 73732
  209.9 38.7 %collective-permute-start.15 = (bf16[4,256,768]{2,1,0:T(8,128)(2,1)}, bf16[4,256,768]{2,1,0:T(8,128)(2,1)}, u32[]{:S(2)}, u32[]{:S(2)}) collective-permute-start(bf16[4,256,768]{2,1,0:T(8,128)(2,1)} %get-tuple-element.89), channel_id=1, source_target_pairs={{0,1},{1,2},{2,3},{4,5},{5,6},{6,7},{8,9},{9,10},{10,11},{12,13},{... | collective-permute-start | bytes 4718600 | tf_op jit(solution)/shard_map/ppermute | solution.py:1004
  212.6 37.5 %collective-permute-start.14 = (bf16[4,256,768]{2,1,0:T(8,128)(2,1)}, bf16[4,256,768]{2,1,0:T(8,128)(2,1)}, u32[]{:S(2)}, u32[]{:S(2)}) collective-permute-start(bf16[4,256,768]{2,1,0:T(8,128)(2,1)} %get-tuple-element.80), channel_id=1, source_target_pairs={{1,0},{2,1},{3,2},{5,4},{6,5},{7,6},{9,8},{10,9},{11,10},{13,12},{... | collective-permute-start | bytes 4718600 | tf_op jit(solution)/shard_map/ppermute | solution.py:1004
  216.1 32.5 %collective-permute-start.13 = (bf16[4,1,768]{2,1,0:T(2,128)(2,1)}, bf16[4,1,768]{2,1,0:T(2,128)(2,1)S(1)}, u32[]{:S(2)}, u32[]{:S(2)}) collective-permute-start(bf16[4,1,768]{2,1,0:T(2,128)(2,1)} %get-tuple-element.88), channel_id=1, source_target_pairs={{0,2},{1,3},{4,6},{5,7},{8,10},{9,11},{12,14},{13,15},{16,18},{17,... | collective-permute-start | bytes 18440 | tf_op jit(solution)/shard_map/ppermute | solution.py:1004
  234.2 23.0 %copy-start.4 = (bf16[4,352,768]{2,1,0:T(8,128)(2,1)S(1)}, bf16[4,352,768]{2,1,0:T(8,128)(2,1)}, u32[]{:S(2)}) copy-start(bf16[4,352,768]{2,1,0:T(8,128)(2,1)} %get-tuple-element.98) | copy-start | bytes 6488068
  252.7 4.6 %collective-permute-start.16 = (bf16[4,352,768]{2,1,0:T(8,128)(2,1)}, bf16[4,352,768]{2,1,0:T(8,128)(2,1)}, u32[]{:S(2)}, u32[]{:S(2)}) collective-permute-start(bf16[4,352,768]{2,1,0:T(8,128)(2,1)} %get-tuple-element.99), channel_id=1, source_target_pairs={{0,4},{4,0},{1,5},{5,1},{2,6},{6,2},{3,7},{7,3},{8,12},{12,8},{9,1... | collective-permute-start | bytes 6488072 | tf_op jit(solution)/shard_map/ppermute | solution.py:1098
  259.4 2.0 copy-start.2
  259.4 5.4 %copy-start.1 = (f32[4,256,768]{2,1,0:T(8,128)S(1)}, f32[4,256,768]{2,1,0:T(8,128)}, u32[]{:S(2)}) copy-start(f32[4,256,768]{2,1,0:T(8,128)} %own_grads.1) | copy-start | bytes 9437188
  261.3 16.4 %collective-permute-start.19 = (bf16[352,768]{1,0:T(8,128)(2,1)}, bf16[352,768]{1,0:T(8,128)(2,1)}, u32[]{:S(2)}, u32[]{:S(2)}) collective-permute-start(bf16[352,768]{1,0:T(8,128)(2,1)} %get-tuple-element.107), channel_id=1, source_target_pairs={{0,24},{8,16},{16,8},{24,0},{1,25},{9,17},{17,9},{25,1},{2,26},{10... | collective-permute-start | bytes 1622024 | tf_op jit(solution)/shard_map/ppermute | solution.py:962
  262.8 25.7 %collective-permute-start.18 = (bf16[352,768]{1,0:T(8,128)(2,1)}, bf16[352,768]{1,0:T(8,128)(2,1)}, u32[]{:S(2)}, u32[]{:S(2)}) collective-permute-start(bf16[352,768]{1,0:T(8,128)(2,1)} %get-tuple-element.108), channel_id=1, source_target_pairs={{0,16},{8,24},{16,0},{24,8},{1,17},{9,25},{17,1},{25,9},{2,18},{10... | collective-permute-start | bytes 1622024 | tf_op jit(solution)/shard_map/ppermute | solution.py:962
  264.1 24.3 %collective-permute-start.17 = (bf16[352,768]{1,0:T(8,128)(2,1)}, bf16[352,768]{1,0:T(8,128)(2,1)}, u32[]{:S(2)}, u32[]{:S(2)}) collective-permute-start(bf16[352,768]{1,0:T(8,128)(2,1)} %get-tuple-element.109), channel_id=1, source_target_pairs={{0,8},{8,0},{16,24},{24,16},{1,9},{9,1},{17,25},{25,17},{2,10},{10... | collective-permute-start | bytes 1622024 | tf_op jit(solution)/shard_map/ppermute | solution.py:962
  290.4 9.4 %collective-permute-start.22 = (bf16[88,768]{1,0:T(8,128)(2,1)S(1)}, bf16[88,768]{1,0:T(8,128)(2,1)S(1)}, u32[]{:S(2)}, u32[]{:S(2)}) collective-permute-start(bf16[88,768]{1,0:T(8,128)(2,1)S(1)} %get-tuple-element.110), channel_id=1, source_target_pairs={{0,3},{1,2},{2,1},{3,0},{4,7},{5,6},{6,5},{7,4},{8,11},{9,10},{10,... | collective-permute-start | bytes 405512 | tf_op jit(solution)/shard_map/ppermute | solution.py:962
  291.0 8.9 %collective-permute-start.20 = (bf16[88,768]{1,0:T(8,128)(2,1)S(1)}, bf16[88,768]{1,0:T(8,128)(2,1)S(1)}, u32[]{:S(2)}, u32[]{:S(2)}) collective-permute-start(bf16[88,768]{1,0:T(8,128)(2,1)S(1)} %get-tuple-element.111), channel_id=1, source_target_pairs={{0,1},{1,0},{2,3},{3,2},{4,5},{5,4},{6,7},{7,6},{8,9},{9,8},{10,11... | collective-permute-start | bytes 405512 | tf_op jit(solution)/shard_map/ppermute | solution.py:962
  292.6 11.1 %collective-permute-start.21 = (bf16[88,768]{1,0:T(8,128)(2,1)S(1)}, bf16[88,768]{1,0:T(8,128)(2,1)S(1)}, u32[]{:S(2)}, u32[]{:S(2)}) collective-permute-start(bf16[88,768]{1,0:T(8,128)(2,1)S(1)} %get-tuple-element.112), channel_id=1, source_target_pairs={{0,2},{1,3},{2,0},{3,1},{4,6},{5,7},{6,4},{7,5},{8,10},{9,11},{10,... | collective-permute-start | bytes 405512 | tf_op jit(solution)/shard_map/ppermute | solution.py:962
Sparse Core Ops, SparseCore 0:
  14.6 33.4 all-gather.4
  50.0 65.7 all-gather.6
  171.2 81.4 reduce-scatter.2
  254.8 30.4 reduce-scatter.4
